TPU v7x, 32 devices: a whole 2x2x4 slice. The times are simulated.
32 devices in a mesh: shard: 4 (over y, x), rep: 8 (over z, core).
Axes of the slice: x: 2, y: 2, z: 4, core: 2. Of those that a mesh axis runs over, the one named last changes fastest.
Arguments:
- tokens: bfloat16 [16384, 1024], P(('shard', 'rep')), may hold values from -6 to 6
- token_order: int32 [16384], P(('shard', 'rep')), may hold values from 0 to 16383, as said below
- lengths: int32 [128], P(('shard', 'rep')), may hold values from 0 to 512, as said below
- cotangent: bfloat16 [16384, 1024], P(('shard', 'rep')), may hold values from -6 to 6
- norm_gain: bfloat16 [2, 1024], P(None, 'shard'), may hold values from 0.5 to 1.5
- norm_shift: bfloat16 [2, 1024], P(None, 'shard'), may hold values from -3 to 3
- qkv_weight: bfloat16 [2, 1024, 3072], P(None, 'shard'), may hold values from -0.1875 to 0.1875
- qkv_bias: bfloat16 [2, 3072], P(None, 'shard'), may hold values from -3 to 3
- out_weight: bfloat16 [2, 1024, 1024], P(None, 'shard'), may hold values from -0.75 to 0.75
- out_bias: bfloat16 [2, 1024], P(None, 'shard'), may hold values from -3 to 3
- up_weight: bfloat16 [2, 1024, 4096], P(None, 'shard'), may hold values from -0.1875 to 0.1875
- up_bias: bfloat16 [2, 4096], P(None, 'shard'), may hold values from -3 to 3
- down_weight: bfloat16 [2, 4096, 1024], P(None, 'shard'), may hold values from -0.1875 to 0.1875
- down_bias: bfloat16 [2, 1024], P(None, 'shard'), may hold values from -3 to 3
Outputs:
- block_output: bfloat16 [16384, 1024], P(('shard', 'rep'))
- input_grad: bfloat16 [16384, 1024], P(('shard', 'rep'))
- norm_gain_grad: float32 [2, 1024], P(None, 'shard')
- norm_shift_grad: float32 [2, 1024], P(None, 'shard')
- qkv_weight_grad: float32 [2, 1024, 3072], P(None, 'shard')
- qkv_bias_grad: float32 [2, 3072], P(None, 'shard')
- out_weight_grad: float32 [2, 1024, 1024], P(None, 'shard')
- out_bias_grad: float32 [2, 1024], P(None, 'shard')
- up_weight_grad: float32 [2, 1024, 4096], P(None, 'shard')
- up_bias_grad: float32 [2, 4096], P(None, 'shard')
- down_weight_grad: float32 [2, 4096, 1024], P(None, 'shard')
- down_bias_grad: float32 [2, 1024], P(None, 'shard')
Inputs may be any that keep to these rules, and one draw needn't show every extreme that they name: `token_order`: A permutation of the tokens that moves whole documents, keeps each document's tokens in order, and maps the 4096 tokens of each index of shard onto themselves; the dealt documents of each device are the slots given by lengths. Each device's 4 lengths sum to 512; slots may be empty; in every draw some device of each index of shard holds one document of 512 tokens.
All inputs are finite; a program needn't handle non-finite values.
Results may differ from a plain program's by a relative error of at most 0.018.
Values may be sent and summed in bfloat16 or wider, within the bound.
No kernel may reach another device: no remote copies, remote signals or barrier semaphores. Data moves between devices by JAX's collectives and lax.ppermute only.
A program may use at most 384 MiB of HBM per device.

v0:
```python
import math

import jax
import jax.numpy as jnp
from jax import lax
from jax.sharding import PartitionSpec as P

HEADS = 16
HEAD = 64
ROT = 16


EPSILON = 1e-05
NEG_FILL = -1e30


def as_sent(x):
    return jax.tree.map(lambda a: a.astype(jnp.bfloat16) if a.dtype == jnp.float32 else a, x)


def doc_layout(lengths, row_count):
    doc_ends = jnp.cumsum(lengths)
    places = jnp.arange(row_count, dtype=jnp.int32)
    passed = doc_ends[None, :] <= places[:, None]
    segment = jnp.sum(passed.astype(jnp.int32), axis=1)
    starts = jnp.sum(jnp.where(passed, lengths[None, :], 0), axis=1)
    return (segment, places - starts)


def rotary_tables(positions):
    half_index = jnp.arange(ROT // 2, dtype=jnp.float32)
    inverse_freq = jnp.exp(half_index * (-2.0 * math.log(10000.0) / ROT))
    angles = positions.astype(jnp.float32)[:, None] * inverse_freq[None, :]
    angles = jnp.concatenate([angles, angles], axis=1)
    return (jnp.cos(angles), jnp.sin(angles))


def rotate_heads(flat, cosine, sine):
    row_count = flat.shape[0]
    heads = flat.reshape(row_count, HEADS, HEAD)
    turning = heads[:, :, :ROT]
    first_half = turning[:, :, : ROT // 2]
    second_half = turning[:, :, ROT // 2 :]
    swapped = jnp.concatenate([-second_half, first_half], axis=2)
    turned = turning * cosine[:, None, :] + swapped * sine[:, None, :]
    return jnp.concatenate([turned, heads[:, :, ROT:]], axis=2).reshape(row_count, HEADS * HEAD)


def exact_gelu(values_in):
    return jax.nn.gelu(values_in, approximate=False)


def norm_parts(stream):
    average = jnp.mean(stream, axis=1, keepdims=True)
    centered = stream - average
    inv_scale = lax.rsqrt(jnp.mean(centered * centered, axis=1, keepdims=True) + EPSILON)
    return (centered * inv_scale, inv_scale)


def contract_rows(left, right):
    return lax.dot_general(
        left, right, (((0,), (0,)), ((), ())), preferred_element_type=jnp.float32
    )


def times_transposed(left, right):
    return lax.dot_general(
        left, right, (((1,), (1,)), ((), ())), preferred_element_type=jnp.float32
    )


def scores_of(query_low, key_low, allowed):
    row_count = query_low.shape[0]
    query_heads = query_low.reshape(row_count, HEADS, HEAD)
    key_heads = key_low.reshape(row_count, HEADS, HEAD)
    scores = jnp.einsum(
        "qhe,khe->hqk", query_heads, key_heads, preferred_element_type=jnp.float32
    ) * HEAD ** (-0.5)
    return jnp.where(allowed[None], scores, NEG_FILL)


def row_picker(wanted, held_rows, piece_rows):
    span_rows = piece_rows[0].shape[0]
    inside = (wanted >= 0) & (wanted < span_rows)
    safe_rows = jnp.clip(wanted, 0, span_rows - 1)
    return tuple(
        (
            jnp.where(inside[:, None], jnp.take(member, safe_rows, axis=0), kept_rows)
            for member, kept_rows in zip(piece_rows, held_rows)
        )
    )


def layer_slices(stacked, layer_index):
    return tuple((member[layer_index] for member in stacked))


def layer_forward(stream, weights, allowed, cosine, sine):
    (
        gain_row,
        shift_row,
        qkv_matrix,
        qkv_offset,
        out_matrix,
        out_offset,
        up_matrix,
        up_offset,
        down_matrix,
        down_offset,
    ) = weights
    row_count, feature_count = stream.shape
    unit, inv_scale = norm_parts(stream)
    normed = (unit * gain_row.astype(jnp.float32) + shift_row.astype(jnp.float32)).astype(
        jnp.bfloat16
    )
    packed = jnp.dot(normed, qkv_matrix, preferred_element_type=jnp.float32) + qkv_offset.astype(
        jnp.float32
    )
    query_low = rotate_heads(packed[:, :feature_count], cosine, sine).astype(jnp.bfloat16)
    key_low = rotate_heads(packed[:, feature_count : 2 * feature_count], cosine, sine).astype(
        jnp.bfloat16
    )
    value_low = packed[:, 2 * feature_count :].astype(jnp.bfloat16)
    scores = scores_of(query_low, key_low, allowed)
    top_score = jnp.max(scores, axis=-1, keepdims=True)
    raised = jnp.exp(scores - top_score)
    row_total = jnp.sum(raised, axis=-1, keepdims=True)
    probs_low = (raised / row_total).astype(jnp.bfloat16)
    log_total = top_score + jnp.log(row_total)
    value_heads = value_low.reshape(row_count, HEADS, HEAD)
    attended_low = (
        jnp.einsum("hqk,khe->qhe", probs_low, value_heads, preferred_element_type=jnp.float32)
        .reshape(row_count, feature_count)
        .astype(jnp.bfloat16)
    )
    pre_act = jnp.dot(normed, up_matrix, preferred_element_type=jnp.float32) + up_offset.astype(
        jnp.float32
    )
    activated = exact_gelu(pre_act).astype(jnp.bfloat16)
    attention_out = jnp.dot(
        attended_low, out_matrix, preferred_element_type=jnp.float32
    ) + out_offset.astype(jnp.float32)
    network_out = jnp.dot(
        activated, down_matrix, preferred_element_type=jnp.float32
    ) + down_offset.astype(jnp.float32)
    new_stream = stream + attention_out + network_out
    return (
        new_stream,
        (
            unit,
            inv_scale,
            normed,
            query_low,
            key_low,
            value_low,
            log_total,
            attended_low,
            pre_act,
            activated,
        ),
    )


def layer_backward(grad_stream, weights, saved, allowed, cosine, sine):
    (
        gain_row,
        shift_row,
        qkv_matrix,
        qkv_offset,
        out_matrix,
        out_offset,
        up_matrix,
        up_offset,
        down_matrix,
        down_offset,
    ) = weights
    (
        unit,
        inv_scale,
        normed,
        query_low,
        key_low,
        value_low,
        log_total,
        attended_low,
        pre_act,
        activated,
    ) = saved
    row_count, feature_count = grad_stream.shape
    branch_grad = grad_stream.astype(jnp.bfloat16)
    offset_grad = jnp.sum(branch_grad.astype(jnp.float32), axis=0)
    act_grad = times_transposed(branch_grad, down_matrix)
    unused_value, gelu_pull = jax.vjp(exact_gelu, pre_act)
    pre_grad = gelu_pull(act_grad)[0].astype(jnp.bfloat16)
    up_offset_grad = jnp.sum(pre_grad.astype(jnp.float32), axis=0)
    attended_grad = times_transposed(branch_grad, out_matrix).astype(jnp.bfloat16)
    query_heads = query_low.reshape(row_count, HEADS, HEAD)
    key_heads = key_low.reshape(row_count, HEADS, HEAD)
    value_heads = value_low.reshape(row_count, HEADS, HEAD)
    grad_heads = attended_grad.reshape(row_count, HEADS, HEAD)
    scores = scores_of(query_low, key_low, allowed)
    probs = jnp.exp(scores - log_total)
    probs_low = probs.astype(jnp.bfloat16)
    value_grad = jnp.einsum(
        "hqk,qhe->khe", probs_low, grad_heads, preferred_element_type=jnp.float32
    )
    prob_grad = jnp.einsum(
        "qhe,khe->hqk", grad_heads, value_heads, preferred_element_type=jnp.float32
    )
    row_dot = jnp.sum(prob_grad * probs, axis=-1, keepdims=True)
    score_grad = (probs * (prob_grad - row_dot)).astype(jnp.bfloat16)
    query_grad = jnp.einsum(
        "hqk,khe->qhe", score_grad, key_heads, preferred_element_type=jnp.float32
    ) * HEAD ** (-0.5)
    key_grad = jnp.einsum(
        "hqk,qhe->khe", score_grad, query_heads, preferred_element_type=jnp.float32
    ) * HEAD ** (-0.5)
    packed_grad = jnp.concatenate(
        [
            rotate_heads(query_grad.reshape(row_count, feature_count), cosine, -sine),
            rotate_heads(key_grad.reshape(row_count, feature_count), cosine, -sine),
            value_grad.reshape(row_count, feature_count),
        ],
        axis=1,
    ).astype(jnp.bfloat16)
    qkv_offset_grad = jnp.sum(packed_grad.astype(jnp.float32), axis=0)
    normed_grad = times_transposed(packed_grad, qkv_matrix) + times_transposed(pre_grad, up_matrix)
    gain_grad = jnp.sum(normed_grad * unit, axis=0)
    shift_grad = jnp.sum(normed_grad, axis=0)
    unit_grad = normed_grad * gain_row.astype(jnp.float32)
    stream_grad = grad_stream + inv_scale * (
        unit_grad
        - jnp.mean(unit_grad, axis=1, keepdims=True)
        - unit * jnp.mean(unit_grad * unit, axis=1, keepdims=True)
    )
    small_grads = (gain_grad, shift_grad, qkv_offset_grad, offset_grad, up_offset_grad)
    operands = (normed, attended_low, activated, packed_grad, branch_grad, pre_grad)
    return (stream_grad, small_grads, operands)


def body(
    tokens,
    token_order,
    lengths,
    cotangent,
    norm_gain,
    norm_shift,
    qkv_weight,
    qkv_bias,
    out_weight,
    out_bias,
    up_weight,
    up_bias,
    down_weight,
    down_bias,
):
    row_count = tokens.shape[0]
    group_rows = row_count * lax.axis_size("rep")
    group_first = lax.axis_index("shard") * group_rows
    all_order = lax.all_gather(token_order, "rep", axis=0, tiled=True)
    inverse = (
        jnp.zeros((group_rows,), jnp.int32)
        .at[all_order - group_first]
        .set(jnp.arange(group_rows, dtype=jnp.int32))
    )
    back_rows = lax.dynamic_slice_in_dim(inverse, lax.axis_index("rep") * row_count, row_count)
    blank = jnp.zeros_like(tokens)
    dealt, dealt_cot = row_picker(
        token_order - group_first,
        (blank, blank),
        (
            lax.all_gather(tokens, "rep", axis=0, tiled=True),
            lax.all_gather(cotangent, "rep", axis=0, tiled=True),
        ),
    )
    segment, positions = doc_layout(lengths, row_count)
    places = jnp.arange(row_count, dtype=jnp.int32)
    allowed = (segment[:, None] == segment[None, :]) & (places[None, :] <= places[:, None])
    cosine, sine = rotary_tables(positions)
    stacked = (
        norm_gain,
        norm_shift,
        qkv_weight,
        qkv_bias,
        out_weight,
        out_bias,
        up_weight,
        up_bias,
        down_weight,
        down_bias,
    )
    layer_count = norm_gain.shape[0]
    stream = dealt.astype(jnp.float32)
    savings = []
    gathered = []
    for layer_index in range(layer_count):
        weights = lax.all_gather(
            as_sent(layer_slices(stacked, layer_index)), "shard", axis=0, tiled=True
        )
        gathered.append(weights)
        stream, saved = layer_forward(stream, weights, allowed, cosine, sine)
        savings.append(saved)
    output_low = stream.astype(jnp.bfloat16)
    grad_stream = dealt_cot.astype(jnp.float32)
    owned = [None] * layer_count
    for layer_index in reversed(range(layer_count)):
        weights = lax.all_gather(
            as_sent(layer_slices(stacked, layer_index)), "shard", axis=0, tiled=True
        )
        grad_stream, small_grads, operands = layer_backward(
            grad_stream, weights, savings[layer_index], allowed, cosine, sine
        )
        gain_grad, shift_grad, qkv_offset_grad, offset_grad, up_offset_grad = small_grads
        normed, attended_low, activated, packed_grad, branch_grad, pre_grad = operands
        local_grads = (
            gain_grad,
            shift_grad,
            contract_rows(normed, packed_grad),
            qkv_offset_grad,
            contract_rows(attended_low, branch_grad),
            offset_grad,
            contract_rows(normed, pre_grad),
            up_offset_grad,
            contract_rows(activated, branch_grad),
            offset_grad,
        )
        scattered = (
            lax.psum_scatter(
                local_grads[0].astype(jnp.bfloat16), "shard", scatter_dimension=0, tiled=True
            ).astype(jnp.float32),
            lax.psum_scatter(
                local_grads[1].astype(jnp.bfloat16), "shard", scatter_dimension=0, tiled=True
            ).astype(jnp.float32),
            lax.psum_scatter(
                local_grads[2].astype(jnp.bfloat16), "shard", scatter_dimension=0, tiled=True
            ).astype(jnp.float32),
            lax.psum_scatter(
                local_grads[3].astype(jnp.bfloat16), "shard", scatter_dimension=0, tiled=True
            ).astype(jnp.float32),
            lax.psum_scatter(
                local_grads[4].astype(jnp.bfloat16), "shard", scatter_dimension=0, tiled=True
            ).astype(jnp.float32),
            lax.psum_scatter(
                local_grads[5].astype(jnp.bfloat16), "shard", scatter_dimension=0, tiled=True
            ).astype(jnp.float32),
            lax.psum_scatter(
                local_grads[6].astype(jnp.bfloat16), "shard", scatter_dimension=0, tiled=True
            ).astype(jnp.float32),
            lax.psum_scatter(
                local_grads[7].astype(jnp.bfloat16), "shard", scatter_dimension=0, tiled=True
            ).astype(jnp.float32),
            lax.psum_scatter(
                local_grads[8].astype(jnp.bfloat16), "shard", scatter_dimension=0, tiled=True
            ).astype(jnp.float32),
            lax.psum_scatter(
                local_grads[9].astype(jnp.bfloat16), "shard", scatter_dimension=0, tiled=True
            ).astype(jnp.float32),
        )
        scattered = (
            lax.psum(scattered[0].astype(jnp.bfloat16), "rep").astype(jnp.float32),
            lax.psum(scattered[1].astype(jnp.bfloat16), "rep").astype(jnp.float32),
            lax.psum(scattered[2].astype(jnp.bfloat16), "rep").astype(jnp.float32),
            lax.psum(scattered[3].astype(jnp.bfloat16), "rep").astype(jnp.float32),
            lax.psum(scattered[4].astype(jnp.bfloat16), "rep").astype(jnp.float32),
            lax.psum(scattered[5].astype(jnp.bfloat16), "rep").astype(jnp.float32),
            lax.psum(scattered[6].astype(jnp.bfloat16), "rep").astype(jnp.float32),
            lax.psum(scattered[7].astype(jnp.bfloat16), "rep").astype(jnp.float32),
            lax.psum(scattered[8].astype(jnp.bfloat16), "rep").astype(jnp.float32),
            lax.psum(scattered[9].astype(jnp.bfloat16), "rep").astype(jnp.float32),
        )
        owned[layer_index] = scattered
    stacked_grads = tuple(
        (
            jnp.stack([owned[layer_index][member_index] for layer_index in range(layer_count)])
            for member_index in range(10)
        )
    )
    final_output, final_grad = row_picker(
        back_rows,
        (blank, blank),
        (
            lax.all_gather(output_low, "rep", axis=0, tiled=True),
            lax.all_gather(grad_stream.astype(jnp.bfloat16), "rep", axis=0, tiled=True),
        ),
    )
    return (final_output, final_grad) + tuple(stacked_grads)


def solution(mesh):
    placed = (
        P(("shard", "rep"), None),
        P(("shard", "rep")),
        P(("shard", "rep")),
        P(("shard", "rep"), None),
        P(None, "shard"),
        P(None, "shard"),
        P(None, "shard", None),
        P(None, "shard"),
        P(None, "shard", None),
        P(None, "shard"),
        P(None, "shard", None),
        P(None, "shard"),
        P(None, "shard", None),
        P(None, "shard"),
    )
    return jax.shard_map(
        body,
        mesh=mesh,
        in_specs=placed,
        out_specs=(
            P(("shard", "rep"), None),
            P(("shard", "rep"), None),
            P(None, "shard"),
            P(None, "shard"),
            P(None, "shard", None),
            P(None, "shard"),
            P(None, "shard", None),
            P(None, "shard"),
            P(None, "shard", None),
            P(None, "shard"),
            P(None, "shard", None),
            P(None, "shard"),
        ),
        check_vma=False,
    )
```

profile of v0, /device:TPU:1, one launch (start us, length us, event | category | flops | bytes accessed | tf_op | source)
XLA Modules:
  0.0 1783.7 jit_solution(4756610597523193485)
XLA Ops:
  104.2 60.7 %all-gather.42.cloned.1.call-done = bf16[1,1024,3072]{2,1,0:T(8,128)(2,1)} async-done(((bf16[1,256,3072]{2,1,0:T(8,128)(2,1)}), bf16[1,1024,3072]{2,1,0:T(8,128)(2,1)}) %all-gather.42.cloned.1.call-update) | async-done | bytes 6291472 | tf_op jit(solution)/shard_map/all_gather | solution.py:297
  215.8 39.2 %all-gather.46.cloned.1.call-done = bf16[1,1024,4096]{2,1,0:T(8,128)(2,1)} async-done(((bf16[1,256,4096]{2,1,0:T(8,128)(2,1)}), bf16[1,1024,4096]{2,1,0:T(8,128)(2,1)}) %all-gather.46.cloned.1.call-update) | async-done | bytes 8388624 | tf_op jit(solution)/shard_map/all_gather | solution.py:297
  255.0 27.8 %multiply_convert_fusion.3 = (bf16[512,4096]{1,0:T(8,128)(2,1)}, f32[512,4096]{1,0:T(8,128)}, f32[512,4096]{1,0:T(8,128)}) fusion(f32[4096]{0:T(1024)S(1)} %bitcast.225, bf16[1,1024,4096]{2,1,0:T(8,128)(2,1)} %all-gather.46.cloned.1.call-done, bf16[512,1024]{1,0:T(8,128)(2,1)S(1)} %get-tuple-element.61, f32[1024]{0:T(1024)S(1)} %bitcast.239, ...), kind=kOutput, calls=%fused_computation.60 | convolution fusion | flops 4436525056 | bytes 30437376 | tf_op jit(solution)/shard_map/dot_general | solution.py:136
  296.2 85.2 %all-gather.48.cloned.1.call-done = bf16[1,4096,1024]{2,1,0:T(8,128)(2,1)} async-done(((bf16[1,1024,1024]{2,1,0:T(8,128)(2,1)}), bf16[1,4096,1024]{2,1,0:T(8,128)(2,1)}) %all-gather.48.cloned.1.call-update) | async-done | bytes 8388624 | tf_op jit(solution)/shard_map/all_gather | solution.py:297
  391.6 73.8 %all-gather.38.cloned.1.call-done = bf16[4096,1024]{1,0:T(8,128)(2,1)} async-done(((bf16[512,1024]{1,0:T(8,128)(2,1)}), bf16[4096,1024]{1,0:T(8,128)(2,1)}) %all-gather.38.cloned.1.call-update) | async-done | bytes 8388624 | tf_op jit(solution)/shard_map/all_gather | solution.py:273
  472.7 28.5 %all-gather.52.cloned.1.call-done = bf16[1,1024,1024]{2,1,0:T(8,128)(2,1)} async-done(((bf16[1,256,1024]{2,1,0:T(8,128)(2,1)}), bf16[1,1024,1024]{2,1,0:T(8,128)(2,1)}) %all-gather.52.cloned.1.call-update) | async-done | bytes 2097168 | tf_op jit(solution)/shard_map/all_gather | solution.py:297
  508.7 64.5 %all-gather.50.cloned.1.call-done = bf16[1,1024,3072]{2,1,0:T(8,128)(2,1)} async-done(((bf16[1,256,3072]{2,1,0:T(8,128)(2,1)}), bf16[1,1024,3072]{2,1,0:T(8,128)(2,1)}) %all-gather.50.cloned.1.call-update) | async-done | bytes 6291472 | tf_op jit(solution)/shard_map/all_gather | solution.py:297
  614.8 16.3 multiply_reduce_fusion.1
  673.4 27.4 %multiply_convert_fusion.2 = (bf16[512,4096]{1,0:T(8,128)(2,1)}, f32[512,4096]{1,0:T(8,128)}, f32[512,4096]{1,0:T(8,128)}) fusion(f32[4096]{0:T(1024)S(1)} %bitcast.227, bf16[512,1024]{1,0:T(8,128)(2,1)} %add_convert_fusion.3, bf16[1,1024,4096]{2,1,0:T(8,128)(2,1)} %all-gather.54.cloned.1.call-done), kind=kOutput, calls=%fused_computation.47 | convolution fusion | flops 4433379328 | bytes 30425088 | tf_op jit(solution)/shard_map/dot_general | solution.py:136
  700.8 51.9 %all-gather.56.cloned.1.call-done = bf16[1,4096,1024]{2,1,0:T(8,128)(2,1)} async-done(((bf16[1,1024,1024]{2,1,0:T(8,128)(2,1)}), bf16[1,4096,1024]{2,1,0:T(8,128)(2,1)}) %all-gather.56.cloned.1.call-update) | async-done | bytes 8388624 | tf_op jit(solution)/shard_map/all_gather | solution.py:297
  752.7 15.8 fusion.159
  807.7 14.7 multiply_reduce_fusion
  873.9 13.6 fusion.160
  961.4 14.8 reduce-scatter.9.cloned.1.call-done
  976.1 89.3 %reduce-scatter.19.cloned.1.call-done = bf16[256,4096]{1,0:T(8,128)(2,1)} async-done(((bf16[1024,4096]{1,0:T(8,128)(2,1)}), bf16[256,4096]{1,0:T(8,128)(2,1)}) %reduce-scatter.19.cloned.1.call-update) | async-done | bytes 2097168 | tf_op jit(solution)/shard_map/reduce_scatter | solution.py:346
  1065.4 90.2 %reduce-scatter.17.cloned.1.call-done = bf16[256,4096]{1,0:T(8,128)(2,1)} async-done(((bf16[1024,4096]{1,0:T(8,128)(2,1)}), bf16[256,4096]{1,0:T(8,128)(2,1)}) %reduce-scatter.17.cloned.1.call-update) | async-done | bytes 2097168 | tf_op jit(solution)/shard_map/reduce_scatter | solution.py:346
  1155.6 89.9 %reduce-scatter.23.cloned.1.call-done = bf16[1024,1024]{1,0:T(8,128)(2,1)} async-done(((bf16[4096,1024]{1,0:T(8,128)(2,1)}), bf16[1024,1024]{1,0:T(8,128)(2,1)}) %reduce-scatter.23.cloned.1.call-update) | async-done | bytes 2097168 | tf_op jit(solution)/shard_map/reduce_scatter | solution.py:352
  1245.5 89.7 %reduce-scatter.21.cloned.1.call-done = bf16[1024,1024]{1,0:T(8,128)(2,1)} async-done(((bf16[4096,1024]{1,0:T(8,128)(2,1)}), bf16[1024,1024]{1,0:T(8,128)(2,1)}) %reduce-scatter.21.cloned.1.call-update) | async-done | bytes 2097168 | tf_op jit(solution)/shard_map/reduce_scatter | solution.py:352
  1338.4 13.4 all-gather.20
  1351.8 15.5 scatter_custom_fusion
  1371.8 13.4 all-reduce.12
  1386.0 25.9 %all-reduce.10 = (bf16[1,256]{1,0:T(2,128)(2,1)S(1)}, bf16[1,256]{1,0:T(2,128)(2,1)S(1)}, bf16[1,256]{1,0:T(2,128)(2,1)S(1)}, bf16[1,256]{1,0:T(2,128)(2,1)S(1)}...) all-reduce(bf16[1,256]{1,0:T(2,128)(2,1)S(1)} %stack.130, ...), channel_id=1, replica_groups=mesh['shard'=4,'rep'=8] {'rep'}, use_global_device_ids=true, to_apply=%region_23.25 | all-reduce | flops 5120 | bytes 20480 | tf_op jit(solution)/shard_map/psum | solution.py:360
  1427.6 75.5 %all-gather.36.cloned.1.call-done = bf16[4096,1024]{1,0:T(8,128)(2,1)} async-done(((bf16[512,1024]{1,0:T(8,128)(2,1)}), bf16[4096,1024]{1,0:T(8,128)(2,1)}) %all-gather.36.cloned.1.call-update) | async-done | bytes 8388624 | tf_op jit(solution)/shard_map/all_gather | solution.py:382
  1511.9 249.2 %all-reduce.15.cloned.1.call-done = (bf16[1,256,3072]{2,1,0:T(8,128)(2,1)}, bf16[1,256,3072]{2,1,0:T(8,128)(2,1)}, bf16[1,256,1024]{2,1,0:T(8,128)(2,1)}, bf16[1...) async-done(((bf16[1,256,3072]{2,1,0:T(8,128)(2,1)}, ...) | async-done | bytes 12582928 | tf_op jit(solution)/shard_map/psum | solution.py:362
  (462 shorter events, 479.5 us)
Async XLA Ops:
  7.2 88.4 %all-gather.34.cloned.1.call-start = ((), (), s32[]{:S(2)}) async-start(), calls=%async_computation.8 | async-start | bytes 9437184 | tf_op jit(solution)/shard_map/all_gather | solution.py:272
  7.9 157.0 %all-gather.42.cloned.1.call-start = ((), (), s32[]{:S(2)}) async-start(), calls=%async_computation.20 | async-start | bytes 7864320 | tf_op jit(solution)/shard_map/all_gather | solution.py:297
  11.7 243.3 %all-gather.46.cloned.1.call-start = ((), (), s32[]{:S(2)}) async-start(), calls=%async_computation.22 | async-start | bytes 10485760 | tf_op jit(solution)/shard_map/all_gather | solution.py:297
  16.6 275.4 %all-gather.44.cloned.1.call-start = ((), (), s32[]{:S(2)}) async-start(), calls=%async_computation.21 | async-start | bytes 2621440 | tf_op jit(solution)/shard_map/all_gather | solution.py:297
  17.7 363.6 %all-gather.48.cloned.1.call-start = ((), (), s32[]{:S(2)}) async-start(), calls=%async_computation.23 | async-start | bytes 10485760 | tf_op jit(solution)/shard_map/all_gather | solution.py:297
  23.0 442.3 %all-gather.38.cloned.1.call-start = ((), (), s32[]{:S(2)}) async-start(), calls=%async_computation.10 | async-start | bytes 9437184 | tf_op jit(solution)/shard_map/all_gather | solution.py:273
  23.6 477.6 %all-gather.52.cloned.1.call-start = ((), (), s32[]{:S(2)}) async-start(), calls=%async_computation.25 | async-start | bytes 2621440 | tf_op jit(solution)/shard_map/all_gather | solution.py:297
  24.3 548.9 %all-gather.50.cloned.1.call-start = ((), (), s32[]{:S(2)}) async-start(), calls=%async_computation.24 | async-start | bytes 7864320 | tf_op jit(solution)/shard_map/all_gather | solution.py:297
  25.1 648.3 %all-gather.54.cloned.1.call-start = ((), (), s32[]{:S(2)}) async-start(), calls=%async_computation.26 | async-start | bytes 10485760 | tf_op jit(solution)/shard_map/all_gather | solution.py:297
  25.8 726.9 %all-gather.56.cloned.1.call-start = ((), (), s32[]{:S(2)}) async-start(), calls=%async_computation.27 | async-start | bytes 10485760 | tf_op jit(solution)/shard_map/all_gather | solution.py:297
  26.4 934.9 %reduce-scatter.15.cloned.1.call-start = ((), (), s32[]{:S(2)}) async-start(), calls=%async_computation.15 | async-start | bytes 2621440 | tf_op jit(solution)/shard_map/reduce_scatter | solution.py:340
  41.5 459.7 %copy-start.91 = (pred[512]{0:T(512)(128)(4,1)}, pred[512]{0:T(512)(128)(4,1)S(1)}, u32[]{:S(2)}) copy-start(pred[512]{0:T(512)(128)(4,1)S(1)} %get-tuple-element.62) | copy-start | bytes 1540
  41.5 459.7 %copy-start.94 = (pred[512]{0:T(512)(128)(4,1)}, pred[512]{0:T(512)(128)(4,1)S(1)}, u32[]{:S(2)}) copy-start(pred[512]{0:T(512)(128)(4,1)S(1)} %get-tuple-element.109) | copy-start | bytes 1540
  74.9 431.7 %copy-start.67 = (f32[1,1024]{1,0:T(1,128)}, f32[1,1024]{1,0:T(1,128)S(1)}, u32[]{:S(2)}) copy-start(f32[1,1024]{1,0:T(1,128)S(1)} %convert_element_type.303) | copy-start | bytes 12292
  673.3 288.0 %reduce-scatter.13.cloned.1.call-start = ((), (), s32[]{:S(2)}) async-start(), calls=%async_computation.14 | async-start | bytes 2621440 | tf_op jit(solution)/shard_map/reduce_scatter | solution.py:340
  790.9 170.5 %reduce-scatter.11.cloned.1.call-start = ((), (), s32[]{:S(2)}) async-start(), calls=%async_computation.13 | async-start | bytes 7864320 | tf_op jit(solution)/shard_map/reduce_scatter | solution.py:334
  800.6 175.6 %reduce-scatter.9.cloned.1.call-start = ((), (), s32[]{:S(2)}) async-start(), calls=%async_computation.12 | async-start | bytes 7864320 | tf_op jit(solution)/shard_map/reduce_scatter | solution.py:334
  862.3 203.1 %reduce-scatter.19.cloned.1.call-start = ((), (), s32[]{:S(2)}) async-start(), calls=%async_computation.17 | async-start | bytes 10485760 | tf_op jit(solution)/shard_map/reduce_scatter | solution.py:346
  872.7 282.9 %reduce-scatter.17.cloned.1.call-start = ((), (), s32[]{:S(2)}) async-start(), calls=%async_computation.16 | async-start | bytes 10485760 | tf_op jit(solution)/shard_map/reduce_scatter | solution.py:346
  896.7 348.8 %reduce-scatter.23.cloned.1.call-start = ((), (), s32[]{:S(2)}) async-start(), calls=%async_computation.19 | async-start | bytes 10485760 | tf_op jit(solution)/shard_map/reduce_scatter | solution.py:352
  907.2 428.0 %reduce-scatter.21.cloned.1.call-start = ((), (), s32[]{:S(2)}) async-start(), calls=%async_computation.18 | async-start | bytes 10485760 | tf_op jit(solution)/shard_map/reduce_scatter | solution.py:352
  916.6 503.8 %all-gather.40.cloned.1.call-start = ((), (), s32[]{:S(2)}) async-start(), calls=%async_computation.11 | async-start | bytes 9437184 | tf_op jit(solution)/shard_map/all_gather | solution.py:383
  934.9 568.2 %all-gather.36.cloned.1.call-start = ((), (), s32[]{:S(2)}) async-start(), calls=%async_computation.9 | async-start | bytes 9437184 | tf_op jit(solution)/shard_map/all_gather | solution.py:382
  961.2 799.8 %all-reduce.15.cloned.1.call-start = ((), (), s32[]{:S(2)}) async-start(), calls=%async_computation.28 | async-start | bytes 25165824 | tf_op jit(solution)/shard_map/psum | solution.py:362
  (117 other events, 3615.7 us)
Sparse Core Ops, SparseCore 0:
  9.6 84.5 all-gather.33
  96.6 68.2 all-gather.41
  167.3 87.5 all-gather.45
  256.7 35.3 all-gather.43
  293.7 87.5 all-gather.47
  382.8 82.4 all-gather.37
  467.7 33.4 all-gather.51
  503.1 70.1 all-gather.49
  575.7 87.6 all-gather.53
  665.0 87.5 all-gather.55
  755.6 35.1 reduce-scatter.14
  794.0 35.1 reduce-scatter.12
  832.7 70.1 reduce-scatter.10
  905.8 70.2 reduce-scatter.8
  979.0 86.3 reduce-scatter.18
  1069.2 86.4 reduce-scatter.16
  1159.1 86.3 reduce-scatter.22
  1248.7 86.4 reduce-scatter.20
  1337.4 82.9 all-gather.39
  1422.4 80.5 all-gather.35
  1506.0 254.9 all-reduce.14
where the time goes:
time: 1790 us; the launch traced here: 1780 us
  waiting for transfers between devices  1120 us (63%)
  matrix products  312 us (17%)
  blocking collectives  129 us (7%)
  local copies, waits for them, and re-layouts  112 us (6%)
  other arithmetic  88.5 us (5%)
  between operations  18.3 us (1%)
    all_gather x8, waiting for transfers between devices, body(): lax.all_gather(as_sent(layer_slices(stacked, layer_index)), 'shard', axis...  339 us
    psum x1, waiting for transfers between devices, body(): lax.psum(scattered[2].astype(jnp.bfloat16), 'rep').astype(jnp.float32)  249 us
    reduce_scatter x2, waiting for transfers between devices, body(): lax.psum_scatter(local_grads[8].astype(jnp.bfloat16), 'shard', scatter_di...  180 us
    reduce_scatter x2, waiting for transfers between devices, body(): lax.psum_scatter(local_grads[6].astype(jnp.bfloat16), 'shard', scatter_di...  180 us
    all_gather x12, blocking collectives, body(): lax.all_gather(as_sent(layer_slices(stacked, layer_index)), 'shard', axis...  76.6 us
    all_gather x1, waiting for transfers between devices, body(): lax.all_gather(output_low, 'rep', axis=0, tiled=True)  75.5 us
    all_gather x1, waiting for transfers between devices, body(): lax.all_gather(cotangent, 'rep', axis=0, tiled=True)  73.8 us
    dot_general x8, matrix products, times_transposed(): lax.dot_general(left, right, (((1,), (1,)), ((), ())), preferred_element_...  65.1 us
  transfers between devices with their start and end apart: 21, of which 16 were waited for; matrix products, arithmetic and copies ran while one was open for 27% of the time, Pallas kernels for 0%

commit v1 on v0

v1 whole, which is shorter than its diff:
```python
import math

import jax
import jax.numpy as jnp
from jax import lax
from jax.experimental import pallas as pl
from jax.experimental.pallas import tpu as pltpu
from jax.sharding import PartitionSpec as P

HEADS = 16
HEAD = 64
ROT = 16
EPSILON = 1e-05
NEG_FILL = -1e30
AXES = ("shard", "rep")
bf16 = jnp.bfloat16
f32 = jnp.float32
VMEM_BYTES = 48 * 1024 * 1024
COLS = 512


def nn(a, b):
    return jnp.dot(a, b, preferred_element_type=f32)


def nt(a, b):
    return lax.dot_general(a, b, (((1,), (1,)), ((), ())), preferred_element_type=f32)


def whole(shape):
    return pl.BlockSpec(shape, lambda *_: (0,) * len(shape))


def row_blocks(rows, width):
    return pl.BlockSpec((rows, width), lambda i, *_: (i, 0))


ANY = pl.BlockSpec(memory_space=pl.ANY)


def call(kernel, scalars, inputs, outputs, grid, scratch=(), aliases={}, flops=0, bytes_=0):
    return pl.pallas_call(
        kernel,
        grid_spec=pltpu.PrefetchScalarGridSpec(
            num_scalar_prefetch=1,
            grid=grid,
            in_specs=[s for _, s in inputs],
            out_specs=[s for _, s in outputs],
            scratch_shapes=list(scratch),
        ),
        out_shape=[o for o, _ in outputs],
        input_output_aliases=aliases,
        compiler_params=pltpu.CompilerParams(vmem_limit_bytes=VMEM_BYTES),
        cost_estimate=pl.CostEstimate(flops=int(flops), bytes_accessed=int(bytes_), transcendentals=0),
    )(scalars, *[a for a, _ in inputs])


class Group:
    def __init__(self, blocks, first_half, extra=0):
        self.blocks = blocks
        self.rows = sum(b[0] for b in blocks) + extra
        self.first_half = first_half

    def cut(self, half):
        return (0, self.first_half) if half == 0 else (self.first_half, self.rows)


def piece_ranges(group, shards):
    ranges = []
    for r in range(shards):
        if bin(r).count("1") > 1:
            ranges += [(r,) + group.cut(0), (r,) + group.cut(1)]
        else:
            ranges.append((r, 0, group.rows))
    return ranges


def assembly(group, shards):
    plan = []
    for a, (r, lo, hi) in enumerate(piece_ranges(group, shards)):
        start = 0
        for rows, key, index in group.blocks:
            first, last = max(lo, start), min(hi, start + rows)
            if first < last:
                plan.append((a, first - lo, last - first, key, index, r, rows, first - start))
            start += rows
    return plan


def assemble_copies(group, shards, own, refs, targets, sems):
    copies = []
    for i, (a, src, rows, key, index, r, per, off) in enumerate(assembly(group, shards)):
        at = pl.multiple_of(lax.bitwise_xor(own, r) * per + off, 16)
        copies.append(
            pltpu.make_async_copy(
                refs[a].at[pl.ds(src, rows), :],
                targets[key].at[index, pl.ds(at, rows), :],
                sems.at[i],
            )
        )
    return copies


def spin(x, c, s1, s2):
    parts = []
    for j in range(x.shape[1] // 128):
        part = x[:, j * 128 : (j + 1) * 128]
        up = pltpu.roll(part, 128 - ROT // 2, 1)
        down = pltpu.roll(part, ROT // 2, 1)
        parts.append(part * c + up * s1 + down * s2)
    return parts


def forward_qkv(own, prev, adds, bias, gain, shift, qkv_b, tables, pieces, group, shards, block=256):
    rows, width = prev.shape
    count = len(pieces)
    n_add = len(adds)
    plan = assembly(group, shards)
    half = COLS

    def kernel(own_ref, *refs):
        prev_ref, *rest = refs
        add_refs, rest = rest[:n_add], rest[n_add:]
        bias_ref, gain_ref, shift_ref, qkvb_ref, c_ref, s1_ref, s2_ref, *rest = rest
        piece_refs, rest = rest[:count], rest[count:]
        stream_ref, unit_ref, inv_ref, normed_ref, q_ref, kv_ref, w_ref, sems = rest

        @pl.when(pl.program_id(0) == 0)
        def _():
            for c in assemble_copies(group, shards, own_ref[0], piece_refs, {"a": w_ref}, sems):
                c.start()

        x = prev_ref[...].astype(f32)
        if n_add:
            for a in add_refs:
                x = x + a[...].astype(f32)
            x = x + bias_ref[...]
        stream_ref[...] = x
        mean = jnp.mean(x, axis=1, keepdims=True)
        centered = x - mean
        inv = lax.rsqrt(jnp.mean(centered * centered, axis=1, keepdims=True) + EPSILON)
        unit = centered * inv
        unit_ref[...] = unit.astype(bf16)
        inv_ref[...] = jnp.broadcast_to(inv, inv_ref.shape)
        normed = (unit * gain_ref[...] + shift_ref[...]).astype(bf16)
        normed_ref[...] = normed

        @pl.when(pl.program_id(0) == 0)
        def _():
            for c in assemble_copies(group, shards, own_ref[0], piece_refs, {"a": w_ref}, sems):
                c.wait()

        c, s1, s2 = c_ref[...], s1_ref[...], s2_ref[...]
        q = nn(normed, w_ref[0]) + qkvb_ref[:, :half]
        for j, part in enumerate(spin(q, c, s1, s2)):
            q_ref[:, j * 128 : (j + 1) * 128] = (part * HEAD ** (-0.5)).astype(bf16)
        k = nn(normed, w_ref[1]) + qkvb_ref[:, half : 2 * half]
        for j, part in enumerate(spin(k, c, s1, s2)):
            kv_ref[:, j * 128 : (j + 1) * 128] = part.astype(bf16)
        v = nn(normed, w_ref[2]) + qkvb_ref[:, 2 * half :]
        kv_ref[:, half:] = v.astype(bf16)

    wide = row_blocks(block, width)
    inputs = (
        [(prev, wide)]
        + [(a, wide) for a in adds]
        + [(v, whole(v.shape)) for v in (bias, gain, shift, qkv_b)]
        + [(t, row_blocks(block, 128)) for t in tables]
        + [(p, ANY) for p in pieces]
    )
    S = jax.ShapeDtypeStruct
    outputs = [
        (S((rows, width), f32), wide),
        (S((rows, width), bf16), wide),
        (S((rows, 128), f32), row_blocks(block, 128)),
        (S((rows, width), bf16), wide),
        (S((rows, half), bf16), row_blocks(block, half)),
        (S((rows, 2 * half), bf16), row_blocks(block, 2 * half)),
    ]
    return call(
        kernel, own, inputs, outputs, (rows // block,),
        [pltpu.VMEM((3, width, half), bf16), pltpu.SemaphoreType.DMA((len(plan),))],
        flops=2 * rows * width * 3 * half, bytes_=rows * width * 12 + 3 * width * half * 2,
    )


def gelu_parts(x):
    z = jnp.abs(x) * math.sqrt(0.5)
    t = 1.0 / (1.0 + 0.3275911 * z)
    poly = t * (
        0.254829592 + t * (-0.284496736 + t * (1.421413741 + t * (-1.453152027 + t * 1.061405429)))
    )
    e = jnp.exp(-0.5 * x * x)
    tail = 0.5 * poly * e
    big = jnp.where(x >= 0, 1.0 - tail, tail)
    return x * big, big + x * e * (1.0 / math.sqrt(2.0 * math.pi))


def forward_up(own, normed, up_b, pieces, group, shards, block=256):
    rows, width = normed.shape
    count = len(pieces)
    plan = assembly(group, shards)
    chunks = len(group.blocks)

    def kernel(own_ref, x_ref, b_ref, *rest):
        piece_refs, rest = rest[:count], rest[count:]
        act_ref, slope_ref, w_ref, sems = rest

        @pl.when(pl.program_id(0) == 0)
        def _():
            copies = assemble_copies(group, shards, own_ref[0], piece_refs, {"u": w_ref}, sems)
            for c in copies:
                c.start()
            for c in copies:
                c.wait()

        for j in range(chunks):
            at = slice(j * COLS, (j + 1) * COLS)
            pre = nn(x_ref[...], w_ref[j]) + b_ref[:, at]
            act, slope = gelu_parts(pre)
            act_ref[:, at] = act.astype(bf16)
            slope_ref[:, at] = slope.astype(bf16)

    S = jax.ShapeDtypeStruct
    ff = chunks * COLS
    out = (S((rows, ff), bf16), row_blocks(block, ff))
    return call(
        kernel, own,
        [(normed, row_blocks(block, width)), (up_b, whole(up_b.shape))] + [(p, ANY) for p in pieces],
        [out, out], (rows // block,),
        [pltpu.VMEM((chunks, width, COLS), bf16), pltpu.SemaphoreType.DMA((len(plan),))],
        flops=4 * rows * width * ff, bytes_=rows * ff * 4 + width * ff * 2 + rows * width * 2,
    )


def forward_out(own, attended, activated, pieces, group, shards, block=256):
    rows, ff = activated.shape
    half = attended.shape[1]
    count = len(pieces)
    plan = assembly(group, shards)
    width = 2 * COLS

    def kernel(own_ref, att_ref, act_ref, *rest):
        piece_refs, rest = rest[:count], rest[count:]
        out_ref, d_ref, o_ref, sems = rest

        @pl.when(pl.program_id(0) == 0)
        def _():
            copies = assemble_copies(
                group, shards, own_ref[0], piece_refs, {"d": d_ref, "o": o_ref}, sems
            )
            for c in copies:
                c.start()
            for c in copies:
                c.wait()

        for j in range(2):
            got = nn(att_ref[...], o_ref[j]) + nn(act_ref[...], d_ref[j])
            out_ref[:, j * COLS : (j + 1) * COLS] = got.astype(bf16)

    S = jax.ShapeDtypeStruct
    return call(
        kernel, own,
        [(attended, row_blocks(block, half)), (activated, row_blocks(block, ff))]
        + [(p, ANY) for p in pieces],
        [(S((rows, width), bf16), row_blocks(block, width))], (rows // block,),
        [
            pltpu.VMEM((2, ff, COLS), bf16),
            pltpu.VMEM((2, half, COLS), bf16),
            pltpu.SemaphoreType.DMA((len(plan),)),
        ],
        flops=2 * rows * width * (ff + half), bytes_=(rows + width) * (ff + half) * 2 + rows * width * 2,
    )[0]


def attend(meta, q, kv, halo, doc_start, block=256):
    rows, width = q.shape
    reach = halo.shape[0]
    heads = width // HEAD

    def kernel(meta_ref, q_ref, kv_ref, halo_ref, ds_ref, out_ref, lse_ref, ext_ref, bias_ref, sems):
        b = pl.program_id(0)

        @pl.when(b == 0)
        def _():
            one = pltpu.make_async_copy(halo_ref, ext_ref.at[pl.ds(0, reach), :], sems.at[0])
            two = pltpu.make_async_copy(kv_ref, ext_ref.at[pl.ds(reach, rows), :], sems.at[1])
            one.start()
            two.start()
            one.wait()
            two.wait()

        def variant(skip):
            count = (reach // block + 1 - skip) * block
            first = pl.multiple_of((b + skip) * block, block)
            key = first - reach + lax.broadcasted_iota(jnp.int32, (block, count), 1)
            query = b * block + lax.broadcasted_iota(jnp.int32, (block, count), 0)
            allowed = (key <= query) & (key >= ds_ref[...])
            bias_ref[:, :count] = jnp.where(allowed, 0.0, NEG_FILL)
            lane = lax.broadcasted_iota(jnp.int32, (block, 128), 1)
            lse = jnp.zeros((block, 128), f32)
            for p in range(width // 128):
                q2 = q_ref[:, p * 128 : (p + 1) * 128]
                k2 = ext_ref[pl.ds(first, count), p * 128 : (p + 1) * 128]
                v2 = ext_ref[pl.ds(first, count), width + p * 128 : width + (p + 1) * 128]
                outs = []
                for side in range(2):
                    mine = (lane < HEAD) if side == 0 else (lane >= HEAD)
                    s = nt(jnp.where(mine, q2, jnp.zeros_like(q2)), k2) + bias_ref[:, :count]
                    top = jnp.max(s, axis=1, keepdims=True)
                    e = jnp.exp(s - top)
                    total = jnp.sum(e, axis=1, keepdims=True)
                    outs.append(nn(e.astype(bf16), v2) / total)
                    lse = jnp.where(lane == 2 * p + side, top + jnp.log(total), lse)
                out_ref[:, p * 128 : (p + 1) * 128] = jnp.where(lane < HEAD, outs[0], outs[1]).astype(bf16)
            lse_ref[...] = jnp.transpose(lse)[:heads]

        for skip in range(reach // block + 1):
            pl.when(meta_ref[b] == skip)(lambda skip=skip: variant(skip))

    S = jax.ShapeDtypeStruct
    return call(
        kernel, meta,
        [
            (q, row_blocks(block, width)), (kv, ANY), (halo, ANY), (doc_start, row_blocks(block, 1)),
        ],
        [
            (S((rows, width), bf16), row_blocks(block, width)),
            (S((heads, rows), f32), pl.BlockSpec((heads, block), lambda i, *_: (0, i))),
        ],
        (rows // block,),
        [
            pltpu.VMEM((rows + reach, 2 * width), bf16),
            pltpu.VMEM((block, reach + block), f32),
            pltpu.SemaphoreType.DMA((2,)),
        ],
        flops=8 * rows * 2 * reach * width, bytes_=(rows + reach) * width * 8,
    )


def attend_back(meta, q, kv, halo, doc_start_row, grad, attended, lse, tables, block=256):
    rows, width = q.shape
    reach = halo.shape[0]
    heads = width // HEAD
    steps = rows // block

    def kernel(meta_ref, q_ref, kv_ref, halo_ref, ds_ref, g_ref, o_ref, lse_ref, c_ref, s1_ref, s2_ref,
               dq_ref, dkv_ref, ext_ref, acc_ref, bias_ref, sems):
        b = pl.program_id(0)

        @pl.when(b == 0)
        def _():
            one = pltpu.make_async_copy(halo_ref, ext_ref.at[pl.ds(0, reach), :], sems.at[0])
            two = pltpu.make_async_copy(kv_ref, ext_ref.at[pl.ds(reach, rows), :], sems.at[1])
            one.start()
            two.start()
            acc_ref[...] = jnp.zeros_like(acc_ref)
            one.wait()
            two.wait()

        def variant(skip):
            count = (reach // block + 1 - skip) * block
            first = pl.multiple_of((b + skip) * block, block)
            key = first - reach + lax.broadcasted_iota(jnp.int32, (count, block), 0)
            query = b * block + lax.broadcasted_iota(jnp.int32, (count, block), 1)
            allowed = (key <= query) & (key >= ds_ref[...])
            bias_ref[:count, :] = jnp.where(allowed, 0.0, NEG_FILL)
            lane = lax.broadcasted_iota(jnp.int32, (block, 128), 1)
            wide_lane = lax.broadcasted_iota(jnp.int32, (count, 128), 1)
            for p in range(width // 128):
                at = slice(p * 128, (p + 1) * 128)
                q2, g2 = q_ref[:, at], g_ref[:, at]
                k2 = ext_ref[pl.ds(first, count), at]
                v2 = ext_ref[pl.ds(first, count), width + p * 128 : width + (p + 1) * 128]
                prod = jnp.transpose(g2.astype(f32) * o_ref[:, at].astype(f32))
                dk = dv = dq = None
                for side in range(2):
                    mine = (lane < HEAD) if side == 0 else (lane >= HEAD)
                    qm = jnp.where(mine, q2, jnp.zeros_like(q2))
                    gm = jnp.where(mine, g2, jnp.zeros_like(g2))
                    km = jnp.where((wide_lane < HEAD) if side == 0 else (wide_lane >= HEAD), k2, jnp.zeros_like(k2))
                    h = 2 * p + side
                    delta = jnp.sum(prod[side * HEAD : (side + 1) * HEAD], axis=0, keepdims=True)
                    prob = jnp.exp(nt(k2, qm) + bias_ref[:count, :] - lse_ref[h : h + 1, :])
                    ds = (prob * (nt(v2, gm) - delta)).astype(bf16)
                    one_dv = nn(prob.astype(bf16), gm)
                    one_dk = nn(ds, qm)
                    one_dq = lax.dot_general(ds, km, (((0,), (0,)), ((), ())), preferred_element_type=f32)
                    dv = one_dv if dv is None else dv + one_dv
                    dk = one_dk if dk is None else dk + one_dk
                    dq = one_dq if dq is None else dq + one_dq
                acc_ref[pl.ds(first, count), at] += dk
                acc_ref[pl.ds(first, count), width + p * 128 : width + (p + 1) * 128] += dv
                turned = spin(dq * HEAD ** (-0.5), c_ref[...], -s1_ref[...], -s2_ref[...])
                dq_ref[:, at] = turned[0].astype(bf16)

        for skip in range(reach // block + 1):
            pl.when(meta_ref[b] == skip)(lambda skip=skip: variant(skip))

        @pl.when(b == steps - 1)
        def _():
            dkv_ref[...] = acc_ref[...].astype(bf16)

    S = jax.ShapeDtypeStruct
    narrow = row_blocks(block, width)
    return call(
        kernel, meta,
        [
            (q, narrow), (kv, ANY), (halo, ANY),
            (doc_start_row, pl.BlockSpec((1, block), lambda i, *_: (0, i))),
            (grad, narrow), (attended, narrow),
            (lse, pl.BlockSpec((heads, block), lambda i, *_: (0, i))),
        ]
        + [(t, row_blocks(block, 128)) for t in tables],
        [
            (S((rows, width), bf16), narrow),
            (S((rows + reach, 2 * width), bf16), whole((rows + reach, 2 * width))),
        ],
        (steps,),
        [
            pltpu.VMEM((rows + reach, 2 * width), bf16),
            pltpu.VMEM((rows + reach, 2 * width), f32),
            pltpu.VMEM((reach + block, block), f32),
            pltpu.SemaphoreType.DMA((2,)),
        ],
        flops=20 * rows * 2 * reach * width, bytes_=(rows + reach) * width * 12,
    )


def backward_branch(own, branch, slope, pieces, group, shards, block=256):
    rows, width = branch.shape
    ff = slope.shape[1]
    half = COLS
    count = len(pieces)
    plan = assembly(group, shards)

    def kernel(own_ref, g_ref, slope_ref, *rest):
        piece_refs, rest = rest[:count], rest[count:]
        pre_ref, att_ref, presum_ref, gsum_ref, d_ref, o_ref, sems = rest
        i = pl.program_id(0)

        @pl.when(i == 0)
        def _():
            copies = assemble_copies(
                group, shards, own_ref[0], piece_refs, {"d": d_ref, "o": o_ref}, sems
            )
            for c in copies:
                c.start()
            presum_ref[...] = jnp.zeros_like(presum_ref)
            gsum_ref[...] = jnp.zeros_like(gsum_ref)
            for c in copies:
                c.wait()

        parts = [g_ref[:, j * COLS : (j + 1) * COLS] for j in range(2)]
        att_ref[...] = (nt(parts[0], o_ref[0]) + nt(parts[1], o_ref[1])).astype(bf16)
        for j in range(ff // COLS):
            at = slice(j * COLS, (j + 1) * COLS)
            got = nt(parts[0], d_ref[0, at, :]) + nt(parts[1], d_ref[1, at, :])
            pre = (got * slope_ref[:, at].astype(f32)).astype(bf16)
            pre_ref[:, at] = pre
            presum_ref[:, at] += jnp.sum(pre.astype(f32), axis=0, keepdims=True)

        core = own_ref[1]
        mine = (i * block // (rows // 2)) == core

        @pl.when(mine)
        def _():
            gsum_ref[...] += jnp.sum(g_ref[...].astype(f32), axis=0, keepdims=True)

    S = jax.ShapeDtypeStruct
    return call(
        kernel, own,
        [(branch, row_blocks(block, width)), (slope, row_blocks(block, ff))] + [(p, ANY) for p in pieces],
        [
            (S((rows, ff), bf16), row_blocks(block, ff)),
            (S((rows, half), bf16), row_blocks(block, half)),
            (S((1, ff), f32), whole((1, ff))),
            (S((1, width), f32), whole((1, width))),
        ],
        (rows // block,),
        [
            pltpu.VMEM((2, ff, COLS), bf16),
            pltpu.VMEM((2, half, COLS), bf16),
            pltpu.SemaphoreType.DMA((len(plan),)),
        ],
        flops=2 * rows * width * (ff + half), bytes_=(2 * rows + width) * (ff + half) * 2 + rows * width * 2,
    )


def backward_normed(own, dq, dkv, halo, pre_grad, unit, tables, a_pieces, u_pieces, a_group, u_group, shards, block=256):
    rows, half = dq.shape
    width, ff = unit.shape[1], pre_grad.shape[1]
    reach = halo.shape[0]
    steps, late = rows // block, (rows - reach) // block
    na, nu = len(a_pieces), len(u_pieces)
    plan_a, plan_u = assembly(a_group, shards), assembly(u_group, shards)

    def kernel(own_ref, dq_ref, dkv_ref, halo_ref, pre_ref, unit_ref, c_ref, s1_ref, s2_ref, *rest):
        a_refs, rest = rest[:na], rest[na:]
        u_refs, rest = rest[:nu], rest[nu:]
        packed_ref, part_ref, bsum_ref, gain_ref, shift_ref, a_ref, u_ref, sem_a, sem_u = rest
        i = pl.program_id(0)

        def copies():
            return assemble_copies(a_group, shards, own_ref[0], a_refs, {"a": a_ref}, sem_a) + assemble_copies(
                u_group, shards, own_ref[0], u_refs, {"u": u_ref}, sem_u
            )

        @pl.when(i == 0)
        def _():
            for c in copies():
                c.start()
            for ref in (bsum_ref, gain_ref, shift_ref):
                ref[...] = jnp.zeros_like(ref)

        dkv_now = dkv_ref[...].astype(f32) + jnp.where(i >= late, halo_ref[...].astype(f32), 0.0)
        packed_ref[:, :half] = dq_ref[...]
        for j, part in enumerate(spin(dkv_now[:, :half], c_ref[...], -s1_ref[...], -s2_ref[...])):
            packed_ref[:, half + j * 128 : half + (j + 1) * 128] = part.astype(bf16)
        packed_ref[:, 2 * half :] = dkv_now[:, half:].astype(bf16)

        @pl.when(i == 0)
        def _():
            for c in copies():
                c.wait()

        bsum_ref[...] += jnp.sum(packed_ref[...].astype(f32), axis=0, keepdims=True)
        for n in range(width // COLS):
            at = slice(n * COLS, (n + 1) * COLS)
            total = None
            for j in range(3):
                got = nt(packed_ref[:, j * COLS : (j + 1) * COLS], a_ref[j, at, :])
                total = got if total is None else total + got
            for j in range(ff // COLS):
                total += nt(pre_ref[:, j * COLS : (j + 1) * COLS], u_ref[j, at, :])
            part_ref[:, at] = total.astype(bf16)
            gain_ref[:, at] += jnp.sum(total * unit_ref[:, at].astype(f32), axis=0, keepdims=True)
            shift_ref[:, at] += jnp.sum(total, axis=0, keepdims=True)

    S = jax.ShapeDtypeStruct
    skip = reach // block
    return call(
        kernel, own,
        [
            (dq, row_blocks(block, half)),
            (dkv, pl.BlockSpec((block, 2 * half), lambda i, *_: (i + skip, 0))),
            (halo, pl.BlockSpec((block, 2 * half), lambda i, *_: (jnp.maximum(i - late, 0), 0))),
            (pre_grad, row_blocks(block, ff)),
            (unit, row_blocks(block, width)),
        ]
        + [(t, row_blocks(block, 128)) for t in tables]
        + [(p, ANY) for p in (*a_pieces, *u_pieces)],
        [
            (S((rows, 3 * half), bf16), row_blocks(block, 3 * half)),
            (S((rows, width), bf16), row_blocks(block, width)),
            (S((1, 3 * half), f32), whole((1, 3 * half))),
            (S((1, width), f32), whole((1, width))),
            (S((1, width), f32), whole((1, width))),
        ],
        (steps,),
        [
            pltpu.VMEM((3, width, COLS), bf16),
            pltpu.VMEM((ff // COLS, width, COLS), bf16),
            pltpu.SemaphoreType.DMA((len(plan_a),)),
            pltpu.SemaphoreType.DMA((len(plan_u),)),
        ],
        flops=2 * rows * width * (ff + 3 * half), bytes_=(rows + width) * (ff + 3 * half) * 2 + rows * width * 4,
    )


def norm_backward(own, grad, parts, unit, inv, gain, block=256):
    rows, width = unit.shape

    def kernel(own_ref, g_ref, p0_ref, p1_ref, unit_ref, inv_ref, gain_ref, new_ref, low_ref):
        u = (p0_ref[...].astype(f32) + p1_ref[...].astype(f32)) * gain_ref[...]
        unit = unit_ref[...].astype(f32)
        new = g_ref[...].astype(f32) + inv_ref[:, :1] * (
            u - jnp.mean(u, axis=1, keepdims=True) - unit * jnp.mean(u * unit, axis=1, keepdims=True)
        )
        new_ref[...] = new
        low_ref[...] = new.astype(bf16)

    S = jax.ShapeDtypeStruct
    wide = row_blocks(block, width)
    return call(
        kernel, own,
        [(grad, wide), (parts[0], wide), (parts[1], wide), (unit, wide), (inv, row_blocks(block, 128)),
         (gain, whole(gain.shape))],
        [(S((rows, width), f32), wide), (S((rows, width), bf16), wide)],
        (rows // block,), bytes_=rows * width * 16, flops=rows * width * 10,
    )


def weight_grads(own, lefts, rights, extra, group, first_half, shards):
    rows = rights.shape[0]
    blocks = rights.shape[1] // COLS
    ks = [l.shape[1] // shards for l in lefts]
    height = sum(ks)
    n_left = len(lefts)
    extra_rows = 0 if extra is None else extra.shape[0] // shards
    total = height * blocks + extra_rows
    ranges = piece_ranges(Group([(total, "", 0)], first_half), shards)

    def kernel(own_ref, *refs):
        left_refs, rest = refs[:n_left], refs[n_left:]
        right_ref, rest = rest[0], rest[1:]
        extra_ref, rest = (None, rest) if extra is None else (rest[0], rest[1:])
        out_refs, flipped = rest[: len(ranges)], rest[len(ranges) :]
        for l, t in zip(left_refs, flipped):
            t[...] = jnp.transpose(l[...])

        def store(r, start, value):
            for (rel, lo, hi), ref in zip(ranges, out_refs):
                first, last = max(lo, start), min(hi, start + value.shape[0])
                if rel == r and first < last:
                    ref[first - lo : last - lo, :] = value[first - start : last - start]

        for r in range(shards):
            s = lax.bitwise_xor(own_ref[0], r)
            for j in range(blocks):
                start = j * height
                right = right_ref[:, j * COLS : (j + 1) * COLS]
                for t, k in zip(flipped, ks):
                    left = t[pl.ds(pl.multiple_of(s * k, k), k), :]
                    store(r, start, nn(left, right).astype(bf16))
                    start += k
            if extra is not None:
                store(r, height * blocks, extra_ref[pl.ds(pl.multiple_of(s * extra_rows, extra_rows), extra_rows), :].astype(bf16))

    S = jax.ShapeDtypeStruct
    extras = [] if extra is None else [extra]
    inputs = [(a, whole(a.shape)) for a in (*lefts, rights, *extras)]
    outputs = [(S((hi - lo, COLS), bf16), whole((hi - lo, COLS))) for _, lo, hi in ranges]
    return call(
        kernel, own, inputs, outputs, (1,),
        [pltpu.VMEM((l.shape[1], rows), bf16) for l in lefts],
        flops=2 * rows * sum(l.shape[1] for l in lefts) * rights.shape[1],
        bytes_=2 * (rows * rights.shape[1] + sum(l.size for l in lefts) + shards * total * COLS),
    )


def pick(core, first, second):
    return jnp.where(core == 0, first, second)


def pack_qkv(own, weight, layer, shards):
    _, rows, columns = weight.shape
    w = columns // (6 * shards)

    def kernel(own_ref, w_ref, out_ref):
        core = own_ref[1]
        for g in range(3):
            for s in range(shards):
                at = (g * shards + s) * 2 * w
                out_ref[g * rows : (g + 1) * rows, s * w : (s + 1) * w] = pick(
                    core, w_ref[0, :, at : at + w], w_ref[0, :, at + w : at + 2 * w]
                )

    shape = (3 * rows, COLS)
    return call(
        kernel, own,
        [(weight, pl.BlockSpec((1, rows, columns), lambda i, *_: (layer, 0, 0)))],
        [(jax.ShapeDtypeStruct(shape, bf16), whole(shape))], (1,), bytes_=rows * columns * 3,
    )[0]


def pack_up(own, weight, layer, shards):
    _, rows, columns = weight.shape
    w = columns // (2 * shards)
    blocks = columns // 2 // COLS

    def kernel(own_ref, w_ref, out_ref):
        core = own_ref[1]
        for s in range(shards):
            j, off = s * w // COLS, s * w % COLS
            at = s * 2 * w
            out_ref[j * rows : (j + 1) * rows, off : off + w] = pick(
                core, w_ref[0, :, at : at + w], w_ref[0, :, at + w : at + 2 * w]
            )

    shape = (blocks * rows, COLS)
    return call(
        kernel, own,
        [(weight, pl.BlockSpec((1, rows, columns), lambda i, *_: (layer, 0, 0)))],
        [(jax.ShapeDtypeStruct(shape, bf16), whole(shape))], (1,), bytes_=rows * columns * 3,
    )[0]


def pack_out(own, down, out, layer):
    dr, orows = down.shape[1] // 2, out.shape[1] // 2
    width = down.shape[2]
    blocks = width // COLS

    def kernel(own_ref, d_ref, o_ref, out_ref):
        for j in range(blocks):
            at = slice(j * COLS, (j + 1) * COLS)
            base = j * (dr + orows)
            out_ref[base : base + dr, :] = d_ref[0, :, at]
            out_ref[base + dr : base + dr + orows, :] = o_ref[0, :, at]

    shape = (blocks * (dr + orows), COLS)
    spec = lambda r: pl.BlockSpec((1, r, width), lambda i, own_ref: (layer, own_ref[1], 0))
    return call(
        kernel, own, [(down, spec(dr)), (out, spec(orows))],
        [(jax.ShapeDtypeStruct(shape, bf16), whole(shape))], (1,), bytes_=(dr + orows) * width * 4,
    )[0]


def unpack_columns(own, mine, theirs, before, layer, layers, rows, kinds, w, shards):
    columns = kinds * shards * 2 * w
    blocks = kinds * shards * w // COLS

    def kernel(own_ref, a_ref, b_ref, *rest):
        out_ref = rest[-1]
        core = own_ref[1]
        for g in range(kinds):
            for s in range(shards):
                c = (g * shards + s) * w
                j, off = c // COLS, c % COLS
                a = a_ref[j * rows : (j + 1) * rows, off : off + w].astype(f32)
                b = b_ref[j * rows : (j + 1) * rows, off : off + w].astype(f32)
                out_ref[0, :, 2 * c : 2 * c + w] = pick(core, a, b)
                out_ref[0, :, 2 * c + w : 2 * c + 2 * w] = pick(core, b, a)

    extra = [] if before is None else [(before, ANY)]
    shape = (blocks * rows, COLS)
    return call(
        kernel, own, [(mine, whole(shape)), (theirs, whole(shape))] + extra,
        [(jax.ShapeDtypeStruct((layers, rows, columns), f32),
          pl.BlockSpec((1, rows, columns), lambda i, *_: (layer, 0, 0)))],
        (1,), aliases={} if before is None else {3: 0}, bytes_=rows * columns * 6,
    )[0]


def unpack_rows(own, mine, theirs, befores, layer, layers, heights, width):
    blocks = width // COLS
    total = sum(heights)

    def kernel(own_ref, a_ref, b_ref, *rest):
        out_refs = rest[-len(heights) :]
        core = own_ref[1]
        for j in range(blocks):
            start = j * total
            for h, ref in zip(heights, out_refs):
                a = a_ref[start : start + h, :].astype(f32)
                b = b_ref[start : start + h, :].astype(f32)
                ref[0, :h, j * COLS : (j + 1) * COLS] = pick(core, a, b)
                ref[0, h:, j * COLS : (j + 1) * COLS] = pick(core, b, a)
                start += h

    extra = [] if befores is None else [(b, ANY) for b in befores]
    shape = (blocks * total, COLS)
    return call(
        kernel, own, [(mine, whole(shape)), (theirs, whole(shape))] + extra,
        [(jax.ShapeDtypeStruct((layers, 2 * h, width), f32),
          pl.BlockSpec((1, 2 * h, width), lambda i, *_: (layer, 0, 0))) for h in heights],
        (1,), aliases={} if befores is None else {3 + i: i for i in range(len(heights))},
        bytes_=total * width * 12,
    )


class Net:
    def __init__(self, shards, reps):
        self.shards, self.reps = shards, reps
        self.bits = [1 << b for b in range(shards.bit_length() - 1)]
        self.chips = reps // 2
        self.shard = lax.axis_index("shard")
        self.rep = lax.axis_index("rep")
        self.core = self.rep % 2
        self.chip = self.rep // 2

    def send(self, value, where):
        pairs = []
        for s in range(self.shards):
            for r in range(self.reps):
                to = where(s, r)
                if to is not None:
                    pairs.append((s * self.reps + r, to[0] * self.reps + to[1]))
        return lax.ppermute(value, AXES, pairs)

    def other_core(self, value):
        return self.send(value, lambda s, r: (s, r ^ 1))

    def flip(self, value, bit):
        return self.send(value, lambda s, r: (s ^ bit, r))

    def next_chip(self, value):
        return self.send(value, lambda s, r: (s, r + 2) if r + 2 < self.reps else None)

    def last_chip(self, value):
        return self.send(value, lambda s, r: (s, r - 2) if r >= 2 else None)

    def last_bit(self, relative, half):
        order = self.bits if half == 0 else self.bits[::-1]
        return [b for b in order if relative & b][-1]

    def gather(self, own, group, after=None):
        if after is not None:
            own, _ = lax.optimization_barrier((own, after))
        pieces = {0: own}
        for bit in self.bits:
            pieces[bit] = self.flip(own, bit)
        near = [pieces[bit] for bit in self.bits]
        got = []
        for r, lo, hi in piece_ranges(group, self.shards):
            if bin(r).count("1") <= 1:
                got.append(pieces[r])
                continue
            half = 0 if lo == 0 else 1
            bit = self.last_bit(r, half)
            source = pieces[r ^ bit]
            part = source[half] if isinstance(source, list) else source[lo:hi]
            pieces.setdefault(r, []).append(self.flip(part, bit))
            got.append(pieces[r][-1])
        return got, near

    def scatter_sum(self, arrays, group):
        ranges = piece_ranges(group, self.shards)
        acc = {}
        for (r, lo, hi), a in zip(ranges, arrays):
            acc.setdefault(r, []).append((lo, hi, a))
        for r in sorted(range(1, self.shards), key=lambda r: (-bin(r).count("1"), r)):
            for lo, hi, a in acc[r]:
                half = 0 if lo == 0 else 1
                bit = self.last_bit(r, half)
                came = self.flip(a, bit)
                target = acc[r ^ bit]
                for i, (tlo, thi, t) in enumerate(target):
                    first, last = max(lo, tlo), min(hi, thi)
                    if first >= last:
                        continue
                    part = came[first - lo : last - lo]
                    if (first, last) == (tlo, thi):
                        new = t.astype(f32) + part.astype(f32)
                    else:
                        new = t.astype(f32) + jnp.pad(
                            part.astype(f32), ((first - tlo, thi - last), (0, 0))
                        )
                    target[i] = (tlo, thi, new.astype(bf16))
        return acc[0][0][2]

    def sum_chips(self, value):
        chips = self.chips
        line = 4 if chips % 4 == 0 else 1
        if line == 4:
            at = self.chip % 4

            def inward(s, r):
                z = (r // 2) % 4
                return (s, r + 2) if z == 0 else (s, r - 2) if z == 3 else None

            def across(s, r):
                z = (r // 2) % 4
                return (s, r + 2) if z == 1 else (s, r - 2) if z == 2 else None

            def outward(s, r):
                z = (r // 2) % 4
                return (s, r - 2) if z == 1 else (s, r + 2) if z == 2 else None

            value = (value.astype(f32) + self.send(value, inward).astype(f32)).astype(bf16)
            value = (value.astype(f32) + self.send(value, across).astype(f32)).astype(bf16)
            back = self.send(value, outward)
            value = jnp.where((at == 0) | (at == 3), back, value)
        step = line
        while step < chips:
            came = self.send(value, lambda s, r, step=step: (s, r ^ (2 * step)))
            value = (value.astype(f32) + came.astype(f32)).astype(bf16)
            step *= 2
        return value


def core_columns(core, rows, kinds, shards):
    cut = rows.reshape(rows.shape[0], kinds * shards, 2, -1)
    return pick(core, cut[:, :, 0], cut[:, :, 1]).reshape(rows.shape[0], -1)


def body(
    tokens,
    token_order,
    lengths,
    cotangent,
    norm_gain,
    norm_shift,
    qkv_weight,
    qkv_bias,
    out_weight,
    out_bias,
    up_weight,
    up_bias,
    down_weight,
    down_bias,
):
    net = Net(lax.axis_size("shard"), lax.axis_size("rep"))
    shards, core = net.shards, net.core
    layers = norm_gain.shape[0]
    row_count, width = tokens.shape
    rows = 2 * row_count
    reach = row_count
    block = 256
    piece = width // shards
    ff = up_weight.shape[2] // 2
    group_first = net.shard * row_count * net.reps
    chip_first = net.chip * rows
    own = jnp.stack([net.shard, core]).astype(jnp.int32)

    ff_piece, head_piece = ff // shards, width // 2 // shards
    group_a = Group([(piece, "a", j) for j in range(3)], 3 * piece // 2)
    group_u = Group([(piece, "u", j) for j in range(ff // COLS)], piece * (ff // COLS) // 2)
    group_o = Group(
        [b for j in range(2) for b in ((ff_piece, "d", j), (head_piece, "o", j))], ff_piece + head_piece
    )
    grads_a = Group([(3 * piece + 16, "", 0)], 3 * piece // 2)

    after = None
    gathered = []
    for l in range(layers):
        layer = []
        for group, packed in (
            (group_a, lambda: pack_qkv(own, qkv_weight, l, shards)),
            (group_u, lambda: pack_up(own, up_weight, l, shards)),
            (group_o, lambda: pack_out(own, down_weight, out_weight, l)),
        ):
            got, after = net.gather(packed(), group, after)
            layer.append(got)
        gathered.append(layer)

    names = (norm_gain, norm_shift, qkv_bias, out_bias, up_bias, down_bias)
    small = lax.all_gather(jnp.concatenate([v.reshape(-1) for v in names]), "shard", axis=0)
    vectors, offset = [], 0
    for v in names:
        part = small[:, offset : offset + v.size].reshape((shards,) + v.shape)
        vectors.append(jnp.moveaxis(part, 0, 1).reshape(layers, -1).astype(f32))
        offset += v.size
    gains, shifts, qkv_b, out_b, up_b, down_b = vectors
    qkv_b = core_columns(core, qkv_b, 3, shards)
    up_b = core_columns(core, up_b, 1, shards)
    branch_b = out_b + down_b

    slots = lengths.shape[0]
    before = jnp.arange(slots)[None, :] < jnp.arange(slots)[:, None]
    dealt_start = jnp.sum(jnp.where(before, lengths[None, :], 0), axis=1)
    hit = dealt_start[:, None] == jnp.arange(row_count)[None, :]
    home = jnp.sum(jnp.where(hit, token_order[None, :], 0), axis=1) - group_first
    docs = lax.all_gather(jnp.stack([home, lengths]), "rep", axis=0)
    home, length = docs[:, 0].reshape(-1), docs[:, 1].reshape(-1)
    place = chip_first + jnp.arange(rows, dtype=jnp.int32)
    inside = (home[None, :] <= place[:, None]) & (place[:, None] < (home + length)[None, :])
    doc_start = jnp.sum(jnp.where(inside, home[None, :], 0), axis=1) - chip_first
    earliest = jnp.min(doc_start.reshape(rows // block, block), axis=1)
    meta = jnp.clip((earliest + reach) // block - jnp.arange(rows // block), 0, reach // block)
    meta = meta.astype(jnp.int32)
    start_column, start_row = doc_start[:, None], doc_start[None, :]

    lane = jnp.arange(128) % HEAD
    positions = (jnp.arange(rows, dtype=jnp.int32) - doc_start).astype(f32)
    inverse_freq = jnp.exp((lane % (ROT // 2)).astype(f32) * (-2.0 * math.log(10000.0) / ROT))
    angles = positions[:, None] * inverse_freq[None, :]
    sine = jnp.sin(angles)
    tables = (
        jnp.where(lane < ROT, jnp.cos(angles), 1.0),
        jnp.where(lane < ROT // 2, -sine, 0.0),
        jnp.where((lane >= ROT // 2) & (lane < ROT), sine, 0.0),
    )

    def pair_rows(x):
        other = net.other_core(x)
        return jnp.concatenate([pick(core, x, other), pick(core, other, x)])

    def own_rows(x):
        return lax.dynamic_slice_in_dim(x, core * row_count, row_count)

    stream, adds = pair_rows(tokens), []
    saved = []
    bias = jnp.zeros((1, width), f32)
    for l in range(layers):
        a_pieces, u_pieces, o_pieces = gathered[l]
        stream, unit, inv, normed, q, kv = forward_qkv(
            own, stream, adds, bias, gains[l : l + 1], shifts[l : l + 1], qkv_b[l : l + 1], tables,
            a_pieces, group_a, shards,
        )
        halo = net.next_chip(kv[rows - reach :])
        activated, slope = forward_up(own, normed, up_b[l : l + 1], u_pieces, group_u, shards)
        attended, lse = attend(meta, q, kv, halo, start_column)
        partial = forward_out(own, attended, activated, o_pieces, group_o, shards)
        adds = [partial, net.other_core(partial)]
        bias = branch_b[l : l + 1]
        saved.append((unit, inv, normed, q, kv, halo, activated, slope, attended, lse))
    block_output = (
        own_rows(stream) + own_rows(adds[0]).astype(f32) + own_rows(adds[1]).astype(f32) + bias
    ).astype(bf16)

    branch = pair_rows(cotangent)
    grad = branch
    reduced = [None] * layers
    for l in reversed(range(layers)):
        a_pieces, u_pieces, o_pieces = gathered[l]
        unit, inv, normed, q, kv, halo, activated, slope, attended, lse = saved[l]
        o_sum = net.scatter_sum(
            weight_grads(own, [activated, attended], branch, None, None, group_o.first_half, shards), group_o
        )
        pre_grad, attended_grad, up_sum, branch_sum = backward_branch(
            own, branch, slope, o_pieces, group_o, shards
        )
        dq, dkv = attend_back(meta, q, kv, halo, start_row, attended_grad, attended, lse, tables)
        halo_grad = net.last_chip(dkv[:reach])
        u_sum = net.scatter_sum(
            weight_grads(own, [normed], pre_grad, None, None, group_u.first_half, shards), group_u
        )
        packed_grad, part, qkv_sum, gain_sum, shift_sum = backward_normed(
            own, dq, dkv, halo_grad, pre_grad, unit, tables, a_pieces, u_pieces, group_a, group_u, shards
        )
        came = net.other_core(part)

        def line(v, width):
            v = v.reshape(shards, -1)
            return jnp.pad(v, ((0, 0), (0, width - v.shape[1])))

        qkv_sum = qkv_sum.reshape(3 * shards, 1, -1)
        nothing = jnp.zeros_like(qkv_sum)
        qkv_sum = jnp.concatenate(
            [pick(core, qkv_sum, nothing), pick(core, nothing, qkv_sum)], axis=1
        )
        extra = jnp.concatenate(
            [
                line(gain_sum, COLS // 2),
                line(shift_sum, COLS // 2),
                line(branch_sum, COLS),
                line(up_sum, COLS),
                line(qkv_sum, 13 * COLS),
            ],
            axis=1,
        ).reshape(shards * 16, COLS)
        a_sum = net.scatter_sum(
            weight_grads(own, [normed], packed_grad, extra, None, group_a.first_half, shards), grads_a
        )
        reduced[l] = (a_sum, u_sum, o_sum)
        grad, branch = norm_backward(own, grad, [part, came], unit, inv, gains[l : l + 1])
    input_grad = own_rows(branch)

    qkv_g = up_g = out_g = down_g = None
    smalls = [None] * layers
    for l in reversed(range(layers)):
        final = [net.sum_chips(v) for v in reduced[l]]
        theirs = [net.other_core(v) for v in final]
        o_before = None if down_g is None else [down_g, out_g]
        down_g, out_g = unpack_rows(
            own, final[2], theirs[2], o_before, l, layers, (ff_piece, head_piece), width
        )
        up_g = unpack_columns(
            own, final[1], theirs[1], up_g, l, layers, piece, 1, ff_piece, shards
        )
        qkv_g = unpack_columns(
            own, final[0], theirs[0], qkv_g, l, layers, piece, 3, head_piece, shards
        )
        smalls[l] = (final[0][3 * piece :], theirs[0][3 * piece :])
    mine, theirs = (jnp.stack([s[i] for s in smalls]).astype(f32) for i in range(2))
    low, high = pick(core, mine, theirs), pick(core, theirs, mine)
    both = low + high
    branch_g = both[:, 1, :piece]
    return (
        block_output,
        input_grad,
        both[:, 0, :piece],
        both[:, 0, COLS // 2 : COLS // 2 + piece],
        qkv_g,
        both[:, 3:5].reshape(layers, -1)[:, : 3 * piece],
        out_g,
        branch_g,
        up_g,
        jnp.concatenate([low[:, 2, :ff_piece], high[:, 2, :ff_piece]], axis=1),
        down_g,
        branch_g,
    )


def solution(mesh):
    rows = P(("shard", "rep"), None)
    vector, matrix = P(None, "shard"), P(None, "shard", None)
    line = P(("shard", "rep"))
    return jax.shard_map(
        body,
        mesh=mesh,
        in_specs=(
            rows, line, line, rows, vector, vector, matrix, vector, matrix, vector,
            matrix, vector, matrix, vector,
        ),
        out_specs=(
            rows, rows, vector, vector, matrix, vector, matrix, vector, matrix, vector,
            matrix, vector,
        ),
        check_vma=False,
    )
```

time: 1790 us -> 899 us (0.50)
  waiting for transfers between devices: 1120 us -> 312 us
  matrix products: 312 us -> 0 us
  Pallas kernels: 0 us -> 290 us
  starting transfers between devices: 1.26 us -> 147 us
  blocking collectives: 129 us -> 31.8 us
  local copies, waits for them, and re-layouts: 112 us -> 47.6 us
  other arithmetic: 88.5 us -> 58.1 us
    all_gather x12 -> x0, waiting for transfers between devices: 495 us -> none  [the longest x8 339 us: body(): lax.all_gather(as_sent(layer_slices(stacked, layer_index)), 'shard', axis...]
    reduce_scatter x8 -> x0, waiting for transfers between devices: 374 us -> none  [the longest x2 180 us: body(): lax.psum_scatter(local_grads[8].astype(jnp.bfloat16), 'shard', scatter_di...]
    dot_general x36 -> x0, matrix products: 312 us -> none  [the longest x8 65.1 us: times_transposed(): lax.dot_general(left, right, (((1,), (1,)), ((), ())), preferred_element_...]
    ppermute x0 -> x82, waiting for transfers between devices: none -> 312 us  [send(): return lax.ppermute(value, AXES, pairs)]
    pallas_call x0 -> x34, Pallas kernels: none -> 290 us  [call(): pl.pallas_call(kernel, grid_spec=pltpu.PrefetchScalarGridSpec(num_scalar_...]
    psum x1 -> x0, waiting for transfers between devices: 249 us -> none  [body(): lax.psum(scattered[2].astype(jnp.bfloat16), 'rep').astype(jnp.float32)]
    ppermute x0 -> x82, starting transfers between devices: none -> 147 us  [send(): return lax.ppermute(value, AXES, pairs)]
    all_gather x13 -> x2, blocking collectives: 90 us -> 31.8 us  [the longest x1 17.3 us: body(): lax.all_gather(jnp.concatenate([v.reshape(-1) for v in names]), 'shard',...]
  transfers between devices with their start and end apart: 21 -> 82, of which waited for: 16 -> 22; matrix products, arithmetic and copies ran while one was open for 27% -> 9% of each run, Pallas kernels for 0% -> 32%
where the time goes in v1:
time: 899 us; the launch traced here: 890 us
  waiting for transfers between devices  312 us (35%)
  Pallas kernels  290 us (32%)
  starting transfers between devices  147 us (16%)
  other arithmetic  58.1 us (6%)
  local copies, waits for them, and re-layouts  47.6 us (5%)
  blocking collectives  31.8 us (4%)
    ppermute x82, waiting for transfers between devices, send(): return lax.ppermute(value, AXES, pairs)  312 us
    pallas_call x34, Pallas kernels, call(): pl.pallas_call(kernel, grid_spec=pltpu.PrefetchScalarGridSpec(num_scalar_...  290 us
    ppermute x82, starting transfers between devices, send(): return lax.ppermute(value, AXES, pairs)  147 us
    convert_element_type x18, other arithmetic, scatter_sum(): target[i] = (tlo, thi, new.astype(bf16))  27.2 us
    unnamed x226, local copies, waits for them, and re-layouts  27 us
  transfers between devices with their start and end apart: 82, of which 22 were waited for; matrix products, arithmetic and copies ran while one was open for 9% of the time, Pallas kernels for 32%

profile of v1, /device:TPU:1, one launch (start us, length us, event | category | flops | bytes accessed | tf_op | source)
XLA Modules:
  0.0 889.5 jit_solution(9979046847901749607)
XLA Ops:
  9.1 17.3 %all-gather.2 = bf16[4,1,5632]{2,1,0:T(2,128)(2,1)S(1)} all-gather(bf16[1,1,5632]{2,1,0:T(2,128)(2,1)S(1)} %reshape.309), channel_id=2, replica_groups=mesh['shard'=4,'rep'=8] {'shard'}, dimensions={0}, use_global_device_ids=true | all-gather | bytes 56320 | tf_op jit(solution)/shard_map/all_gather | solution.py:928
  27.0 14.5 %all-gather.3 = s32[8,2,4]{2,1,0:T(2,128)S(1)} all-gather(s32[1,2,4]{2,1,0:T(2,128)S(1)} %add_bitcast_fusion), channel_id=3, replica_groups=mesh['shard'=4,'rep'=8] {'rep'}, dimensions={0}, use_global_device_ids=true | all-gather | bytes 288 | tf_op jit(solution)/shard_map/all_gather | solution.py:944
  54.1 25.6 %collective-permute-done.3.refs_11_.rest_3_ = bf16[384,512]{1,0:T(8,128)(2,1)S(1)} collective-permute-done((bf16[384,512]{1,0:T(8,128)(2,1)S(1)}, bf16[384,512]{1,0:T(8,128)(2,1)S(1)}, u32[]{:S(2)}, u32[]{:S(2)}) %collective-permute-start.3) | collective-permute-done | bytes 393248 | tf_op jit(solution)/shard_map/ppermute | solution.py:779
  118.3 12.4 %shard_map.231 = (bf16[1024,512]{1,0:T(8,128)(2,1)S(1)}, f32[8,1024]{1,0:T(8,128)S(1)}) custom-call(s32[4]{0:T(128)S(1)} %subtract_clamp_fusion.meta_ref, bf16[1024,512]{1,0:T(8,128)(2,1)S(1)} %copy-done.69, bf16[1024,1024]{1,0:T(8,128)(2,1)S(1)} %copy-done.31, bf16[512,1024]{1,0:T(8,128)(2,1)} %collective-permute-done.5.halo_ref, s32[1024,1]{1,0:T(8,128)S(1)} %copy-done.33), custom_call_target="tpu_custom_call" | custom-call | flops 4294967296 | bytes 6291456 | tf_op jit(solution)/shard_map/pallas_call | solution.py:42
  139.6 15.6 %shard_map.233 = (bf16[1024,2048]{1,0:T(8,128)(2,1)}, bf16[1024,2048]{1,0:T(8,128)(2,1)}) custom-call(s32[2]{0:T(128)S(1)} %pad_add_fusion.own_ref, bf16[1024,1024]{1,0:T(8,128)(2,1)} %get-tuple-element.100.x_ref.refs_0_, f32[1,2048]{1,0:T(1,128)S(1)} %bitcast.100, bf16[1024,512]{1,0:T(8,128)(2,1)S(1)} %copy-done.19, bf16[1024,512]{1,0:T(8,128)(2,1)S(1)} %copy-done.40, ...), custom_call_target="tpu_custom_call" | custom-call | flops 8589934592 | bytes 14680064 | tf_op jit(solution)/shard_map/pallas_call | solution.py:42
  156.8 12.1 %shard_map.235.refs_1_ = bf16[1024,1024]{1,0:T(8,128)(2,1)} custom-call(s32[2]{0:T(128)S(1)} %pad_add_fusion.own_ref, bf16[1024,512]{1,0:T(8,128)(2,1)S(1)} %get-tuple-element.99.att_ref.o_ref.refs_1_, bf16[1024,2048]{1,0:T(8,128)(2,1)} %get-tuple-element.102.act_ref.refs_0_, bf16[1280,512]{1,0:T(8,128)(2,1)} %shard_map.234.rest_0_, ...), custom_call_target="tpu_custom_call" | custom-call | flops 5368709120 | bytes 12582912 | tf_op jit(solution)/shard_map/pallas_call | solution.py:42
  180.7 18.5 %collective-permute-done.20.rest_1_.rest_6_ = bf16[1024,512]{1,0:T(8,128)(2,1)S(1)} collective-permute-done((bf16[1024,512]{1,0:T(8,128)(2,1)S(1)}, bf16[1024,512]{1,0:T(8,128)(2,1)S(1)}, u32[]{:S(2)}, u32[]{:S(2)}) %collective-permute-start.20) | collective-permute-done | bytes 1048608 | tf_op jit(solution)/shard_map/ppermute | solution.py:779
  229.5 17.0 %collective-permute-done.22.rest_3_.rest_8_ = bf16[512,512]{1,0:T(8,128)(2,1)S(1)} collective-permute-done((bf16[512,512]{1,0:T(8,128)(2,1)S(1)}, bf16[512,512]{1,0:T(8,128)(2,1)S(1)}, u32[]{:S(2)}, u32[]{:S(2)}) %collective-permute-start.22) | collective-permute-done | bytes 524320 | tf_op jit(solution)/shard_map/ppermute | solution.py:779
  247.7 15.6 %shard_map.240 = (bf16[1024,2048]{1,0:T(8,128)(2,1)}, bf16[1024,2048]{1,0:T(8,128)(2,1)}) custom-call(s32[2]{0:T(128)S(1)} %pad_add_fusion.own_ref, bf16[1024,1024]{1,0:T(8,128)(2,1)} %get-tuple-element.109.x_ref.refs_0_, f32[1,2048]{1,0:T(1,128)S(1)} %bitcast.99, bf16[1024,512]{1,0:T(8,128)(2,1)S(1)} %shard_map.239.rest_0_.rest_5_, ...), custom_call_target="tpu_custom_call" | custom-call | flops 8589934592 | bytes 14680064 | tf_op jit(solution)/shard_map/pallas_call | solution.py:42
  291.2 12.1 %shard_map.243 = (bf16[1024,2048]{1,0:T(8,128)(2,1)}, bf16[1024,512]{1,0:T(8,128)(2,1)S(1)}, f32[1,2048]{1,0:T(1,128)S(1)}, f32[1,1024]{1,0:T(1,128)S(1)}) custom-call(s32[2]{0:T(128)S(1)} %pad_add_fusion.own_ref, bf16[1024,1024]{1,0:T(8,128)(2,1)} %pad_maximum_fusion.1.g_ref.refs_2_, bf16[1024,2048]{1,0:T(8,128)(2,1)} %get-tuple-element.113.slope_ref, ...), custom_call_target="tpu_custom_call" | custom-call | flops 5368709120 | bytes 17825792 | tf_op jit(solution)/shard_map/pallas_call | solution.py:42
  316.1 19.2 %shard_map.244 = (bf16[1024,512]{1,0:T(8,128)(2,1)S(1)}, bf16[1536,1024]{1,0:T(8,128)(2,1)}) custom-call(s32[4]{0:T(128)S(1)} %subtract_clamp_fusion.meta_ref, bf16[1024,512]{1,0:T(8,128)(2,1)S(1)} %copy-done.51, bf16[1024,1024]{1,0:T(8,128)(2,1)} %get-tuple-element.107.kv_ref, bf16[512,1024]{1,0:T(8,128)(2,1)S(1)} %collective-permute-done.19.halo_ref, ...), custom_call_target="tpu_custom_call" | custom-call | flops 10737418240 | bytes 9437184 | tf_op jit(solution)/shard_map/pallas_call | solution.py:42
  364.3 16.4 %shard_map.245 = (bf16[1024,1536]{1,0:T(8,128)(2,1)}, bf16[1024,1024]{1,0:T(8,128)(2,1)}, f32[1,1536]{1,0:T(1,128)S(1)}, f32[1,1024]{1,0:T(1,128)S(1)}, f32[1,1024]{1,0:T(1,128)S(1)}) custom-call(s32[2]{0:T(128)S(1)} %pad_add_fusion.own_ref, bf16[1024,512]{1,0:T(8,128)(2,1)} %copy-done.76, bf16[1536,1024]{1,0:T(8,128)(2,1)} %get-tuple-element.117.dkv_ref, ...), custom_call_target="tpu_custom_call" | custom-call | flops 7516192768 | bytes 18874368 | tf_op jit(solution)/shard_map/pallas_call | solution.py:42
  407.1 13.2 %collective-permute-done.42 = bf16[784,512]{1,0:T(8,128)(2,1)} collective-permute-done((bf16[784,512]{1,0:T(8,128)(2,1)}, bf16[784,512]{1,0:T(8,128)(2,1)}, u32[]{:S(2)}, u32[]{:S(2)}) %collective-permute-start.42) | collective-permute-done | bytes 802848 | tf_op jit(solution)/shard_map/ppermute | solution.py:779
  465.7 13.1 %collective-permute-done.45 = bf16[784,512]{1,0:T(8,128)(2,1)S(1)} collective-permute-done((bf16[784,512]{1,0:T(8,128)(2,1)S(1)}, bf16[784,512]{1,0:T(8,128)(2,1)S(1)}, u32[]{:S(2)}, u32[]{:S(2)}) %collective-permute-start.45) | collective-permute-done | bytes 802848 | tf_op jit(solution)/shard_map/ppermute | solution.py:779
  491.4 12.2 %shard_map.247 = (bf16[1024,2048]{1,0:T(8,128)(2,1)}, bf16[1024,512]{1,0:T(8,128)(2,1)S(1)}, f32[1,2048]{1,0:T(1,128)S(1)}, f32[1,1024]{1,0:T(1,128)S(1)}) custom-call(s32[2]{0:T(128)S(1)} %pad_add_fusion.own_ref, bf16[1024,1024]{1,0:T(8,128)(2,1)} %copy-done.50, bf16[1024,2048]{1,0:T(8,128)(2,1)} %get-tuple-element.124.slope_ref, ...), custom_call_target="tpu_custom_call" | custom-call | flops 5368709120 | bytes 17825792 | tf_op jit(solution)/shard_map/pallas_call | solution.py:42
  503.6 19.4 %shard_map.248 = (bf16[1024,512]{1,0:T(8,128)(2,1)S(1)}, bf16[1536,1024]{1,0:T(8,128)(2,1)}) custom-call(s32[4]{0:T(128)S(1)} %subtract_clamp_fusion.meta_ref, bf16[1024,512]{1,0:T(8,128)(2,1)S(1)} %copy-done.70, bf16[1024,1024]{1,0:T(8,128)(2,1)} %get-tuple-element.98.kv_ref, bf16[512,1024]{1,0:T(8,128)(2,1)} %collective-permute-done.5.halo_ref, ...), custom_call_target="tpu_custom_call" | custom-call | flops 10737418240 | bytes 9437184 | tf_op jit(solution)/shard_map/pallas_call | solution.py:42
  565.0 30.7 %collective-permute-done.32.halo_ref = bf16[512,1024]{1,0:T(8,128)(2,1)S(1)} collective-permute-done((bf16[512,1024]{1,0:T(8,128)(2,1)S(1)}, bf16[512,1024]{1,0:T(8,128)(2,1)S(1)}, u32[]{:S(2)}, u32[]{:S(2)}) %collective-permute-start.32) | collective-permute-done | bytes 1048608 | tf_op jit(solution)/shard_map/ppermute | solution.py:779
  596.7 16.8 %shard_map.249 = (bf16[1024,1536]{1,0:T(8,128)(2,1)}, bf16[1024,1024]{1,0:T(8,128)(2,1)}, f32[1,1536]{1,0:T(1,128)S(1)}, f32[1,1024]{1,0:T(1,128)S(1)}, f32[1,1024]{1,0:T(1,128)S(1)}) custom-call(s32[2]{0:T(128)S(1)} %pad_add_fusion.own_ref, bf16[1024,512]{1,0:T(8,128)(2,1)} %copy-done.75, bf16[1536,1024]{1,0:T(8,128)(2,1)} %get-tuple-element.128.dkv_ref, ...), custom_call_target="tpu_custom_call" | custom-call | flops 7516192768 | bytes 18874368 | tf_op jit(solution)/shard_map/pallas_call | solution.py:42
  636.3 21.9 %collective-permute-done.36 = bf16[400,512]{1,0:T(8,128)(2,1)S(1)} collective-permute-done((bf16[400,512]{1,0:T(8,128)(2,1)S(1)}, bf16[400,512]{1,0:T(8,128)(2,1)S(1)}, u32[]{:S(2)}, u32[]{:S(2)}) %collective-permute-start.36) | collective-permute-done | bytes 409632 | tf_op jit(solution)/shard_map/ppermute | solution.py:779
  665.8 19.1 %collective-permute-start.70 = (bf16[1024,512]{1,0:T(8,128)(2,1)S(1)}, bf16[1024,512]{1,0:T(8,128)(2,1)S(1)}, u32[]{:S(2)}, u32[]{:S(2)}) collective-permute-start(bf16[1024,512]{1,0:T(8,128)(2,1)S(1)} %add_convert_fusion.20), channel_id=1, source_target_pairs={{0,2},{1,3},{6,4},{7,5},{8,10},{9,11},{14,12},{15,13},{16,18},{17,... | collective-permute-start | bytes 3145736 | tf_op jit(solution)/shard_map/ppermute | solution.py:779
  726.6 16.1 %collective-permute-done.38 = bf16[784,512]{1,0:T(8,128)(2,1)S(1)} collective-permute-done((bf16[784,512]{1,0:T(8,128)(2,1)S(1)}, bf16[784,512]{1,0:T(8,128)(2,1)S(1)}, u32[]{:S(2)}, u32[]{:S(2)}) %collective-permute-start.38) | collective-permute-done | bytes 802848 | tf_op jit(solution)/shard_map/ppermute | solution.py:779
  779.8 46.5 %collective-permute-done.40 = bf16[784,512]{1,0:T(8,128)(2,1)} collective-permute-done((bf16[784,512]{1,0:T(8,128)(2,1)S(1)}, bf16[784,512]{1,0:T(8,128)(2,1)}, u32[]{:S(2)}, u32[]{:S(2)}) %collective-permute-start.40) | collective-permute-done | bytes 802848 | tf_op jit(solution)/shard_map/ppermute | solution.py:779
  828.5 20.1 %collective-permute-done.72 = bf16[1024,512]{1,0:T(8,128)(2,1)S(1)} collective-permute-done((bf16[1024,512]{1,0:T(8,128)(2,1)S(1)}, bf16[1024,512]{1,0:T(8,128)(2,1)S(1)}, u32[]{:S(2)}, u32[]{:S(2)}) %collective-permute-start.72) | collective-permute-done | bytes 1048608 | tf_op jit(solution)/shard_map/ppermute | solution.py:779
  849.6 27.1 %collective-permute-done.56 = bf16[1280,512]{1,0:T(8,128)(2,1)S(1)} collective-permute-done((bf16[1280,512]{1,0:T(8,128)(2,1)S(1)}, bf16[1280,512]{1,0:T(8,128)(2,1)S(1)}, u32[]{:S(2)}, u32[]{:S(2)}) %collective-permute-start.56) | collective-permute-done | bytes 1310752 | tf_op jit(solution)/shard_map/ppermute | solution.py:779
  (543 shorter events, 434.1 us)
Async XLA Ops:
  46.6 51.6 %collective-permute-start.6 = (bf16[1024,512]{1,0:T(8,128)(2,1)S(1)}, bf16[1024,512]{1,0:T(8,128)(2,1)S(1)}, u32[]{:S(2)}, u32[]{:S(2)}) collective-permute-start(bf16[1024,512]{1,0:T(8,128)(2,1)S(1)} %shard_map.232.rest_0_.rest_5_), channel_id=1, source_target_pairs={{0,8},{1,9},{2,10},{3,11},{4,12},{5,13},{6,14},{7,15},{8,0},{9,1},... | collective-permute-start | bytes 3145736 | tf_op jit(solution)/shard_map/ppermute | solution.py:779
  47.0 51.3 %collective-permute-start.7 = (bf16[1024,512]{1,0:T(8,128)(2,1)S(1)}, bf16[1024,512]{1,0:T(8,128)(2,1)S(1)}, u32[]{:S(2)}, u32[]{:S(2)}) collective-permute-start(bf16[1024,512]{1,0:T(8,128)(2,1)S(1)} %shard_map.232.rest_0_.rest_5_), channel_id=1, source_target_pairs={{0,16},{1,17},{2,18},{3,19},{4,20},{5,21},{6,22},{7,23},{8,24},{9,... | collective-permute-start | bytes 3145736 | tf_op jit(solution)/shard_map/ppermute | solution.py:779
  176.5 47.1 %collective-permute-start.29 = (bf16[512,1024]{1,0:T(8,128)(2,1)S(1)}, bf16[512,1024]{1,0:T(8,128)(2,1)S(1)}, u32[]{:S(2)}, u32[]{:S(2)}) collective-permute-start(bf16[512,1024]{1,0:T(8,128)(2,1)S(1)} %copy-done.83), channel_id=1, source_target_pairs={{0,1},{1,0},{2,3},{3,2},{4,5},{5,4},{6,7},{7,6},{8,9},{9,8},{10,11... | collective-permute-start | bytes 3145736 | tf_op jit(solution)/shard_map/ppermute | solution.py:779
  199.3 64.1 %collective-permute-start.24 = (bf16[1280,512]{1,0:T(8,128)(2,1)S(1)}, bf16[1280,512]{1,0:T(8,128)(2,1)S(1)}, u32[]{:S(2)}, u32[]{:S(2)}) collective-permute-start(bf16[1280,512]{1,0:T(8,128)(2,1)S(1)} %shard_map.241.rest_0_), channel_id=1, source_target_pairs={{0,8},{1,9},{2,10},{3,11},{4,12},{5,13},{6,14},{7,15},{8,0},{9,1},... | collective-permute-start | bytes 3932168 | tf_op jit(solution)/shard_map/ppermute | solution.py:779
  206.7 57.6 %collective-permute-start.25 = (bf16[1280,512]{1,0:T(8,128)(2,1)S(1)}, bf16[1280,512]{1,0:T(8,128)(2,1)}, u32[]{:S(2)}, u32[]{:S(2)}) collective-permute-start(bf16[1280,512]{1,0:T(8,128)(2,1)S(1)} %shard_map.241.rest_0_), channel_id=1, source_target_pairs={{0,16},{1,17},{2,18},{3,19},{4,20},{5,21},{6,22},{7,23},{8,24},{9,... | collective-permute-start | bytes 3932168 | tf_op jit(solution)/shard_map/ppermute | solution.py:779
  291.0 99.6 %collective-permute-start.60 = (bf16[640,512]{1,0:T(8,128)(2,1)}, bf16[640,512]{1,0:T(8,128)(2,1)}, u32[]{:S(2)}, u32[]{:S(2)}) collective-permute-start(bf16[640,512]{1,0:T(8,128)(2,1)} %get-tuple-element.165), channel_id=1, source_target_pairs={{0,8},{1,9},{2,10},{3,11},{4,12},{5,13},{6,14},{7,15},{8,0},{9,1},... | collective-permute-start | bytes 1966088 | tf_op jit(solution)/shard_map/ppermute | solution.py:779
  291.0 107.9 %collective-permute-start.58 = (bf16[640,512]{1,0:T(8,128)(2,1)}, bf16[640,512]{1,0:T(8,128)(2,1)}, u32[]{:S(2)}, u32[]{:S(2)}) collective-permute-start(bf16[640,512]{1,0:T(8,128)(2,1)} %get-tuple-element.163), channel_id=1, source_target_pairs={{0,16},{1,17},{2,18},{3,19},{4,20},{5,21},{6,22},{7,23},{8,24},{9,... | collective-permute-start | bytes 1966088 | tf_op jit(solution)/shard_map/ppermute | solution.py:779
  352.6 107.4 %collective-permute-start.28 = (bf16[1024,1024]{1,0:T(8,128)(2,1)}, bf16[1024,1024]{1,0:T(8,128)(2,1)}, u32[]{:S(2)}, u32[]{:S(2)}) collective-permute-start(bf16[1024,1024]{1,0:T(8,128)(2,1)} %shard_map.242), channel_id=1, source_target_pairs={{0,1},{1,0},{2,3},{3,2},{4,5},{5,4},{6,7},{7,6},{8,9},{9,8},{10,11... | collective-permute-start | bytes 6291464 | tf_op jit(solution)/shard_map/ppermute | solution.py:779
  404.1 46.8 %collective-permute-start.61 = (bf16[1280,512]{1,0:T(8,128)(2,1)}, bf16[1280,512]{1,0:T(8,128)(2,1)}, u32[]{:S(2)}, u32[]{:S(2)}) collective-permute-start(bf16[1280,512]{1,0:T(8,128)(2,1)} %add_convert_fusion.3), channel_id=1, source_target_pairs={{0,16},{1,17},{2,18},{3,19},{4,20},{5,21},{6,22},{7,23},{8,24},{9,... | collective-permute-start | bytes 3932168 | tf_op jit(solution)/shard_map/ppermute | solution.py:779
  404.1 48.2 %collective-permute-start.59 = (bf16[1280,512]{1,0:T(8,128)(2,1)}, bf16[1280,512]{1,0:T(8,128)(2,1)}, u32[]{:S(2)}, u32[]{:S(2)}) collective-permute-start(bf16[1280,512]{1,0:T(8,128)(2,1)} %add_convert_fusion.5), channel_id=1, source_target_pairs={{0,8},{1,9},{2,10},{3,11},{4,12},{5,13},{6,14},{7,15},{8,0},{9,1},... | collective-permute-start | bytes 3932168 | tf_op jit(solution)/shard_map/ppermute | solution.py:779
  420.3 61.2 %collective-permute-start.31 = (bf16[1024,1024]{1,0:T(8,128)(2,1)}, bf16[1024,1024]{1,0:T(8,128)(2,1)S(1)}, u32[]{:S(2)}, u32[]{:S(2)}) collective-permute-start(bf16[1024,1024]{1,0:T(8,128)(2,1)} %get-tuple-element.120.p0_ref), channel_id=1, source_target_pairs={{0,1},{1,0},{2,3},{3,2},{4,5},{5,4},{6,7},{7,6},{8,9},{9,8},{10,11... | collective-permute-start | bytes 6291464 | tf_op jit(solution)/shard_map/ppermute | solution.py:779
  455.7 95.4 %collective-permute-start.62 = (bf16[1280,512]{1,0:T(8,128)(2,1)}, bf16[1280,512]{1,0:T(8,128)(2,1)}, u32[]{:S(2)}, u32[]{:S(2)}) collective-permute-start(bf16[1280,512]{1,0:T(8,128)(2,1)} %add_convert_fusion.2), channel_id=1, source_target_pairs={{0,2},{1,3},{6,4},{7,5},{8,10},{9,11},{14,12},{15,13},{16,18},{17,... | collective-permute-start | bytes 3932168 | tf_op jit(solution)/shard_map/ppermute | solution.py:779
  464.1 164.5 %collective-permute-start.79 = (bf16[1024,512]{1,0:T(8,128)(2,1)}, bf16[1024,512]{1,0:T(8,128)(2,1)}, u32[]{:S(2)}, u32[]{:S(2)}) collective-permute-start(bf16[1024,512]{1,0:T(8,128)(2,1)} %add_convert_fusion.13), channel_id=1, source_target_pairs={{2,4},{3,5},{4,2},{5,3},{10,12},{11,13},{12,10},{13,11},{18,20},{1... | collective-permute-start | bytes 3145736 | tf_op jit(solution)/shard_map/ppermute | solution.py:779
  480.0 148.8 %collective-permute-start.46 = (bf16[784,512]{1,0:T(8,128)(2,1)}, bf16[784,512]{1,0:T(8,128)(2,1)}, u32[]{:S(2)}, u32[]{:S(2)}) collective-permute-start(bf16[784,512]{1,0:T(8,128)(2,1)} %add_convert_fusion.26), channel_id=1, source_target_pairs={{2,4},{3,5},{4,2},{5,3},{10,12},{11,13},{12,10},{13,11},{18,20},{1... | collective-permute-start | bytes 2408456 | tf_op jit(solution)/shard_map/ppermute | solution.py:779
  560.9 62.5 %collective-permute-start.50 = (bf16[640,512]{1,0:T(8,128)(2,1)}, bf16[640,512]{1,0:T(8,128)(2,1)}, u32[]{:S(2)}, u32[]{:S(2)}) collective-permute-start(bf16[640,512]{1,0:T(8,128)(2,1)} %get-tuple-element.158), channel_id=1, source_target_pairs={{0,16},{1,17},{2,18},{3,19},{4,20},{5,21},{6,22},{7,23},{8,24},{9,... | collective-permute-start | bytes 1966088 | tf_op jit(solution)/shard_map/ppermute | solution.py:779
  562.9 96.3 %collective-permute-start.69 = (bf16[1024,512]{1,0:T(8,128)(2,1)}, bf16[1024,512]{1,0:T(8,128)(2,1)}, u32[]{:S(2)}, u32[]{:S(2)}) collective-permute-start(bf16[1024,512]{1,0:T(8,128)(2,1)} %add_convert_fusion.21), channel_id=1, source_target_pairs={{0,16},{1,17},{2,18},{3,19},{4,20},{5,21},{6,22},{7,23},{8,24},{9,... | collective-permute-start | bytes 3145736 | tf_op jit(solution)/shard_map/ppermute | solution.py:779
  595.7 64.9 %collective-permute-start.67 = (bf16[1024,512]{1,0:T(8,128)(2,1)}, bf16[1024,512]{1,0:T(8,128)(2,1)}, u32[]{:S(2)}, u32[]{:S(2)}) collective-permute-start(bf16[1024,512]{1,0:T(8,128)(2,1)} %add_convert_fusion.23), channel_id=1, source_target_pairs={{0,8},{1,9},{2,10},{3,11},{4,12},{5,13},{6,14},{7,15},{8,0},{9,1},... | collective-permute-start | bytes 3145736 | tf_op jit(solution)/shard_map/ppermute | solution.py:779
  663.9 46.7 %collective-permute-start.35 = (bf16[784,512]{1,0:T(8,128)(2,1)S(1)}, bf16[784,512]{1,0:T(8,128)(2,1)S(1)}, u32[]{:S(2)}, u32[]{:S(2)}) collective-permute-start(bf16[784,512]{1,0:T(8,128)(2,1)S(1)} %add_convert_fusion.36), channel_id=1, source_target_pairs={{0,8},{1,9},{2,10},{3,11},{4,12},{5,13},{6,14},{7,15},{8,0},{9,1},... | collective-permute-start | bytes 2408456 | tf_op jit(solution)/shard_map/ppermute | solution.py:779
  664.2 47.7 %collective-permute-start.37 = (bf16[784,512]{1,0:T(8,128)(2,1)S(1)}, bf16[784,512]{1,0:T(8,128)(2,1)S(1)}, u32[]{:S(2)}, u32[]{:S(2)}) collective-permute-start(bf16[784,512]{1,0:T(8,128)(2,1)S(1)} %add_convert_fusion.34), channel_id=1, source_target_pairs={{0,16},{1,17},{2,18},{3,19},{4,20},{5,21},{6,22},{7,23},{8,24},{9,... | collective-permute-start | bytes 2408456 | tf_op jit(solution)/shard_map/ppermute | solution.py:779
  699.0 67.6 %collective-permute-start.33 = (bf16[1024,1024]{1,0:T(8,128)(2,1)S(1)}, bf16[1024,1024]{1,0:T(8,128)(2,1)S(1)}, u32[]{:S(2)}, u32[]{:S(2)}) collective-permute-start(bf16[1024,1024]{1,0:T(8,128)(2,1)S(1)} %copy-done.6), channel_id=1, source_target_pairs={{0,1},{1,0},{2,3},{3,2},{4,5},{5,4},{6,7},{7,6},{8,9},{9,8},{10,11... | collective-permute-start | bytes 6291464 | tf_op jit(solution)/shard_map/ppermute | solution.py:779
  756.6 69.7 %collective-permute-start.40 = (bf16[784,512]{1,0:T(8,128)(2,1)S(1)}, bf16[784,512]{1,0:T(8,128)(2,1)}, u32[]{:S(2)}, u32[]{:S(2)}) collective-permute-start(bf16[784,512]{1,0:T(8,128)(2,1)S(1)} %add_convert_fusion.31), channel_id=1, source_target_pairs={{2,0},{3,1},{4,6},{5,7},{10,8},{11,9},{12,14},{13,15},{18,16},{19,... | collective-permute-start | bytes 2408456 | tf_op jit(solution)/shard_map/ppermute | solution.py:779
  758.3 90.4 %collective-permute-start.72 = (bf16[1024,512]{1,0:T(8,128)(2,1)S(1)}, bf16[1024,512]{1,0:T(8,128)(2,1)S(1)}, u32[]{:S(2)}, u32[]{:S(2)}) collective-permute-start(bf16[1024,512]{1,0:T(8,128)(2,1)S(1)} %add_convert_fusion.18), channel_id=1, source_target_pairs={{2,0},{3,1},{4,6},{5,7},{10,8},{11,9},{12,14},{13,15},{18,16},{19,... | collective-permute-start | bytes 3145736 | tf_op jit(solution)/shard_map/ppermute | solution.py:779
  759.6 117.2 %collective-permute-start.56 = (bf16[1280,512]{1,0:T(8,128)(2,1)S(1)}, bf16[1280,512]{1,0:T(8,128)(2,1)S(1)}, u32[]{:S(2)}, u32[]{:S(2)}) collective-permute-start(bf16[1280,512]{1,0:T(8,128)(2,1)S(1)} %add_convert_fusion.6), channel_id=1, source_target_pairs={{2,0},{3,1},{4,6},{5,7},{10,8},{11,9},{12,14},{13,15},{18,16},{19,... | collective-permute-start | bytes 3932168 | tf_op jit(solution)/shard_map/ppermute | solution.py:779
  827.6 50.0 %collective-permute-start.48 = (bf16[784,512]{1,0:T(8,128)(2,1)S(1)}, bf16[784,512]{1,0:T(8,128)(2,1)S(1)}, u32[]{:S(2)}, u32[]{:S(2)}) collective-permute-start(bf16[784,512]{1,0:T(8,128)(2,1)S(1)} %broadcast_select_fusion.9.a_ref), channel_id=1, source_target_pairs={{0,1},{1,0},{2,3},{3,2},{4,5},{5,4},{6,7},{7,6},{8,9},{9,8},{10,11... | collective-permute-start | bytes 2408456 | tf_op jit(solution)/shard_map/ppermute | solution.py:779
  (156 other events, 2932.4 us)

commit v2 on v1

--- a/solution.py
+++ b/solution.py
@@ -51,7 +51,7 @@
         out_shape=[o for o, _ in outputs],
         input_output_aliases=aliases,
         compiler_params=pltpu.CompilerParams(vmem_limit_bytes=VMEM_BYTES),
-        cost_estimate=pl.CostEstimate(flops=int(flops), bytes_accessed=int(bytes_), transcendentals=0),
+        cost_estimate=pl.CostEstimate(flops=1, bytes_accessed=1, transcendentals=0),
     )(scalars, *[a for a, _ in inputs])
 
 
@@ -73,6 +73,35 @@
         else:
             ranges.append((r, 0, group.rows))
     return ranges
+
+
+def hop_bits(shards, half):
+    bits = [1 << b for b in range(shards.bit_length() - 1)]
+    return bits if half == 0 else bits[::-1]
+
+
+def last_bit(shards, relative, half):
+    return [b for b in hop_bits(shards, half) if relative & b][-1]
+
+
+def sum_rounds(shards):
+    keys = [(r, h) for r in range(1, shards) for h in range(2)]
+    goes = {(r, h): (r ^ last_bit(shards, r, h), h) for r, h in keys}
+    depth = {}
+    for key in sorted(keys, key=lambda k: -bin(k[0]).count("1")):
+        before = [depth[k] for k, to in goes.items() if to == key]
+        depth[key] = 1 + max(before) if before else 0
+    rounds = {}
+    for key in sorted(keys, key=lambda k: (depth[k], -bin(k[0]).count("1"), k)):
+        rounds.setdefault((depth[key], last_bit(shards, *key)), []).append(key)
+    return rounds, goes
+
+
+def store_rows(refs, halves, start, value):
+    for (lo, hi), ref in zip(halves, refs):
+        first, last = max(lo, start), min(hi, start + value.shape[0])
+        if first < last:
+            ref[first - lo : last - lo, :] = value[first - start : last - start]
 
 
 def assembly(group, shards):
@@ -111,7 +140,7 @@
     return parts
 
 
-def forward_qkv(own, prev, adds, bias, gain, shift, qkv_b, tables, pieces, group, shards, block=256):
+def forward_qkv(own, layer, prev, adds, biases, gain, shift, qkv_b, tables, pieces, group, shards, block=256):
     rows, width = prev.shape
     count = len(pieces)
     n_add = len(adds)
@@ -121,7 +150,9 @@
     def kernel(own_ref, *refs):
         prev_ref, *rest = refs
         add_refs, rest = rest[:n_add], rest[n_add:]
-        bias_ref, gain_ref, shift_ref, qkvb_ref, c_ref, s1_ref, s2_ref, *rest = rest
+        bias_refs, rest = rest[: len(biases)], rest[len(biases) :]
+        gain_ref, shift_ref, qkvb_ref, c_ref, s1_ref, s2_ref, *rest = rest
+        now = slice(layer, layer + 1)
         piece_refs, rest = rest[:count], rest[count:]
         stream_ref, unit_ref, inv_ref, normed_ref, q_ref, kv_ref, w_ref, sems = rest
 
@@ -134,7 +165,8 @@
         if n_add:
             for a in add_refs:
                 x = x + a[...].astype(f32)
-            x = x + bias_ref[...]
+            for b in bias_refs:
+                x = x + b[layer - 1 : layer, :]
         stream_ref[...] = x
         mean = jnp.mean(x, axis=1, keepdims=True)
         centered = x - mean
@@ -142,7 +174,7 @@
         unit = centered * inv
         unit_ref[...] = unit.astype(bf16)
         inv_ref[...] = jnp.broadcast_to(inv, inv_ref.shape)
-        normed = (unit * gain_ref[...] + shift_ref[...]).astype(bf16)
+        normed = (unit * gain_ref[now, :] + shift_ref[now, :]).astype(bf16)
         normed_ref[...] = normed
 
         @pl.when(pl.program_id(0) == 0)
@@ -151,20 +183,20 @@
                 c.wait()
 
         c, s1, s2 = c_ref[...], s1_ref[...], s2_ref[...]
-        q = nn(normed, w_ref[0]) + qkvb_ref[:, :half]
+        q = nn(normed, w_ref[0]) + qkvb_ref[now, :half]
         for j, part in enumerate(spin(q, c, s1, s2)):
             q_ref[:, j * 128 : (j + 1) * 128] = (part * HEAD ** (-0.5)).astype(bf16)
-        k = nn(normed, w_ref[1]) + qkvb_ref[:, half : 2 * half]
+        k = nn(normed, w_ref[1]) + qkvb_ref[now, half : 2 * half]
         for j, part in enumerate(spin(k, c, s1, s2)):
             kv_ref[:, j * 128 : (j + 1) * 128] = part.astype(bf16)
-        v = nn(normed, w_ref[2]) + qkvb_ref[:, 2 * half :]
+        v = nn(normed, w_ref[2]) + qkvb_ref[now, 2 * half :]
         kv_ref[:, half:] = v.astype(bf16)
 
     wide = row_blocks(block, width)
     inputs = (
         [(prev, wide)]
         + [(a, wide) for a in adds]
-        + [(v, whole(v.shape)) for v in (bias, gain, shift, qkv_b)]
+        + [(v, whole(v.shape)) for v in (*biases, gain, shift, qkv_b)]
         + [(t, row_blocks(block, 128)) for t in tables]
         + [(p, ANY) for p in pieces]
     )
@@ -196,7 +228,7 @@
     return x * big, big + x * e * (1.0 / math.sqrt(2.0 * math.pi))
 
 
-def forward_up(own, normed, up_b, pieces, group, shards, block=256):
+def forward_up(own, layer, normed, up_b, pieces, group, shards, block=256):
     rows, width = normed.shape
     count = len(pieces)
     plan = assembly(group, shards)
@@ -216,7 +248,7 @@
 
         for j in range(chunks):
             at = slice(j * COLS, (j + 1) * COLS)
-            pre = nn(x_ref[...], w_ref[j]) + b_ref[:, at]
+            pre = nn(x_ref[...], w_ref[j]) + b_ref[layer : layer + 1, at]
             act, slope = gelu_parts(pre)
             act_ref[:, at] = act.astype(bf16)
             slope_ref[:, at] = slope.astype(bf16)
@@ -568,11 +600,11 @@
     )
 
 
-def norm_backward(own, grad, parts, unit, inv, gain, block=256):
+def norm_backward(own, layer, grad, parts, unit, inv, gain, block=256):
     rows, width = unit.shape
 
     def kernel(own_ref, g_ref, p0_ref, p1_ref, unit_ref, inv_ref, gain_ref, new_ref, low_ref):
-        u = (p0_ref[...].astype(f32) + p1_ref[...].astype(f32)) * gain_ref[...]
+        u = (p0_ref[...].astype(f32) + p1_ref[...].astype(f32)) * gain_ref[layer : layer + 1, :]
         unit = unit_ref[...].astype(f32)
         new = g_ref[...].astype(f32) + inv_ref[:, :1] * (
             u - jnp.mean(u, axis=1, keepdims=True) - unit * jnp.mean(u * unit, axis=1, keepdims=True)
@@ -591,29 +623,38 @@
     )
 
 
-def weight_grads(own, lefts, rights, extra, group, first_half, shards):
+def weight_grads(own, lefts, rights, extra, group, shards):
     rows = rights.shape[0]
     blocks = rights.shape[1] // COLS
     ks = [l.shape[1] // shards for l in lefts]
     height = sum(ks)
     n_left = len(lefts)
     extra_rows = 0 if extra is None else extra.shape[0] // shards
-    total = height * blocks + extra_rows
-    ranges = piece_ranges(Group([(total, "", 0)], first_half), shards)
+    rounds, _ = sum_rounds(shards)
+    size = [hi - lo for lo, hi in (group.cut(0), group.cut(1))]
+    parts = {}
+    shapes = [(group.rows, COLS)]
+    parts[0] = [(0, 0, 0, group.rows)]
+    for i, keys in enumerate(rounds.values()):
+        at = 0
+        for r, h in keys:
+            parts.setdefault(r, []).append((i + 1, at) + group.cut(h))
+            at += size[h]
+        shapes.append((at, COLS))
 
     def kernel(own_ref, *refs):
         left_refs, rest = refs[:n_left], refs[n_left:]
         right_ref, rest = rest[0], rest[1:]
         extra_ref, rest = (None, rest) if extra is None else (rest[0], rest[1:])
-        out_refs, flipped = rest[: len(ranges)], rest[len(ranges) :]
+        out_refs, flipped = rest[: len(shapes)], rest[len(shapes) :]
         for l, t in zip(left_refs, flipped):
             t[...] = jnp.transpose(l[...])
 
         def store(r, start, value):
-            for (rel, lo, hi), ref in zip(ranges, out_refs):
+            for i, at, lo, hi in parts[r]:
                 first, last = max(lo, start), min(hi, start + value.shape[0])
-                if rel == r and first < last:
-                    ref[first - lo : last - lo, :] = value[first - start : last - start]
+                if first < last:
+                    out_refs[i][at + first - lo : at + last - lo, :] = value[first - start : last - start]
 
         for r in range(shards):
             s = lax.bitwise_xor(own_ref[0], r)
@@ -630,12 +671,9 @@
     S = jax.ShapeDtypeStruct
     extras = [] if extra is None else [extra]
     inputs = [(a, whole(a.shape)) for a in (*lefts, rights, *extras)]
-    outputs = [(S((hi - lo, COLS), bf16), whole((hi - lo, COLS))) for _, lo, hi in ranges]
-    return call(
-        kernel, own, inputs, outputs, (1,),
+    return call(
+        kernel, own, inputs, [(S(s, bf16), whole(s)) for s in shapes], (1,),
         [pltpu.VMEM((l.shape[1], rows), bf16) for l in lefts],
-        flops=2 * rows * sum(l.shape[1] for l in lefts) * rights.shape[1],
-        bytes_=2 * (rows * rights.shape[1] + sum(l.size for l in lefts) + shards * total * COLS),
     )
 
 
@@ -643,92 +681,198 @@
     return jnp.where(core == 0, first, second)
 
 
-def pack_qkv(own, weight, layer, shards):
+def vector_places(widths):
+    places, row, column = {}, 0, 0
+    for name, (layers, width) in widths.items():
+        places[name] = []
+        for _ in range(layers):
+            parts, done = [], 0
+            while done < width:
+                take = min(COLS - column, width - done)
+                parts.append((row, column, take, done))
+                done += take
+                column += take
+                if column == COLS:
+                    row, column = row + 1, 0
+            places[name].append(parts)
+    return places
+
+
+def pack_qkv(own, weight, layer, group, shards, vectors=None):
     _, rows, columns = weight.shape
     w = columns // (6 * shards)
-
-    def kernel(own_ref, w_ref, out_ref):
+    halves = [(0, group.rows)]
+    names = [] if vectors is None else list(vectors)
+    places = vector_places({n: vectors[n].shape for n in names})
+
+    def kernel(own_ref, w_ref, *rest):
+        vec_refs, rest = rest[: len(names)], rest[len(names) :]
+        out_refs = rest[:1]
         core = own_ref[1]
+        if names:
+            tmp = rest[1]
+            tmp[...] = jnp.zeros_like(tmp)
+            for n, ref in zip(names, vec_refs):
+                for l, parts in enumerate(places[n]):
+                    for row, column, take, first in parts:
+                        tmp[row : row + 1, column : column + take] = ref[l : l + 1, first : first + take].astype(f32)
+            store_rows(out_refs, halves, 3 * rows, tmp[...].astype(bf16))
         for g in range(3):
+            parts = []
             for s in range(shards):
                 at = (g * shards + s) * 2 * w
-                out_ref[g * rows : (g + 1) * rows, s * w : (s + 1) * w] = pick(
-                    core, w_ref[0, :, at : at + w], w_ref[0, :, at + w : at + 2 * w]
+                parts.append(pick(core, w_ref[0, :, at : at + w], w_ref[0, :, at + w : at + 2 * w]))
+            store_rows(out_refs, halves, g * rows, jnp.concatenate(parts, axis=1))
+
+    return call(
+        kernel, own,
+        [(weight, pl.BlockSpec((1, rows, columns), lambda i, *_: (layer, 0, 0)))]
+        + [(vectors[n], whole(vectors[n].shape)) for n in names],
+        piece_output(group), (1,),
+        [pltpu.VMEM((16, COLS), f32)] if names else [], bytes_=rows * columns * 3,
+    )
+
+
+def whole_vectors(own, pieces, group, first, widths, shards, kinds):
+    ranges = piece_ranges(group, shards)
+    takes = [(a, r, first - lo) for a, (r, lo, hi) in enumerate(ranges) if lo <= first and first + 16 <= hi]
+    names = list(widths)
+    places = vector_places(widths)
+
+    def kernel(own_ref, *refs):
+        piece_refs, rest = refs[: len(takes)], refs[len(takes) :]
+        out_refs, (all_ref, sems) = rest[: len(names)], rest[len(names) :]
+        core = own_ref[1]
+        copies = []
+        for i, ((_, r, at), ref) in enumerate(zip(takes, piece_refs)):
+            copies.append(
+                pltpu.make_async_copy(
+                    ref.at[pl.ds(at, 16), :], all_ref.at[lax.bitwise_xor(own_ref[0], r)], sems.at[i]
                 )
-
-    shape = (3 * rows, COLS)
+            )
+        for c in copies:
+            c.start()
+        for c in copies:
+            c.wait()
+        rows = [all_ref[s].astype(f32) for s in range(shards)]
+
+        def piece_of(name, l, lo, hi):
+            width = widths[name][1]
+            s = lo // width
+            lo, hi = lo - s * width, hi - s * width
+            got = []
+            for row, column, take, start in places[name][l]:
+                a, b = max(lo, start), min(hi, start + take)
+                if a < b:
+                    got.append(rows[s][row : row + 1, column + a - start : column + b - start])
+            return got[0] if len(got) == 1 else jnp.concatenate(got, axis=1)
+
+        for name, ref in zip(names, out_refs):
+            layers, width = widths[name]
+            for l in range(layers):
+                if not kinds[name]:
+                    for s in range(shards):
+                        ref[l : l + 1, s * width : (s + 1) * width] = piece_of(name, l, s * width, (s + 1) * width)
+                    continue
+                blocks = kinds[name] * shards
+                w = width * shards // (2 * blocks)
+                for b in range(blocks):
+                    ref[l : l + 1, b * w : (b + 1) * w] = pick(
+                        core, piece_of(name, l, 2 * b * w, (2 * b + 1) * w),
+                        piece_of(name, l, (2 * b + 1) * w, (2 * b + 2) * w),
+                    )
+
+    outs = []
+    for n in names:
+        shape = (8, widths[n][1] * shards // (2 if kinds[n] else 1))
+        outs.append((jax.ShapeDtypeStruct(shape, f32), whole(shape)))
+    return call(
+        kernel, own, [(pieces[a], ANY) for a, _, _ in takes], outs, (1,),
+        [pltpu.VMEM((shards, 16, COLS), bf16), pltpu.SemaphoreType.DMA((len(takes),))], bytes_=shards * 16 * COLS * 2,
+    )
+
+
+def piece_output(group):
+    shape = (group.rows, COLS)
+    return [(jax.ShapeDtypeStruct(shape, bf16), whole(shape))]
+
+
+def pack_up(own, weight, layer, group, shards):
+    _, rows, columns = weight.shape
+    w = columns // (2 * shards)
+    halves = [(0, group.rows)]
+
+    def kernel(own_ref, w_ref, *out_refs):
+        core = own_ref[1]
+        for j in range(columns // 2 // COLS):
+            parts = []
+            for s in range(j * COLS // w, (j + 1) * COLS // w):
+                at = s * 2 * w
+                parts.append(pick(core, w_ref[0, :, at : at + w], w_ref[0, :, at + w : at + 2 * w]))
+            value = parts[0] if len(parts) == 1 else jnp.concatenate(parts, axis=1)
+            store_rows(out_refs, halves, j * rows, value)
+
     return call(
         kernel, own,
         [(weight, pl.BlockSpec((1, rows, columns), lambda i, *_: (layer, 0, 0)))],
-        [(jax.ShapeDtypeStruct(shape, bf16), whole(shape))], (1,), bytes_=rows * columns * 3,
-    )[0]
-
-
-def pack_up(own, weight, layer, shards):
-    _, rows, columns = weight.shape
-    w = columns // (2 * shards)
-    blocks = columns // 2 // COLS
-
-    def kernel(own_ref, w_ref, out_ref):
-        core = own_ref[1]
-        for s in range(shards):
-            j, off = s * w // COLS, s * w % COLS
-            at = s * 2 * w
-            out_ref[j * rows : (j + 1) * rows, off : off + w] = pick(
-                core, w_ref[0, :, at : at + w], w_ref[0, :, at + w : at + 2 * w]
-            )
-
-    shape = (blocks * rows, COLS)
-    return call(
-        kernel, own,
-        [(weight, pl.BlockSpec((1, rows, columns), lambda i, *_: (layer, 0, 0)))],
-        [(jax.ShapeDtypeStruct(shape, bf16), whole(shape))], (1,), bytes_=rows * columns * 3,
-    )[0]
-
-
-def pack_out(own, down, out, layer):
+        piece_output(group), (1,), bytes_=rows * columns * 3,
+    )
+
+
+def pack_out(own, down, out, layer, group):
+    halves = [(0, group.rows)]
     dr, orows = down.shape[1] // 2, out.shape[1] // 2
     width = down.shape[2]
     blocks = width // COLS
 
-    def kernel(own_ref, d_ref, o_ref, out_ref):
+    def kernel(own_ref, d_ref, o_ref, *out_refs):
         for j in range(blocks):
             at = slice(j * COLS, (j + 1) * COLS)
             base = j * (dr + orows)
-            out_ref[base : base + dr, :] = d_ref[0, :, at]
-            out_ref[base + dr : base + dr + orows, :] = o_ref[0, :, at]
-
-    shape = (blocks * (dr + orows), COLS)
+            store_rows(out_refs, halves, base, d_ref[0, :, at])
+            store_rows(out_refs, halves, base + dr, o_ref[0, :, at])
+
     spec = lambda r: pl.BlockSpec((1, r, width), lambda i, own_ref: (layer, own_ref[1], 0))
     return call(
         kernel, own, [(down, spec(dr)), (out, spec(orows))],
-        [(jax.ShapeDtypeStruct(shape, bf16), whole(shape))], (1,), bytes_=(dr + orows) * width * 4,
-    )[0]
+        piece_output(group), (1,), bytes_=(dr + orows) * width * 4,
+    )
+
+
+def read_rows(refs, lo, hi):
+    got, start = [], 0
+    for ref in refs:
+        first, last = max(lo, start), min(hi, start + ref.shape[0])
+        if first < last:
+            got.append(ref[first - start : last - start, :])
+        start += ref.shape[0]
+    return got[0] if len(got) == 1 else jnp.concatenate(got)
 
 
 def unpack_columns(own, mine, theirs, before, layer, layers, rows, kinds, w, shards):
     columns = kinds * shards * 2 * w
-    blocks = kinds * shards * w // COLS
-
-    def kernel(own_ref, a_ref, b_ref, *rest):
-        out_ref = rest[-1]
+
+    n = len(mine)
+
+    def kernel(own_ref, *refs):
+        a_refs, b_refs, out_ref = refs[:n], refs[n : 2 * n], refs[-1]
         core = own_ref[1]
-        for g in range(kinds):
-            for s in range(shards):
-                c = (g * shards + s) * w
-                j, off = c // COLS, c % COLS
-                a = a_ref[j * rows : (j + 1) * rows, off : off + w].astype(f32)
-                b = b_ref[j * rows : (j + 1) * rows, off : off + w].astype(f32)
+        for j in range(kinds * shards * w // COLS):
+            a_block = read_rows(a_refs, j * rows, (j + 1) * rows)
+            b_block = read_rows(b_refs, j * rows, (j + 1) * rows)
+            for c in range(j * COLS, (j + 1) * COLS, w):
+                off = c % COLS
+                a = a_block[:, off : off + w].astype(f32)
+                b = b_block[:, off : off + w].astype(f32)
                 out_ref[0, :, 2 * c : 2 * c + w] = pick(core, a, b)
                 out_ref[0, :, 2 * c + w : 2 * c + 2 * w] = pick(core, b, a)
 
     extra = [] if before is None else [(before, ANY)]
-    shape = (blocks * rows, COLS)
-    return call(
-        kernel, own, [(mine, whole(shape)), (theirs, whole(shape))] + extra,
+    return call(
+        kernel, own, [(v, whole(v.shape)) for v in (*mine, *theirs)] + extra,
         [(jax.ShapeDtypeStruct((layers, rows, columns), f32),
           pl.BlockSpec((1, rows, columns), lambda i, *_: (layer, 0, 0)))],
-        (1,), aliases={} if before is None else {3: 0}, bytes_=rows * columns * 6,
+        (1,), aliases={} if before is None else {1 + 2 * n: 0}, bytes_=rows * columns * 6,
     )[0]
 
 
@@ -736,25 +880,26 @@
     blocks = width // COLS
     total = sum(heights)
 
-    def kernel(own_ref, a_ref, b_ref, *rest):
-        out_refs = rest[-len(heights) :]
+    n = len(mine)
+
+    def kernel(own_ref, *refs):
+        a_refs, b_refs, out_refs = refs[:n], refs[n : 2 * n], refs[-len(heights) :]
         core = own_ref[1]
         for j in range(blocks):
             start = j * total
             for h, ref in zip(heights, out_refs):
-                a = a_ref[start : start + h, :].astype(f32)
-                b = b_ref[start : start + h, :].astype(f32)
+                a = read_rows(a_refs, start, start + h).astype(f32)
+                b = read_rows(b_refs, start, start + h).astype(f32)
                 ref[0, :h, j * COLS : (j + 1) * COLS] = pick(core, a, b)
                 ref[0, h:, j * COLS : (j + 1) * COLS] = pick(core, b, a)
                 start += h
 
     extra = [] if befores is None else [(b, ANY) for b in befores]
-    shape = (blocks * total, COLS)
-    return call(
-        kernel, own, [(mine, whole(shape)), (theirs, whole(shape))] + extra,
+    return call(
+        kernel, own, [(v, whole(v.shape)) for v in (*mine, *theirs)] + extra,
         [(jax.ShapeDtypeStruct((layers, 2 * h, width), f32),
           pl.BlockSpec((1, 2 * h, width), lambda i, *_: (layer, 0, 0))) for h in heights],
-        (1,), aliases={} if befores is None else {3 + i: i for i in range(len(heights))},
+        (1,), aliases={} if befores is None else {1 + 2 * n + i: i for i in range(len(heights))},
         bytes_=total * width * 12,
     )
 
@@ -790,58 +935,10 @@
     def last_chip(self, value):
         return self.send(value, lambda s, r: (s, r - 2) if r >= 2 else None)
 
-    def last_bit(self, relative, half):
-        order = self.bits if half == 0 else self.bits[::-1]
-        return [b for b in order if relative & b][-1]
-
-    def gather(self, own, group, after=None):
-        if after is not None:
-            own, _ = lax.optimization_barrier((own, after))
-        pieces = {0: own}
-        for bit in self.bits:
-            pieces[bit] = self.flip(own, bit)
-        near = [pieces[bit] for bit in self.bits]
-        got = []
-        for r, lo, hi in piece_ranges(group, self.shards):
-            if bin(r).count("1") <= 1:
-                got.append(pieces[r])
-                continue
-            half = 0 if lo == 0 else 1
-            bit = self.last_bit(r, half)
-            source = pieces[r ^ bit]
-            part = source[half] if isinstance(source, list) else source[lo:hi]
-            pieces.setdefault(r, []).append(self.flip(part, bit))
-            got.append(pieces[r][-1])
-        return got, near
-
-    def scatter_sum(self, arrays, group):
-        ranges = piece_ranges(group, self.shards)
-        acc = {}
-        for (r, lo, hi), a in zip(ranges, arrays):
-            acc.setdefault(r, []).append((lo, hi, a))
-        for r in sorted(range(1, self.shards), key=lambda r: (-bin(r).count("1"), r)):
-            for lo, hi, a in acc[r]:
-                half = 0 if lo == 0 else 1
-                bit = self.last_bit(r, half)
-                came = self.flip(a, bit)
-                target = acc[r ^ bit]
-                for i, (tlo, thi, t) in enumerate(target):
-                    first, last = max(lo, tlo), min(hi, thi)
-                    if first >= last:
-                        continue
-                    part = came[first - lo : last - lo]
-                    if (first, last) == (tlo, thi):
-                        new = t.astype(f32) + part.astype(f32)
-                    else:
-                        new = t.astype(f32) + jnp.pad(
-                            part.astype(f32), ((first - tlo, thi - last), (0, 0))
-                        )
-                    target[i] = (tlo, thi, new.astype(bf16))
-        return acc[0][0][2]
-
-    def sum_chips(self, value):
+    def chip_steps(self):
         chips = self.chips
         line = 4 if chips % 4 == 0 else 1
+        steps = []
         if line == 4:
             at = self.chip % 4
 
@@ -857,21 +954,148 @@
                 z = (r // 2) % 4
                 return (s, r - 2) if z == 1 else (s, r + 2) if z == 2 else None
 
-            value = (value.astype(f32) + self.send(value, inward).astype(f32)).astype(bf16)
-            value = (value.astype(f32) + self.send(value, across).astype(f32)).astype(bf16)
-            back = self.send(value, outward)
-            value = jnp.where((at == 0) | (at == 3), back, value)
+            steps += [(inward, None), (across, None), (outward, (at == 0) | (at == 3))]
         step = line
         while step < chips:
-            came = self.send(value, lambda s, r, step=step: (s, r ^ (2 * step)))
-            value = (value.astype(f32) + came.astype(f32)).astype(bf16)
+            steps.append((lambda s, r, step=step: (s, r ^ (2 * step)), None))
             step *= 2
-        return value
-
-
-def core_columns(core, rows, kinds, shards):
-    cut = rows.reshape(rows.shape[0], kinds * shards, 2, -1)
-    return pick(core, cut[:, :, 0], cut[:, :, 1]).reshape(rows.shape[0], -1)
+        return steps
+
+
+class Clock:
+    def __init__(self):
+        self.last = None
+
+    def tie(self, value):
+        if self.last is None:
+            return value
+        return lax.optimization_barrier((value, self.last))[0]
+
+    def mark(self, value):
+        self.last = value
+
+
+class Gather:
+    def __init__(self, net, group, own):
+        self.net, self.group, self.own = net, group, own[0]
+
+    def near(self, clock):
+        own = clock.tie(self.own)
+        clock.mark(own)
+        self.pieces = {0: [own]}
+        for bit in self.net.bits:
+            self.pieces[bit] = [self.net.flip(own, bit)]
+
+    def far(self, clock):
+        net, bits = self.net, self.net.bits
+        for bit, came in zip(bits, clock.tie(tuple(self.pieces[bit][0] for bit in bits))):
+            self.pieces[bit] = [came]
+        got, parts = [], []
+        for r, lo, hi in piece_ranges(self.group, net.shards):
+            if bin(r).count("1") <= 1:
+                got.append(self.pieces[r][0])
+                continue
+            half = 0 if lo == 0 else 1
+            bit = last_bit(net.shards, r, half)
+            source = self.pieces[r ^ bit]
+            part = source[half] if len(source) == 2 else source[0][lo:hi]
+            parts.append(part)
+            self.pieces.setdefault(r, []).append(net.flip(part, bit))
+            got.append(self.pieces[r][-1])
+        clock.mark(tuple(parts))
+        self.arrays = got
+
+    def arrived(self, clock):
+        self.arrays = list(clock.tie(tuple(self.arrays)))
+        clock.mark(tuple(self.arrays[-2:]))
+
+
+def sum_low(values):
+    total = values[0].astype(f32)
+    for v in values[1:]:
+        total = total + v.astype(f32)
+    return total.astype(bf16)
+
+
+class Reduce:
+    def __init__(self, net, clock, group, arrays, apart):
+        self.at = None
+        self.steps = self.run(net, clock, group, arrays, apart)
+
+    def step(self, name):
+        while self.at != name:
+            self.at = next(self.steps)
+
+    def run(self, net, clock, group, arrays, apart):
+        rounds, goes = sum_rounds(net.shards)
+        last = max(d for d, _ in rounds)
+        cuts = [group.cut(h) for h in range(2)]
+        size = [hi - lo for lo, hi in cuts]
+        own = arrays[0]
+        held = dict(zip(rounds, arrays[1:]))
+        came = {}
+        for now in range(last + 1):
+            sent = {}
+            for (d, bit), keys in rounds.items():
+                if d != now:
+                    continue
+                value = held[d, bit]
+                if any(k in came for k in keys):
+                    parts, at = [], 0
+                    for r, h in keys:
+                        mine = value if len(keys) == 1 else value[at : at + size[h]]
+                        parts.append(sum_low([mine] + came.get((r, h), [])))
+                        at += size[h]
+                    value = parts[0] if len(parts) == 1 else jnp.concatenate(parts)
+                    clock.mark(value)
+                sent[d, bit] = net.flip(value, bit)
+            yield "r0" if now == 0 else "r1" if now == last else None
+            sent = clock.tie(sent)
+            for key, value in sent.items():
+                at = 0
+                for r, h in rounds[key]:
+                    part = value if len(rounds[key]) == 1 else value[at : at + size[h]]
+                    came.setdefault(goes[r, h], []).append(part)
+                    at += size[h]
+        halves = [sum_low([own[lo:hi]] + came[0, h]) for h, (lo, hi) in enumerate(cuts)]
+        self.chains = {}
+        for name, value in zip("ab", halves) if apart else [("", jnp.concatenate(halves))]:
+            clock.mark(value)
+            self.chains[name] = ChipSum(net, clock, value)
+        yield "r2"
+
+
+class ChipSum:
+    def __init__(self, net, clock, value):
+        self.steps = self.run(net, clock, value)
+        self.at = next(self.steps)
+
+    def step(self, name):
+        while self.at != name:
+            self.at = next(self.steps)
+
+    def run(self, net, clock, value):
+        for i, (where, replaced) in enumerate(net.chip_steps()):
+            came = net.send(value, where)
+            yield f"r{2 + i}" if i < 3 else None
+            came = clock.tie(came)
+            value = sum_low([value, came]) if replaced is None else jnp.where(replaced, came, value)
+            clock.mark(value)
+        theirs = net.other_core(value)
+        yield "r5"
+        self.mine, self.theirs = value, clock.tie(theirs)
+        clock.mark(self.theirs)
+        yield "r6"
+
+
+ORDER = """
+g0a0 docs g1a0 g2a0 g0u0 f10 g1u0 h0 g2u0 g0o0 f20 f30 g1o0 g2o0 g0a1 f40 g1a1 g2a1
+g0u1 f11 g1u1 h1 g2u1 g0o1 f21 f31 g1o1 wo1 f41 g2o1 r0o1 bb1 ab1 p1 r1o1 out
+wu1 r0u1 r2o1 bn1 wa1 r1u1 nb1 r0a1 r3o1 r2u1 wo0 r1a1 bb0 r3u1 r4o1 r2a1 r0o0 ab0
+r4u1 r3a1 r5o1 r1o0 r6o1 p0 wu0 r5u1 r2o0 r6u1 r0u0 r4a1 bn0 r1u0 r3o0 nb0 r2u0 wa0
+r0a0 r4o0 r3u0 r1a0 r5a1 r2a0 r4u0 r3a0a r3a0b r4a0a r5o0 r6a1 r4a0b r5a0a r5u0 r6o0 r5a0b r6u0
+r6a0
+""".split()
 
 
 def body(
@@ -902,40 +1126,35 @@
     group_first = net.shard * row_count * net.reps
     chip_first = net.chip * rows
     own = jnp.stack([net.shard, core]).astype(jnp.int32)
+    clock = Clock()
 
     ff_piece, head_piece = ff // shards, width // 2 // shards
-    group_a = Group([(piece, "a", j) for j in range(3)], 3 * piece // 2)
+    a_blocks = [(piece, "a", j) for j in range(3)]
+    group_a0 = Group(a_blocks, 3 * piece // 2, 16)
+    group_a = Group(a_blocks, 3 * piece // 2)
     group_u = Group([(piece, "u", j) for j in range(ff // COLS)], piece * (ff // COLS) // 2)
     group_o = Group(
         [b for j in range(2) for b in ((ff_piece, "d", j), (head_piece, "o", j))], ff_piece + head_piece
     )
     grads_a = Group([(3 * piece + 16, "", 0)], 3 * piece // 2)
 
-    after = None
-    gathered = []
+    def pair_rows(x):
+        other = net.other_core(x)
+        return jnp.concatenate([pick(core, x, other), pick(core, other, x)])
+
+    def own_rows(x):
+        return lax.dynamic_slice_in_dim(x, core * row_count, row_count)
+
+    small = {
+        "gain": norm_gain, "shift": norm_shift, "qkv": qkv_bias, "out": out_bias, "up": up_bias, "down": down_bias
+    }
+    gathers = []
     for l in range(layers):
-        layer = []
-        for group, packed in (
-            (group_a, lambda: pack_qkv(own, qkv_weight, l, shards)),
-            (group_u, lambda: pack_up(own, up_weight, l, shards)),
-            (group_o, lambda: pack_out(own, down_weight, out_weight, l)),
-        ):
-            got, after = net.gather(packed(), group, after)
-            layer.append(got)
-        gathered.append(layer)
-
-    names = (norm_gain, norm_shift, qkv_bias, out_bias, up_bias, down_bias)
-    small = lax.all_gather(jnp.concatenate([v.reshape(-1) for v in names]), "shard", axis=0)
-    vectors, offset = [], 0
-    for v in names:
-        part = small[:, offset : offset + v.size].reshape((shards,) + v.shape)
-        vectors.append(jnp.moveaxis(part, 0, 1).reshape(layers, -1).astype(f32))
-        offset += v.size
-    gains, shifts, qkv_b, out_b, up_b, down_b = vectors
-    qkv_b = core_columns(core, qkv_b, 3, shards)
-    up_b = core_columns(core, up_b, 1, shards)
-    branch_b = out_b + down_b
-
+        gathers += [
+            Gather(net, group_a0 if l == 0 else group_a, pack_qkv(own, qkv_weight, l, group_a if l else group_a0, shards, None if l else small)),
+            Gather(net, group_u, pack_up(own, up_weight, l, group_u, shards)),
+            Gather(net, group_o, pack_out(own, down_weight, out_weight, l, group_o)),
+        ]
     slots = lengths.shape[0]
     before = jnp.arange(slots)[None, :] < jnp.arange(slots)[:, None]
     dealt_start = jnp.sum(jnp.where(before, lengths[None, :], 0), axis=1)
@@ -962,98 +1181,180 @@
         jnp.where((lane >= ROT // 2) & (lane < ROT), sine, 0.0),
     )
 
-    def pair_rows(x):
-        other = net.other_core(x)
-        return jnp.concatenate([pick(core, x, other), pick(core, other, x)])
-
-    def own_rows(x):
-        return lax.dynamic_slice_in_dim(x, core * row_count, row_count)
-
-    stream, adds = pair_rows(tokens), []
-    saved = []
-    bias = jnp.zeros((1, width), f32)
-    for l in range(layers):
-        a_pieces, u_pieces, o_pieces = gathered[l]
+    stream0 = pair_rows(tokens)
+    branch_top = pair_rows(cotangent)
+    top = layers - 1
+    at = [dict() for _ in range(layers)]
+    sums = {}
+    common = {}
+
+    def forward_first(l):
+        a = gathers[3 * l]
+        if l == 0:
+            common["vectors"] = whole_vectors(
+                own, a.arrays, group_a0, 3 * piece, {n: v.shape for n, v in small.items()}, shards,
+                {"gain": 0, "shift": 0, "qkv": 3, "out": 0, "up": 1, "down": 0},
+            )
+            before, adds, biases = stream0, [], []
+        else:
+            before, adds = at[l - 1]["stream"], at[l - 1]["adds"]
+            biases = [common["vectors"][3], common["vectors"][5]]
+        gains, shifts, qkv_b, _, _, _ = common["vectors"]
         stream, unit, inv, normed, q, kv = forward_qkv(
-            own, stream, adds, bias, gains[l : l + 1], shifts[l : l + 1], qkv_b[l : l + 1], tables,
-            a_pieces, group_a, shards,
+            own, l, clock.tie(before), adds, biases, gains, shifts, qkv_b, tables, a.arrays, a.group, shards
         )
-        halo = net.next_chip(kv[rows - reach :])
-        activated, slope = forward_up(own, normed, up_b[l : l + 1], u_pieces, group_u, shards)
-        attended, lse = attend(meta, q, kv, halo, start_column)
-        partial = forward_out(own, attended, activated, o_pieces, group_o, shards)
-        adds = [partial, net.other_core(partial)]
-        bias = branch_b[l : l + 1]
-        saved.append((unit, inv, normed, q, kv, halo, activated, slope, attended, lse))
-    block_output = (
-        own_rows(stream) + own_rows(adds[0]).astype(f32) + own_rows(adds[1]).astype(f32) + bias
-    ).astype(bf16)
-
-    branch = pair_rows(cotangent)
-    grad = branch
-    reduced = [None] * layers
-    for l in reversed(range(layers)):
-        a_pieces, u_pieces, o_pieces = gathered[l]
-        unit, inv, normed, q, kv, halo, activated, slope, attended, lse = saved[l]
-        o_sum = net.scatter_sum(
-            weight_grads(own, [activated, attended], branch, None, None, group_o.first_half, shards), group_o
+        clock.mark(q)
+        at[l].update(stream=stream, unit=unit, inv=inv, normed=normed, q=q, kv=kv)
+
+    def send_halo(l):
+        part = clock.tie(at[l]["kv"])[rows - reach :]
+        clock.mark(part)
+        at[l]["halo"] = net.next_chip(part)
+
+    def forward_second(l):
+        at[l]["activated"], at[l]["slope"] = forward_up(
+            own, l, clock.tie(at[l]["normed"]), common["vectors"][4], gathers[3 * l + 1].arrays, group_u, shards
         )
-        pre_grad, attended_grad, up_sum, branch_sum = backward_branch(
-            own, branch, slope, o_pieces, group_o, shards
+        clock.mark(at[l]["slope"])
+
+    def forward_third(l):
+        at[l]["attended"], at[l]["lse"] = attend(
+            meta, clock.tie(at[l]["q"]), at[l]["kv"], at[l]["halo"], start_column
         )
-        dq, dkv = attend_back(meta, q, kv, halo, start_row, attended_grad, attended, lse, tables)
-        halo_grad = net.last_chip(dkv[:reach])
-        u_sum = net.scatter_sum(
-            weight_grads(own, [normed], pre_grad, None, None, group_u.first_half, shards), group_u
+        clock.mark(at[l]["lse"])
+
+    def forward_fourth(l):
+        partial = forward_out(
+            own, clock.tie(at[l]["attended"]), at[l]["activated"], gathers[3 * l + 2].arrays, group_o, shards
         )
-        packed_grad, part, qkv_sum, gain_sum, shift_sum = backward_normed(
-            own, dq, dkv, halo_grad, pre_grad, unit, tables, a_pieces, u_pieces, group_a, group_u, shards
-        )
-        came = net.other_core(part)
+        clock.mark(partial)
+        at[l]["adds"] = [partial, net.other_core(partial)]
+
+    def branch_of(l):
+        return branch_top if l == top else at[l + 1]["branch"]
+
+    def output():
+        adds = at[top]["adds"]
+        value = own_rows(clock.tie(at[top]["stream"])) + own_rows(adds[0]).astype(f32) + own_rows(adds[1]).astype(f32)
+        out_b, down_b = common["vectors"][3], common["vectors"][5]
+        common["output"] = (value + out_b[top : top + 1] + down_b[top : top + 1]).astype(bf16)
+        clock.mark(common["output"])
+
+    def reduce(name, l, group, lefts, rights, extra=None):
+        got = weight_grads(own, [clock.tie(lefts[0])] + lefts[1:], rights, extra, group, shards)
+        clock.mark(got[0])
+        sums[name, l] = Reduce(net, clock, group, got, name == "a" and l == 0)
+
+    def grads_out(l):
+        reduce("o", l, group_o, [at[l]["activated"], at[l]["attended"]], branch_of(l))
+
+    def grads_up(l):
+        reduce("u", l, group_u, [at[l]["normed"]], at[l]["pre_grad"])
+
+    def grads_qkv(l):
+        qkv_sum = at[l]["qkv_sum"].reshape(3 * shards, 1, -1)
+        nothing = jnp.zeros_like(qkv_sum)
+        qkv_sum = jnp.concatenate([pick(core, qkv_sum, nothing), pick(core, nothing, qkv_sum)], axis=1)
 
         def line(v, width):
             v = v.reshape(shards, -1)
             return jnp.pad(v, ((0, 0), (0, width - v.shape[1])))
 
-        qkv_sum = qkv_sum.reshape(3 * shards, 1, -1)
-        nothing = jnp.zeros_like(qkv_sum)
-        qkv_sum = jnp.concatenate(
-            [pick(core, qkv_sum, nothing), pick(core, nothing, qkv_sum)], axis=1
-        )
         extra = jnp.concatenate(
             [
-                line(gain_sum, COLS // 2),
-                line(shift_sum, COLS // 2),
-                line(branch_sum, COLS),
-                line(up_sum, COLS),
+                line(at[l]["gain_sum"], COLS // 2),
+                line(at[l]["shift_sum"], COLS // 2),
+                line(at[l]["branch_sum"], COLS),
+                line(at[l]["up_sum"], COLS),
                 line(qkv_sum, 13 * COLS),
             ],
             axis=1,
         ).reshape(shards * 16, COLS)
-        a_sum = net.scatter_sum(
-            weight_grads(own, [normed], packed_grad, extra, None, group_a.first_half, shards), grads_a
+        reduce("a", l, grads_a, [at[l]["normed"]], at[l]["packed_grad"], extra)
+
+    def backward_first(l):
+        pre_grad, attended_grad, up_sum, branch_sum = backward_branch(
+            own, clock.tie(branch_of(l)), at[l]["slope"], gathers[3 * l + 2].arrays, group_o, shards
         )
-        reduced[l] = (a_sum, u_sum, o_sum)
-        grad, branch = norm_backward(own, grad, [part, came], unit, inv, gains[l : l + 1])
-    input_grad = own_rows(branch)
-
-    qkv_g = up_g = out_g = down_g = None
-    smalls = [None] * layers
-    for l in reversed(range(layers)):
-        final = [net.sum_chips(v) for v in reduced[l]]
-        theirs = [net.other_core(v) for v in final]
-        o_before = None if down_g is None else [down_g, out_g]
-        down_g, out_g = unpack_rows(
-            own, final[2], theirs[2], o_before, l, layers, (ff_piece, head_piece), width
+        clock.mark(attended_grad)
+        at[l].update(pre_grad=pre_grad, attended_grad=attended_grad, up_sum=up_sum, branch_sum=branch_sum)
+
+    def backward_attention(l):
+        d = at[l]
+        d["dq"], d["dkv"] = attend_back(
+            meta, clock.tie(d["q"]), d["kv"], d["halo"], start_row, d["attended_grad"], d["attended"], d["lse"], tables
         )
-        up_g = unpack_columns(
-            own, final[1], theirs[1], up_g, l, layers, piece, 1, ff_piece, shards
+        clock.mark(d["dq"])
+
+    def send_halo_back(l):
+        part = clock.tie(at[l]["dkv"])[:reach]
+        clock.mark(part)
+        at[l]["halo_grad"] = net.last_chip(part)
+
+    def backward_norm_in(l):
+        d = at[l]
+        a = gathers[3 * l]
+        d["packed_grad"], part, d["qkv_sum"], d["gain_sum"], d["shift_sum"] = backward_normed(
+            own, clock.tie(d["dq"]), d["dkv"], d["halo_grad"], d["pre_grad"], d["unit"], tables,
+            a.arrays, gathers[3 * l + 1].arrays, a.group, group_u, shards,
         )
-        qkv_g = unpack_columns(
-            own, final[0], theirs[0], qkv_g, l, layers, piece, 3, head_piece, shards
+        clock.mark(part)
+        d["parts"] = [part, net.other_core(part)]
+
+    def backward_norm(l):
+        d = at[l]
+        grad = branch_top if l == top else at[l + 1]["grad"]
+        d["grad"], d["branch"] = norm_backward(
+            own, l, clock.tie(grad), d["parts"], d["unit"], d["inv"], common["vectors"][0]
         )
-        smalls[l] = (final[0][3 * piece :], theirs[0][3 * piece :])
-    mine, theirs = (jnp.stack([s[i] for s in smalls]).astype(f32) for i in range(2))
+        clock.mark(d["branch"])
+
+    def finish(name, l):
+        chains = [c for _, c in sorted(sums[name, l].chains.items())]
+        for c in chains:
+            c.step("r6")
+        mine, theirs = [c.mine for c in chains], [c.theirs for c in chains]
+        if name == "o":
+            got = unpack_rows(own, mine, theirs, common.get(name), l, layers, (ff_piece, head_piece), width)
+        else:
+            kinds, w = (3, head_piece) if name == "a" else (1, ff_piece)
+            got = unpack_columns(own, mine, theirs, common.get(name), l, layers, piece, kinds, w, shards)
+        common[name] = got
+        clock.mark(got)
+        if name == "a":
+            common["small", l] = mine[-1][-16:], theirs[-1][-16:]
+
+    kernels = {
+        "f1": forward_first, "f2": forward_second, "f3": forward_third, "f4": forward_fourth, "h": send_halo,
+        "wo": grads_out, "wu": grads_up, "wa": grads_qkv, "bb": backward_first, "ab": backward_attention,
+        "p": send_halo_back, "bn": backward_norm_in, "nb": backward_norm,
+    }
+    others = {"docs": lambda: clock.mark(docs), "out": output}
+    for token in ORDER:
+        if token in others:
+            others[token]()
+        elif token[:-1] in kernels:
+            kernels[token[:-1]](int(token[-1]))
+        else:
+            stage, name, l = token[:2], token[2], int(token[3])
+            weights = gathers[3 * l + "auo".index(name)]
+            if stage == "g0":
+                weights.near(clock)
+            elif stage == "g1":
+                weights.far(clock)
+            elif stage == "g2":
+                weights.arrived(clock)
+            elif stage == "r6":
+                finish(name, l)
+            elif stage in ("r0", "r1", "r2"):
+                sums[name, l].step(stage)
+            else:
+                sums[name, l].chains[token[4:]].step(stage)
+    block_output, input_grad = common["output"], own_rows(at[0]["branch"])
+    (down_g, out_g), up_g, qkv_g = common["o"], common["u"], common["a"]
+    mine, theirs = (
+        jnp.stack([common["small", l][i] for l in range(layers)]).astype(f32) for i in range(2)
+    )
     low, high = pick(core, mine, theirs), pick(core, theirs, mine)
     both = low + high
     branch_g = both[:, 1, :piece]

time: 899 us -> 772 us (0.86)
  waiting for transfers between devices: 312 us -> 177 us
  blocking collectives: 31.8 us -> 11.8 us
  starting transfers between devices: 147 us -> 159 us
  other arithmetic: 58.1 us -> 69.9 us
    ppermute x82 -> x86, waiting for transfers between devices: 312 us -> 177 us  [send(): return lax.ppermute(value, AXES, pairs)]
    all_gather x1 -> x0, blocking collectives: 17.3 us -> none  [body(): lax.all_gather(jnp.concatenate([v.reshape(-1) for v in names]), 'shard',...]
    ppermute x82 -> x86, starting transfers between devices: 147 us -> 159 us  [send(): return lax.ppermute(value, AXES, pairs)]
    unnamed x226 -> x268, local copies, waits for them, and re-layouts: 27 us -> 34.3 us
    pallas_call x34 -> x35, Pallas kernels: 290 us -> 292 us  [call(): pl.pallas_call(kernel, grid_spec=pltpu.PrefetchScalarGridSpec(num_scalar_...]
  transfers between devices with their start and end apart: 82 -> 86, of which waited for: 22 -> 28; matrix products, arithmetic and copies ran while one was open for 9% -> 11% of each run, Pallas kernels for 32% -> 36%
where the time goes in v2:
time: 772 us; the launch traced here: 764 us
  Pallas kernels  292 us (38%)
  waiting for transfers between devices  177 us (23%)
  starting transfers between devices  159 us (21%)
  other arithmetic  69.9 us (9%)
  local copies, waits for them, and re-layouts  51.1 us (7%)
  blocking collectives  11.8 us (2%)
    pallas_call x35, Pallas kernels, call(): pl.pallas_call(kernel, grid_spec=pltpu.PrefetchScalarGridSpec(num_scalar_...  292 us
    ppermute x86, waiting for transfers between devices, send(): return lax.ppermute(value, AXES, pairs)  177 us
    ppermute x86, starting transfers between devices, send(): return lax.ppermute(value, AXES, pairs)  159 us
    convert_element_type x34, other arithmetic, sum_low(): return total.astype(bf16)  42 us
    unnamed x268, local copies, waits for them, and re-layouts  34.3 us
  transfers between devices with their start and end apart: 86, of which 28 were waited for; matrix products, arithmetic and copies ran while one was open for 11% of the time, Pallas kernels for 36%

profile of v2, /device:TPU:1, one launch (start us, length us, event | category | flops | bytes accessed | tf_op | source)
XLA Modules:
  0.0 763.9 jit_solution(593312543469701896)
XLA Ops:
  12.4 11.8 %all-gather.1 = s32[8,2,4]{2,1,0:T(2,128)S(1)} all-gather(s32[1,2,4]{2,1,0:T(2,128)S(1)} %add_bitcast_fusion), channel_id=2, replica_groups=mesh['shard'=4,'rep'=8] {'rep'}, dimensions={0}, use_global_device_ids=true | all-gather | bytes 288 | tf_op jit(solution)/shard_map/all_gather | solution.py:1163
  86.3 16.8 %shard_map.236 = (bf16[1024,2048]{1,0:T(8,128)(2,1)}, bf16[1024,2048]{1,0:T(8,128)(2,1)}) custom-call(s32[2]{0:T(128)S(1)} %pad_add_fusion.own_ref, bf16[1024,1024]{1,0:T(8,128)(2,1)} %get-tuple-element.399.x_ref.refs_0_, f32[8,2048]{1,0:T(8,128)S(1)} %get-tuple-element.246.b_ref, bf16[1024,512]{1,0:T(8,128)(2,1)} %shard_map.229.rest_0_.rest_5_, ...), custom_call_target="tpu_custom_call" | custom-call | flops 1 | bytes 1 | tf_op jit(solution)/shard_map/pallas_call | solution.py:42
  103.1 12.5 %shard_map.237 = (bf16[1024,512]{1,0:T(8,128)(2,1)S(1)}, f32[8,1024]{1,0:T(8,128)S(1)}) custom-call(s32[4]{0:T(128)S(1)} %subtract_clamp_fusion.meta_ref, bf16[1024,512]{1,0:T(8,128)(2,1)S(1)} %copy-done.32, bf16[1024,1024]{1,0:T(8,128)(2,1)S(1)} %copy-done.6, bf16[512,1024]{1,0:T(8,128)(2,1)} %collective-permute-done.11.halo_ref, s32[1024,1]{1,0:T(8,128)S(1)} %copy-done.30), custom_call_target="tpu_custom_call" | custom-call | flops 1 | bytes 1 | tf_op jit(solution)/shard_map/pallas_call | solution.py:42
  130.0 11.4 %shard_map.238.refs_1_ = bf16[1024,1024]{1,0:T(8,128)(2,1)} custom-call(s32[2]{0:T(128)S(1)} %pad_add_fusion.own_ref, bf16[1024,512]{1,0:T(8,128)(2,1)S(1)} %get-tuple-element.259.att_ref.refs_1_.o_ref, bf16[1024,2048]{1,0:T(8,128)(2,1)} %get-tuple-element.346.act_ref.refs_0_, bf16[1280,512]{1,0:T(8,128)(2,1)} %shard_map.235.rest_0_, ...), custom_call_target="tpu_custom_call" | custom-call | flops 1 | bytes 1 | tf_op jit(solution)/shard_map/pallas_call | solution.py:42
  141.4 13.4 %collective-permute-start.18 = (bf16[1024,1024]{1,0:T(8,128)(2,1)}, bf16[1024,1024]{1,0:T(8,128)(2,1)S(1)}, u32[]{:S(2)}, u32[]{:S(2)}) collective-permute-start(bf16[1024,1024]{1,0:T(8,128)(2,1)} %shard_map.238.refs_1_), channel_id=1, source_target_pairs={{0,1},{1,0},{2,3},{3,2},{4,5},{5,4},{6,7},{7,6},{8,9},{9,8},{10,11... | collective-permute-start | bytes 6291464 | tf_op jit(solution)/shard_map/ppermute | solution.py:924
  168.9 11.9 %shard_map.239 = (f32[1024,1024]{1,0:T(8,128)}, bf16[1024,1024]{1,0:T(8,128)(2,1)}, f32[1024,128]{1,0:T(8,128)S(1)}, bf16[1024,1024]{1,0:T(8,128)(2,1)}, bf16[10...) custom-call(s32[2]{0:T(128)S(1)} %pad_add_fusion.own_ref, f32[1024,1024]{1,0:T(8,128)} %get-tuple-element.269.refs_0_, ...), custom_call_target="tpu_custom_call" | custom-call | flops 1 | bytes 1 | tf_op jit(solution)/shard_map/pallas_call | solution.py:42
  212.1 15.6 %shard_map.241 = (bf16[1024,2048]{1,0:T(8,128)(2,1)}, bf16[1024,2048]{1,0:T(8,128)(2,1)}) custom-call(s32[2]{0:T(128)S(1)} %pad_add_fusion.own_ref, bf16[1024,1024]{1,0:T(8,128)(2,1)} %get-tuple-element.328.x_ref.refs_0_, f32[8,2048]{1,0:T(8,128)S(1)} %get-tuple-element.246.b_ref, bf16[1024,512]{1,0:T(8,128)(2,1)S(1)} %shard_map.233.rest_0_.rest_5_, ...), custom_call_target="tpu_custom_call" | custom-call | flops 1 | bytes 1 | tf_op jit(solution)/shard_map/pallas_call | solution.py:42
  227.8 11.7 %shard_map.242 = (bf16[1024,512]{1,0:T(8,128)(2,1)S(1)}, f32[8,1024]{1,0:T(8,128)S(1)}) custom-call(s32[4]{0:T(128)S(1)} %subtract_clamp_fusion.meta_ref, bf16[1024,512]{1,0:T(8,128)(2,1)S(1)} %copy-done.34, bf16[1024,1024]{1,0:T(8,128)(2,1)S(1)} %copy-done.7, bf16[512,1024]{1,0:T(8,128)(2,1)S(1)} %collective-permute-done.25.halo_ref, s32[1024,1]{1,0:T(8,128)S(1)} %copy-done.31), custom_call_target="tpu_custom_call" | custom-call | flops 1 | bytes 1 | tf_op jit(solution)/shard_map/pallas_call | solution.py:42
  246.0 11.4 %shard_map.243 = (bf16[1280,512]{1,0:T(8,128)(2,1)S(1)}, bf16[1280,512]{1,0:T(8,128)(2,1)S(1)}, bf16[1280,512]{1,0:T(8,128)(2,1)}, bf16[640,512]{1,0:T(8,128)(2,1)S(1)}, bf16[640,512]{1,0:T(8,128)(2,1)S(1)}) custom-call(s32[2]{0:T(128)S(1)} %pad_add_fusion.own_ref, bf16[1024,2048]{1,0:T(8,128)(2,1)} %get-tuple-element.295.refs_0_.act_ref, ...), custom_call_target="tpu_custom_call" | custom-call | flops 1 | bytes 1 | tf_op jit(solution)/shard_map/pallas_call | solution.py:42
  259.8 10.9 %shard_map.244 = bf16[1024,1024]{1,0:T(8,128)(2,1)} custom-call(s32[2]{0:T(128)S(1)} %pad_add_fusion.own_ref, bf16[1024,512]{1,0:T(8,128)(2,1)S(1)} %get-tuple-element.301.refs_1_.att_ref.o_ref, bf16[1024,2048]{1,0:T(8,128)(2,1)} %get-tuple-element.295.refs_0_.act_ref, bf16[1280,512]{1,0:T(8,128)(2,1)S(1)} %shard_map.240.rest_0_, ...), custom_call_target="tpu_custom_call" | custom-call | flops 1 | bytes 1 | tf_op jit(solution)/shard_map/pallas_call | solution.py:42
  275.8 12.1 %shard_map.245 = (bf16[1024,2048]{1,0:T(8,128)(2,1)}, bf16[1024,512]{1,0:T(8,128)(2,1)S(1)}, f32[1,2048]{1,0:T(1,128)S(1)}, f32[1,1024]{1,0:T(1,128)S(1)}) custom-call(s32[2]{0:T(128)S(1)} %pad_add_fusion.own_ref, bf16[1024,1024]{1,0:T(8,128)(2,1)} %pad_maximum_fusion.1.refs_2_.g_ref, bf16[1024,2048]{1,0:T(8,128)(2,1)} %get-tuple-element.290.slope_ref, ...), custom_call_target="tpu_custom_call" | custom-call | flops 1 | bytes 1 | tf_op jit(solution)/shard_map/pallas_call | solution.py:42
  287.9 19.1 %shard_map.246 = (bf16[1024,512]{1,0:T(8,128)(2,1)S(1)}, bf16[1536,1024]{1,0:T(8,128)(2,1)}) custom-call(s32[4]{0:T(128)S(1)} %subtract_clamp_fusion.meta_ref, bf16[1024,512]{1,0:T(8,128)(2,1)S(1)} %copy-done.34, bf16[1024,1024]{1,0:T(8,128)(2,1)} %get-tuple-element.281.kv_ref, bf16[512,1024]{1,0:T(8,128)(2,1)S(1)} %copy-done.36, s32[1,1024]{1,0:T(1,128)S(1)} %bitcast.36, ...), custom_call_target="tpu_custom_call" | custom-call | flops 1 | bytes 1 | tf_op jit(solution)/shard_map/pallas_call | solution.py:42
  342.8 16.4 %shard_map.248 = (bf16[1024,1536]{1,0:T(8,128)(2,1)}, bf16[1024,1024]{1,0:T(8,128)(2,1)}, f32[1,1536]{1,0:T(1,128)S(1)}, f32[1,1024]{1,0:T(1,128)S(1)}, f32[1,1024]{1,0:T(1,128)S(1)}) custom-call(s32[2]{0:T(128)S(1)} %pad_add_fusion.own_ref, bf16[1024,512]{1,0:T(8,128)(2,1)} %copy-done.71, bf16[1536,1024]{1,0:T(8,128)(2,1)} %get-tuple-element.312.dkv_ref, ...), custom_call_target="tpu_custom_call" | custom-call | flops 1 | bytes 1 | tf_op jit(solution)/shard_map/pallas_call | solution.py:42
  379.4 12.1 %collective-permute-done.32 = bf16[1024,512]{1,0:T(8,128)(2,1)} collective-permute-done((bf16[1024,512]{1,0:T(8,128)(2,1)}, bf16[1024,512]{1,0:T(8,128)(2,1)}, u32[]{:S(2)}, u32[]{:S(2)}) %collective-permute-start.32) | collective-permute-done | bytes 1048608 | tf_op jit(solution)/shard_map/ppermute | solution.py:924
  406.1 15.2 %collective-permute-done.38 = bf16[512,512]{1,0:T(8,128)(2,1)S(1)} collective-permute-done((bf16[512,512]{1,0:T(8,128)(2,1)S(1)}, bf16[512,512]{1,0:T(8,128)(2,1)S(1)}, u32[]{:S(2)}, u32[]{:S(2)}) %collective-permute-start.38) | collective-permute-done | bytes 524320 | tf_op jit(solution)/shard_map/ppermute | solution.py:924
  427.8 11.4 %shard_map.251 = (bf16[1280,512]{1,0:T(8,128)(2,1)S(1)}, bf16[1280,512]{1,0:T(8,128)(2,1)S(1)}, bf16[1280,512]{1,0:T(8,128)(2,1)}, bf16[640,512]{1,0:T(8,128)(2,1)S(1)}, bf16[640,512]{1,0:T(8,128)(2,1)S(1)}) custom-call(s32[2]{0:T(128)S(1)} %pad_add_fusion.own_ref, bf16[1024,2048]{1,0:T(8,128)(2,1)} %get-tuple-element.346.act_ref.refs_0_, ...), custom_call_target="tpu_custom_call" | custom-call | flops 1 | bytes 1 | tf_op jit(solution)/shard_map/pallas_call | solution.py:42
  444.0 12.3 %shard_map.252 = (bf16[1024,2048]{1,0:T(8,128)(2,1)}, bf16[1024,512]{1,0:T(8,128)(2,1)S(1)}, f32[1,2048]{1,0:T(1,128)S(1)}, f32[1,1024]{1,0:T(1,128)S(1)}) custom-call(s32[2]{0:T(128)S(1)} %pad_add_fusion.own_ref, bf16[1024,1024]{1,0:T(8,128)(2,1)} %copy-done.17, bf16[1024,2048]{1,0:T(8,128)(2,1)} %get-tuple-element.250.slope_ref, ...), custom_call_target="tpu_custom_call" | custom-call | flops 1 | bytes 1 | tf_op jit(solution)/shard_map/pallas_call | solution.py:42
  479.0 19.2 %shard_map.253 = (bf16[1024,512]{1,0:T(8,128)(2,1)S(1)}, bf16[1536,1024]{1,0:T(8,128)(2,1)}) custom-call(s32[4]{0:T(128)S(1)} %subtract_clamp_fusion.meta_ref, bf16[1024,512]{1,0:T(8,128)(2,1)S(1)} %copy-done.33, bf16[1024,1024]{1,0:T(8,128)(2,1)} %get-tuple-element.240.kv_ref, bf16[512,1024]{1,0:T(8,128)(2,1)} %collective-permute-done.11.halo_ref, ...), custom_call_target="tpu_custom_call" | custom-call | flops 1 | bytes 1 | tf_op jit(solution)/shard_map/pallas_call | solution.py:42
  545.9 16.5 %collective-permute-done.61.halo_ref = bf16[512,1024]{1,0:T(8,128)(2,1)S(1)} collective-permute-done((bf16[512,1024]{1,0:T(8,128)(2,1)S(1)}, bf16[512,1024]{1,0:T(8,128)(2,1)S(1)}, u32[]{:S(2)}, u32[]{:S(2)}) %collective-permute-start.61) | collective-permute-done | bytes 1048608 | tf_op jit(solution)/shard_map/ppermute | solution.py:924
  563.5 16.5 %shard_map.257 = (bf16[1024,1536]{1,0:T(8,128)(2,1)}, bf16[1024,1024]{1,0:T(8,128)(2,1)}, f32[1,1536]{1,0:T(1,128)S(1)}, f32[1,1024]{1,0:T(1,128)S(1)}, f32[1,1024]{1,0:T(1,128)S(1)}) custom-call(s32[2]{0:T(128)S(1)} %pad_add_fusion.own_ref, bf16[1024,512]{1,0:T(8,128)(2,1)} %copy-done.68, bf16[1536,1024]{1,0:T(8,128)(2,1)} %get-tuple-element.375.dkv_ref, ...), custom_call_target="tpu_custom_call" | custom-call | flops 1 | bytes 1 | tf_op jit(solution)/shard_map/pallas_call | solution.py:42
  580.7 18.7 %collective-permute-start.56 = (bf16[1280,512]{1,0:T(8,128)(2,1)}, bf16[1280,512]{1,0:T(8,128)(2,1)}, u32[]{:S(2)}, u32[]{:S(2)}) collective-permute-start(bf16[1280,512]{1,0:T(8,128)(2,1)} %pad_maximum_fusion.3), channel_id=1, source_target_pairs={{0,2},{1,3},{6,4},{7,5},{8,10},{9,11},{14,12},{15,13},{16,18},{17,... | collective-permute-start | bytes 3932168 | tf_op jit(solution)/shard_map/ppermute | solution.py:924
  608.5 18.2 %collective-permute-done.56 = bf16[1280,512]{1,0:T(8,128)(2,1)} collective-permute-done((bf16[1280,512]{1,0:T(8,128)(2,1)}, bf16[1280,512]{1,0:T(8,128)(2,1)}, u32[]{:S(2)}, u32[]{:S(2)}) %collective-permute-start.56) | collective-permute-done | bytes 1310752 | tf_op jit(solution)/shard_map/ppermute | solution.py:924
  658.8 9.7 %collective-permute-done.67 = bf16[1024,512]{1,0:T(8,128)(2,1)} collective-permute-done((bf16[1024,512]{1,0:T(8,128)(2,1)}, bf16[1024,512]{1,0:T(8,128)(2,1)}, u32[]{:S(2)}, u32[]{:S(2)}) %collective-permute-start.67) | collective-permute-done | bytes 1048608 | tf_op jit(solution)/shard_map/ppermute | solution.py:924
  719.3 26.2 %collective-permute-done.82 = bf16[384,512]{1,0:T(8,128)(2,1)S(1)} collective-permute-done((bf16[384,512]{1,0:T(8,128)(2,1)S(1)}, bf16[384,512]{1,0:T(8,128)(2,1)S(1)}, u32[]{:S(2)}, u32[]{:S(2)}) %collective-permute-start.82) | collective-permute-done | bytes 393248 | tf_op jit(solution)/shard_map/ppermute | solution.py:924
  (587 shorter events, 409.6 us)
Async XLA Ops:
  74.6 41.1 %collective-permute-start.10 = (bf16[1280,512]{1,0:T(8,128)(2,1)}, bf16[1280,512]{1,0:T(8,128)(2,1)}, u32[]{:S(2)}, u32[]{:S(2)}) collective-permute-start(bf16[1280,512]{1,0:T(8,128)(2,1)} %shard_map.235.rest_0_), channel_id=1, source_target_pairs={{0,16},{1,17},{2,18},{3,19},{4,20},{5,21},{6,22},{7,23},{8,24},{9,... | collective-permute-start | bytes 3932168 | tf_op jit(solution)/shard_map/ppermute | solution.py:924
  75.6 40.1 %collective-permute-start.9 = (bf16[1280,512]{1,0:T(8,128)(2,1)}, bf16[1280,512]{1,0:T(8,128)(2,1)}, u32[]{:S(2)}, u32[]{:S(2)}) collective-permute-start(bf16[1280,512]{1,0:T(8,128)(2,1)} %shard_map.235.rest_0_), channel_id=1, source_target_pairs={{0,8},{1,9},{2,10},{3,11},{4,12},{5,13},{6,14},{7,15},{8,0},{9,1},... | collective-permute-start | bytes 3932168 | tf_op jit(solution)/shard_map/ppermute | solution.py:924
  202.7 36.8 %collective-permute-start.24 = (bf16[1280,512]{1,0:T(8,128)(2,1)S(1)}, bf16[1280,512]{1,0:T(8,128)(2,1)S(1)}, u32[]{:S(2)}, u32[]{:S(2)}) collective-permute-start(bf16[1280,512]{1,0:T(8,128)(2,1)S(1)} %shard_map.240.rest_0_), channel_id=1, source_target_pairs={{0,16},{1,17},{2,18},{3,19},{4,20},{5,21},{6,22},{7,23},{8,24},{9,... | collective-permute-start | bytes 3932168 | tf_op jit(solution)/shard_map/ppermute | solution.py:924
  203.6 35.9 %collective-permute-start.23 = (bf16[1280,512]{1,0:T(8,128)(2,1)S(1)}, bf16[1280,512]{1,0:T(8,128)(2,1)S(1)}, u32[]{:S(2)}, u32[]{:S(2)}) collective-permute-start(bf16[1280,512]{1,0:T(8,128)(2,1)S(1)} %shard_map.240.rest_0_), channel_id=1, source_target_pairs={{0,8},{1,9},{2,10},{3,11},{4,12},{5,13},{6,14},{7,15},{8,0},{9,1},... | collective-permute-start | bytes 3932168 | tf_op jit(solution)/shard_map/ppermute | solution.py:924
  258.4 51.4 %collective-permute-start.27 = (bf16[1280,512]{1,0:T(8,128)(2,1)}, bf16[1280,512]{1,0:T(8,128)(2,1)S(1)}, u32[]{:S(2)}, u32[]{:S(2)}) collective-permute-start(bf16[1280,512]{1,0:T(8,128)(2,1)} %get-tuple-element.298), channel_id=1, source_target_pairs={{0,8},{1,9},{2,10},{3,11},{4,12},{5,13},{6,14},{7,15},{8,0},{9,1},... | collective-permute-start | bytes 3932168 | tf_op jit(solution)/shard_map/ppermute | solution.py:924
  258.7 51.1 %collective-permute-start.28 = (bf16[1280,512]{1,0:T(8,128)(2,1)S(1)}, bf16[1280,512]{1,0:T(8,128)(2,1)S(1)}, u32[]{:S(2)}, u32[]{:S(2)}) collective-permute-start(bf16[1280,512]{1,0:T(8,128)(2,1)S(1)} %get-tuple-element.299), channel_id=1, source_target_pairs={{0,16},{1,17},{2,18},{3,19},{4,20},{5,21},{6,22},{7,23},{8,24},{9,... | collective-permute-start | bytes 3932168 | tf_op jit(solution)/shard_map/ppermute | solution.py:924
  270.8 44.2 %collective-permute-start.31 = (bf16[1024,1024]{1,0:T(8,128)(2,1)}, bf16[1024,1024]{1,0:T(8,128)(2,1)}, u32[]{:S(2)}, u32[]{:S(2)}) collective-permute-start(bf16[1024,1024]{1,0:T(8,128)(2,1)} %shard_map.244), channel_id=1, source_target_pairs={{0,1},{1,0},{2,3},{3,2},{4,5},{5,4},{6,7},{7,6},{8,9},{9,8},{10,11... | collective-permute-start | bytes 6291464 | tf_op jit(solution)/shard_map/ppermute | solution.py:924
  359.2 36.5 %collective-permute-start.37 = (bf16[1024,1024]{1,0:T(8,128)(2,1)}, bf16[1024,1024]{1,0:T(8,128)(2,1)}, u32[]{:S(2)}, u32[]{:S(2)}) collective-permute-start(bf16[1024,1024]{1,0:T(8,128)(2,1)} %get-tuple-element.327.p0_ref), channel_id=1, source_target_pairs={{0,1},{1,0},{2,3},{3,2},{4,5},{5,4},{6,7},{7,6},{8,9},{9,8},{10,11... | collective-permute-start | bytes 6291464 | tf_op jit(solution)/shard_map/ppermute | solution.py:924
  361.9 41.7 %collective-permute-start.40 = (bf16[1280,512]{1,0:T(8,128)(2,1)}, bf16[1280,512]{1,0:T(8,128)(2,1)}, u32[]{:S(2)}, u32[]{:S(2)}) collective-permute-start(bf16[1280,512]{1,0:T(8,128)(2,1)} %pad_maximum_fusion.2), channel_id=1, source_target_pairs={{0,2},{1,3},{6,4},{7,5},{8,10},{9,11},{14,12},{15,13},{16,18},{17,... | collective-permute-start | bytes 3932168 | tf_op jit(solution)/shard_map/ppermute | solution.py:924
  378.3 63.1 %collective-permute-start.46 = (bf16[768,512]{1,0:T(8,128)(2,1)S(1)}, bf16[768,512]{1,0:T(8,128)(2,1)}, u32[]{:S(2)}, u32[]{:S(2)}) collective-permute-start(bf16[768,512]{1,0:T(8,128)(2,1)S(1)} %get-tuple-element.352), channel_id=1, source_target_pairs={{0,16},{1,17},{2,18},{3,19},{4,20},{5,21},{6,22},{7,23},{8,24},{9,... | collective-permute-start | bytes 2359304 | tf_op jit(solution)/shard_map/ppermute | solution.py:924
  391.5 50.0 %collective-permute-start.45 = (bf16[800,512]{1,0:T(8,128)(2,1)S(1)}, bf16[800,512]{1,0:T(8,128)(2,1)}, u32[]{:S(2)}, u32[]{:S(2)}) collective-permute-start(bf16[800,512]{1,0:T(8,128)(2,1)S(1)} %get-tuple-element.351), channel_id=1, source_target_pairs={{0,8},{1,9},{2,10},{3,11},{4,12},{5,13},{6,14},{7,15},{8,0},{9,1},... | collective-permute-start | bytes 2457608 | tf_op jit(solution)/shard_map/ppermute | solution.py:924
  425.6 35.7 %collective-permute-start.43 = (bf16[1280,512]{1,0:T(8,128)(2,1)S(1)}, bf16[1280,512]{1,0:T(8,128)(2,1)}, u32[]{:S(2)}, u32[]{:S(2)}) collective-permute-start(bf16[1280,512]{1,0:T(8,128)(2,1)S(1)} %add_convert_fusion.3), channel_id=1, source_target_pairs={{2,4},{3,5},{4,2},{5,3},{10,12},{11,13},{12,10},{13,11},{18,20},{1... | collective-permute-start | bytes 3932168 | tf_op jit(solution)/shard_map/ppermute | solution.py:924
  459.7 38.6 %collective-permute-start.51 = (bf16[1024,512]{1,0:T(8,128)(2,1)}, bf16[1024,512]{1,0:T(8,128)(2,1)}, u32[]{:S(2)}, u32[]{:S(2)}) collective-permute-start(bf16[1024,512]{1,0:T(8,128)(2,1)} %add_convert_fusion.7), channel_id=1, source_target_pairs={{2,4},{3,5},{4,2},{5,3},{10,12},{11,13},{12,10},{13,11},{18,20},{1... | collective-permute-start | bytes 3145736 | tf_op jit(solution)/shard_map/ppermute | solution.py:924
  464.2 37.8 %collective-permute-start.47 = (bf16[1280,512]{1,0:T(8,128)(2,1)}, bf16[1280,512]{1,0:T(8,128)(2,1)}, u32[]{:S(2)}, u32[]{:S(2)}) collective-permute-start(bf16[1280,512]{1,0:T(8,128)(2,1)} %add_convert_fusion.2), channel_id=1, source_target_pairs={{2,0},{3,1},{4,6},{5,7},{10,8},{11,9},{12,14},{13,15},{18,16},{19,... | collective-permute-start | bytes 3932168 | tf_op jit(solution)/shard_map/ppermute | solution.py:924
  537.0 65.1 %collective-permute-start.57 = (bf16[1024,512]{1,0:T(8,128)(2,1)}, bf16[1024,512]{1,0:T(8,128)(2,1)}, u32[]{:S(2)}, u32[]{:S(2)}) collective-permute-start(bf16[1024,512]{1,0:T(8,128)(2,1)} %get-tuple-element.383), channel_id=1, source_target_pairs={{0,8},{1,9},{2,10},{3,11},{4,12},{5,13},{6,14},{7,15},{8,0},{9,1},... | collective-permute-start | bytes 3145736 | tf_op jit(solution)/shard_map/ppermute | solution.py:924
  537.1 65.0 %collective-permute-start.58 = (bf16[1024,512]{1,0:T(8,128)(2,1)}, bf16[1024,512]{1,0:T(8,128)(2,1)}, u32[]{:S(2)}, u32[]{:S(2)}) collective-permute-start(bf16[1024,512]{1,0:T(8,128)(2,1)} %get-tuple-element.384), channel_id=1, source_target_pairs={{0,16},{1,17},{2,18},{3,19},{4,20},{5,21},{6,22},{7,23},{8,24},{9,... | collective-permute-start | bytes 3145736 | tf_op jit(solution)/shard_map/ppermute | solution.py:924
  580.0 51.6 %collective-permute-start.62 = (bf16[1024,1024]{1,0:T(8,128)(2,1)}, bf16[1024,1024]{1,0:T(8,128)(2,1)}, u32[]{:S(2)}, u32[]{:S(2)}) collective-permute-start(bf16[1024,1024]{1,0:T(8,128)(2,1)} %get-tuple-element.389.p0_ref), channel_id=1, source_target_pairs={{0,1},{1,0},{2,3},{3,2},{4,5},{5,4},{6,7},{7,6},{8,9},{9,8},{10,11... | collective-permute-start | bytes 6291464 | tf_op jit(solution)/shard_map/ppermute | solution.py:924
  580.7 46.0 %collective-permute-start.56 = (bf16[1280,512]{1,0:T(8,128)(2,1)}, bf16[1280,512]{1,0:T(8,128)(2,1)}, u32[]{:S(2)}, u32[]{:S(2)}) collective-permute-start(bf16[1280,512]{1,0:T(8,128)(2,1)} %pad_maximum_fusion.3), channel_id=1, source_target_pairs={{0,2},{1,3},{6,4},{7,5},{8,10},{9,11},{14,12},{15,13},{16,18},{17,... | collective-permute-start | bytes 3932168 | tf_op jit(solution)/shard_map/ppermute | solution.py:924
  600.8 76.4 %collective-permute-start.71 = (bf16[784,512]{1,0:T(8,128)(2,1)}, bf16[784,512]{1,0:T(8,128)(2,1)}, u32[]{:S(2)}, u32[]{:S(2)}) collective-permute-start(bf16[784,512]{1,0:T(8,128)(2,1)} %add_convert_fusion.9), channel_id=1, source_target_pairs={{2,0},{3,1},{4,6},{5,7},{10,8},{11,9},{12,14},{13,15},{18,16},{19,... | collective-permute-start | bytes 2408456 | tf_op jit(solution)/shard_map/ppermute | solution.py:924
  676.0 35.3 %collective-permute-start.77 = (bf16[1280,512]{1,0:T(8,128)(2,1)S(1)}, bf16[1280,512]{1,0:T(8,128)(2,1)S(1)}, u32[]{:S(2)}, u32[]{:S(2)}) collective-permute-start(bf16[1280,512]{1,0:T(8,128)(2,1)S(1)} %add_convert_fusion), channel_id=1, source_target_pairs={{2,0},{3,1},{4,6},{5,7},{10,8},{11,9},{12,14},{13,15},{18,16},{19,... | collective-permute-start | bytes 3932168 | tf_op jit(solution)/shard_map/ppermute | solution.py:924
  707.8 37.7 %collective-permute-start.81 = (bf16[1024,512]{1,0:T(8,128)(2,1)S(1)}, bf16[1024,512]{1,0:T(8,128)(2,1)S(1)}, u32[]{:S(2)}, u32[]{:S(2)}) collective-permute-start(bf16[1024,512]{1,0:T(8,128)(2,1)S(1)} %add_convert_fusion.4), channel_id=1, source_target_pairs={{2,0},{3,1},{4,6},{5,7},{10,8},{11,9},{12,14},{13,15},{18,16},{19,... | collective-permute-start | bytes 3145736 | tf_op jit(solution)/shard_map/ppermute | solution.py:924
  710.0 35.5 %collective-permute-start.82 = (bf16[384,512]{1,0:T(8,128)(2,1)S(1)}, bf16[384,512]{1,0:T(8,128)(2,1)S(1)}, u32[]{:S(2)}, u32[]{:S(2)}) collective-permute-start(bf16[384,512]{1,0:T(8,128)(2,1)S(1)} %add_convert_fusion.33), channel_id=1, source_target_pairs={{2,0},{3,1},{4,6},{5,7},{10,8},{11,9},{12,14},{13,15},{18,16},{19,... | collective-permute-start | bytes 1179656 | tf_op jit(solution)/shard_map/ppermute | solution.py:924
  711.5 36.2 %collective-permute-start.80 = (bf16[1280,512]{1,0:T(8,128)(2,1)S(1)}, bf16[1280,512]{1,0:T(8,128)(2,1)S(1)}, u32[]{:S(2)}, u32[]{:S(2)}) collective-permute-start(bf16[1280,512]{1,0:T(8,128)(2,1)S(1)} %broadcast_select_fusion.refs_0_), channel_id=1, source_target_pairs={{0,1},{1,0},{2,3},{3,2},{4,5},{5,4},{6,7},{7,6},{8,9},{9,8},{10,11... | collective-permute-start | bytes 3932168 | tf_op jit(solution)/shard_map/ppermute | solution.py:924
  717.8 36.4 %collective-permute-start.79 = (bf16[400,512]{1,0:T(8,128)(2,1)S(1)}, bf16[400,512]{1,0:T(8,128)(2,1)S(1)}, u32[]{:S(2)}, u32[]{:S(2)}) collective-permute-start(bf16[400,512]{1,0:T(8,128)(2,1)S(1)} %add_convert_fusion.27), channel_id=1, source_target_pairs={{2,0},{3,1},{4,6},{5,7},{10,8},{11,9},{12,14},{13,15},{18,16},{19,... | collective-permute-start | bytes 1228808 | tf_op jit(solution)/shard_map/ppermute | solution.py:924
  (191 other events, 2577.4 us)

commit v3 on v2

--- a/solution.py
+++ b/solution.py
@@ -140,8 +140,9 @@
     return parts
 
 
-def forward_qkv(own, layer, prev, adds, biases, gain, shift, qkv_b, tables, pieces, group, shards, block=256):
+def forward_qkv(own, layer, prev, adds, biases, gain, shift, qkv_b, tables, pieces, group, shards, tail, block=256):
     rows, width = prev.shape
+    late = (rows - tail) // block
     count = len(pieces)
     n_add = len(adds)
     plan = assembly(group, shards)
@@ -154,7 +155,7 @@
         gain_ref, shift_ref, qkvb_ref, c_ref, s1_ref, s2_ref, *rest = rest
         now = slice(layer, layer + 1)
         piece_refs, rest = rest[:count], rest[count:]
-        stream_ref, unit_ref, inv_ref, normed_ref, q_ref, kv_ref, w_ref, sems = rest
+        stream_ref, unit_ref, inv_ref, normed_ref, q_ref, kv_ref, tail_ref, w_ref, sems = rest
 
         @pl.when(pl.program_id(0) == 0)
         def _():
@@ -192,6 +193,10 @@
         v = nn(normed, w_ref[2]) + qkvb_ref[now, 2 * half :]
         kv_ref[:, half:] = v.astype(bf16)
 
+        @pl.when(pl.program_id(0) >= late)
+        def _():
+            tail_ref[...] = kv_ref[...]
+
     wide = row_blocks(block, width)
     inputs = (
         [(prev, wide)]
@@ -208,6 +213,7 @@
         (S((rows, width), bf16), wide),
         (S((rows, half), bf16), row_blocks(block, half)),
         (S((rows, 2 * half), bf16), row_blocks(block, 2 * half)),
+        (S((tail, 2 * half), bf16), pl.BlockSpec((block, 2 * half), lambda i, *_: (jnp.maximum(i - late, 0), 0))),
     ]
     return call(
         kernel, own, inputs, outputs, (rows // block,),
@@ -377,7 +383,7 @@
     steps = rows // block
 
     def kernel(meta_ref, q_ref, kv_ref, halo_ref, ds_ref, g_ref, o_ref, lse_ref, c_ref, s1_ref, s2_ref,
-               dq_ref, dkv_ref, ext_ref, acc_ref, bias_ref, sems):
+               dq_ref, dkv_ref, far_ref, ext_ref, acc_ref, bias_ref, sems):
         b = pl.program_id(0)
 
         @pl.when(b == 0)
@@ -431,7 +437,8 @@
 
         @pl.when(b == steps - 1)
         def _():
-            dkv_ref[...] = acc_ref[...].astype(bf16)
+            far_ref[...] = acc_ref[:reach, :].astype(bf16)
+            dkv_ref[...] = acc_ref[reach:, :].astype(bf16)
 
     S = jax.ShapeDtypeStruct
     narrow = row_blocks(block, width)
@@ -446,7 +453,8 @@
         + [(t, row_blocks(block, 128)) for t in tables],
         [
             (S((rows, width), bf16), narrow),
-            (S((rows + reach, 2 * width), bf16), whole((rows + reach, 2 * width))),
+            (S((rows, 2 * width), bf16), whole((rows, 2 * width))),
+            (S((reach, 2 * width), bf16), whole((reach, 2 * width))),
         ],
         (steps,),
         [
@@ -570,12 +578,11 @@
             shift_ref[:, at] += jnp.sum(total, axis=0, keepdims=True)
 
     S = jax.ShapeDtypeStruct
-    skip = reach // block
     return call(
         kernel, own,
         [
             (dq, row_blocks(block, half)),
-            (dkv, pl.BlockSpec((block, 2 * half), lambda i, *_: (i + skip, 0))),
+            (dkv, row_blocks(block, 2 * half)),
             (halo, pl.BlockSpec((block, 2 * half), lambda i, *_: (jnp.maximum(i - late, 0), 0))),
             (pre_grad, row_blocks(block, ff)),
             (unit, row_blocks(block, width)),
@@ -619,7 +626,7 @@
         [(grad, wide), (parts[0], wide), (parts[1], wide), (unit, wide), (inv, row_blocks(block, 128)),
          (gain, whole(gain.shape))],
         [(S((rows, width), f32), wide), (S((rows, width), bf16), wide)],
-        (rows // block,), bytes_=rows * width * 16, flops=rows * width * 10,
+        (rows // block,), flops=2 * rows * width * width,
     )
 
 
@@ -674,7 +681,66 @@
     return call(
         kernel, own, inputs, [(S(s, bf16), whole(s)) for s in shapes], (1,),
         [pltpu.VMEM((l.shape[1], rows), bf16) for l in lefts],
-    )
+        flops=2 * rows * sum(l.shape[1] for l in lefts) * rights.shape[1],
+    )
+
+
+def combine(own, arrays, outs):
+    n = len(arrays)
+
+    def kernel(own_ref, *refs):
+        for ref, (_, segments) in zip(refs[n:], outs):
+            for start, rows, terms in segments:
+                total = None
+                for a, first in terms:
+                    part = refs[a][first : first + rows, :]
+                    if len(terms) > 1:
+                        part = part.astype(f32)
+                    total = part if total is None else total + part
+                ref[start : start + rows, :] = total.astype(bf16)
+
+    shapes = [(rows, arrays[0].shape[1]) for rows, _ in outs]
+    return call(
+        kernel, own, [(a, whole(a.shape)) for a in arrays],
+        [(jax.ShapeDtypeStruct(s, bf16), whole(s)) for s in shapes], (1,),
+    )
+
+
+def choose(own, first, second):
+    def kernel(own_ref, a_ref, b_ref, out_ref):
+        out_ref[...] = jnp.where(own_ref[2] == 1, b_ref[...], a_ref[...])
+
+    return call(
+        kernel, own, [(a, whole(a.shape)) for a in (first, second)],
+        [(jax.ShapeDtypeStruct(first.shape, bf16), whole(first.shape))], (1,),
+    )[0]
+
+
+def extra_rows(own, gain_sum, shift_sum, branch_sum, up_sum, qkv_sum, shards):
+    piece, ffp = gain_sum.shape[1] // shards, up_sum.shape[1] // shards
+    w = qkv_sum.shape[1] // (3 * shards)
+    shape = (16 * shards, COLS)
+
+    def kernel(own_ref, gain_ref, shift_ref, branch_ref, up_ref, qkv_ref, out_ref):
+        core = own_ref[1]
+        out_ref[...] = jnp.zeros_like(out_ref)
+        for s in range(shards):
+            row = 16 * s
+            at = slice(s * piece, (s + 1) * piece)
+            out_ref[row : row + 1, :piece] = gain_ref[:, at]
+            out_ref[row : row + 1, COLS // 2 : COLS // 2 + piece] = shift_ref[:, at]
+            out_ref[row + 1 : row + 2, :piece] = branch_ref[:, at]
+            out_ref[row + 2 : row + 3, :ffp] = up_ref[:, s * ffp : (s + 1) * ffp]
+            for t in range(3 * piece // w):
+                b = s * (3 * piece // w) + t
+                value = qkv_ref[:, (b // 2) * w : (b // 2 + 1) * w]
+                r, c = divmod(t * w, COLS)
+                out_ref[row + 3 + r : row + 4 + r, c : c + w] = jnp.where(core == b % 2, value, 0.0)
+
+    return call(
+        kernel, own, [(a, whole(a.shape)) for a in (gain_sum, shift_sum, branch_sum, up_sum, qkv_sum)],
+        [(jax.ShapeDtypeStruct(shape, f32), whole(shape))], (1,),
+    )[0]
 
 
 def pick(core, first, second):
@@ -930,10 +996,10 @@
         return self.send(value, lambda s, r: (s ^ bit, r))
 
     def next_chip(self, value):
-        return self.send(value, lambda s, r: (s, r + 2) if r + 2 < self.reps else None)
+        return self.send(value, lambda s, r: (s, (r + 2) % self.reps))
 
     def last_chip(self, value):
-        return self.send(value, lambda s, r: (s, r - 2) if r >= 2 else None)
+        return self.send(value, lambda s, r: (s, (r - 2) % self.reps))
 
     def chip_steps(self):
         chips = self.chips
@@ -990,16 +1056,22 @@
         net, bits = self.net, self.net.bits
         for bit, came in zip(bits, clock.tie(tuple(self.pieces[bit][0] for bit in bits))):
             self.pieces[bit] = [came]
-        got, parts = [], []
+        cuts, sources, outs = [], [], []
         for r, lo, hi in piece_ranges(self.group, net.shards):
-            if bin(r).count("1") <= 1:
+            if bin(r).count("1") == 2:
+                bit = last_bit(net.shards, r, 0 if lo == 0 else 1)
+                sources.append(self.pieces[r ^ bit][0])
+                outs.append((hi - lo, [(0, hi - lo, [(len(sources) - 1, lo)])]))
+        cuts = list(combine(net.own, sources, outs))
+        parts, got = list(cuts), []
+        for r, lo, hi in piece_ranges(self.group, net.shards):
+            count = bin(r).count("1")
+            if count <= 1:
                 got.append(self.pieces[r][0])
                 continue
             half = 0 if lo == 0 else 1
             bit = last_bit(net.shards, r, half)
-            source = self.pieces[r ^ bit]
-            part = source[half] if len(source) == 2 else source[0][lo:hi]
-            parts.append(part)
+            part = cuts.pop(0) if count == 2 else self.pieces[r ^ bit][half]
             self.pieces.setdefault(r, []).append(net.flip(part, bit))
             got.append(self.pieces[r][-1])
         clock.mark(tuple(parts))
@@ -1008,13 +1080,6 @@
     def arrived(self, clock):
         self.arrays = list(clock.tie(tuple(self.arrays)))
         clock.mark(tuple(self.arrays[-2:]))
-
-
-def sum_low(values):
-    total = values[0].astype(f32)
-    for v in values[1:]:
-        total = total + v.astype(f32)
-    return total.astype(bf16)
 
 
 class Reduce:
@@ -1035,34 +1100,49 @@
         held = dict(zip(rounds, arrays[1:]))
         came = {}
         for now in range(last + 1):
-            sent = {}
-            for (d, bit), keys in rounds.items():
-                if d != now:
-                    continue
-                value = held[d, bit]
-                if any(k in came for k in keys):
-                    parts, at = [], 0
-                    for r, h in keys:
-                        mine = value if len(keys) == 1 else value[at : at + size[h]]
-                        parts.append(sum_low([mine] + came.get((r, h), [])))
+            current = [key for key in rounds if key[0] == now]
+            if now:
+                given, outs = [held[key] for key in current], []
+                for i, key in enumerate(current):
+                    segments, at = [], 0
+                    for r, h in rounds[key]:
+                        terms = [(i, at)]
+                        for a, first in came.pop((r, h), []):
+                            terms.append((len(given), first))
+                            given.append(a)
+                        segments.append((at, size[h], terms))
                         at += size[h]
-                    value = parts[0] if len(parts) == 1 else jnp.concatenate(parts)
-                    clock.mark(value)
-                sent[d, bit] = net.flip(value, bit)
+                    outs.append((at, segments))
+                values = combine(net.own, given, outs)
+                clock.mark(tuple(values))
+                held.update(zip(current, values))
+            sent = {key: net.flip(held[key], key[1]) for key in current}
             yield "r0" if now == 0 else "r1" if now == last else None
-            sent = clock.tie(sent)
-            for key, value in sent.items():
+            for key, value in clock.tie(sent).items():
                 at = 0
                 for r, h in rounds[key]:
-                    part = value if len(rounds[key]) == 1 else value[at : at + size[h]]
-                    came.setdefault(goes[r, h], []).append(part)
+                    came.setdefault(goes[r, h], []).append((value, at))
                     at += size[h]
-        halves = [sum_low([own[lo:hi]] + came[0, h]) for h, (lo, hi) in enumerate(cuts)]
-        self.chains = {}
-        for name, value in zip("ab", halves) if apart else [("", jnp.concatenate(halves))]:
-            clock.mark(value)
-            self.chains[name] = ChipSum(net, clock, value)
+        given, segments = [own], []
+        for h, (lo, hi) in enumerate(cuts):
+            terms = [(0, lo)]
+            for a, first in came[0, h]:
+                terms.append((len(given), first))
+                given.append(a)
+            segments.append((lo, hi - lo, terms))
+        if apart:
+            outs = [(rows, [(0, rows, terms)]) for _, rows, terms in segments]
+        else:
+            outs = [(group.rows, segments)]
+        values = combine(net.own, given, outs)
+        clock.mark(tuple(values))
+        self.chains = {n: ChipSum(net, clock, v) for n, v in zip("ab" if apart else [""], values)}
         yield "r2"
+
+
+def add(own, a, b):
+    rows = a.shape[0]
+    return combine(own, [a, b], [(rows, [(0, rows, [(0, 0), (1, 0)])])])[0]
 
 
 class ChipSum:
@@ -1079,7 +1159,7 @@
             came = net.send(value, where)
             yield f"r{2 + i}" if i < 3 else None
             came = clock.tie(came)
-            value = sum_low([value, came]) if replaced is None else jnp.where(replaced, came, value)
+            value = add(net.own, value, came) if replaced is None else choose(net.own, value, came)
             clock.mark(value)
         theirs = net.other_core(value)
         yield "r5"
@@ -1088,14 +1168,15 @@
         yield "r6"
 
 
-ORDER = """
-g0a0 docs g1a0 g2a0 g0u0 f10 g1u0 h0 g2u0 g0o0 f20 f30 g1o0 g2o0 g0a1 f40 g1a1 g2a1
-g0u1 f11 g1u1 h1 g2u1 g0o1 f21 f31 g1o1 wo1 f41 g2o1 r0o1 bb1 ab1 p1 r1o1 out
-wu1 r0u1 r2o1 bn1 wa1 r1u1 nb1 r0a1 r3o1 r2u1 wo0 r1a1 bb0 r3u1 r4o1 r2a1 r0o0 ab0
-r4u1 r3a1 r5o1 r1o0 r6o1 p0 wu0 r5u1 r2o0 r6u1 r0u0 r4a1 bn0 r1u0 r3o0 nb0 r2u0 wa0
-r0a0 r4o0 r3u0 r1a0 r5a1 r2a0 r4u0 r3a0a r3a0b r4a0a r5o0 r6a1 r4a0b r5a0a r5u0 r6o0 r5a0b r6u0
-r6a0
-""".split()
+ORDER = (
+    "g0a0", "docs", "g1a0", "g2a0", "g0u0", "f10", "g1u0", "h0", "g2u0", "g0o0", "f20", "f30", "g1o0", "g2o0",
+    "g0a1", "f40", "g1a1", "g2a1", "g0u1", "f11", "g1u1", "h1", "g2u1", "g0o1", "f21", "f31", "g1o1", "wo1",
+    "f41", "g2o1", "r0o1", "bb1", "ab1", "p1", "r1o1", "out", "wu1", "r0u1", "r2o1", "bn1", "wa1", "r1u1",
+    "nb1", "r0a1", "r3o1", "r2u1", "wo0", "r1a1", "bb0", "r3u1", "r4o1", "r2a1", "r0o0", "ab0", "r4u1", "r3a1",
+    "r5o1", "r1o0", "r6o1", "p0", "wu0", "r5u1", "r2o0", "r6u1", "r0u0", "r4a1", "bn0", "r1u0", "r3o0", "nb0",
+    "r2u0", "wa0", "r0a0", "r4o0", "r3u0", "r1a0", "r5a1", "r2a0", "r4u0", "r3a0a", "r3a0b", "r4a0a", "r5o0", "r6a1",
+    "r4a0b", "r5a0a", "r5u0", "r6o0", "r5a0b", "r6u0", "r6a0",
+)
 
 
 def body(
@@ -1125,7 +1206,9 @@
     ff = up_weight.shape[2] // 2
     group_first = net.shard * row_count * net.reps
     chip_first = net.chip * rows
-    own = jnp.stack([net.shard, core]).astype(jnp.int32)
+    edge = (net.chip % 4 == 0) | (net.chip % 4 == 3)
+    own = jnp.stack([net.shard, core, edge.astype(jnp.int32)]).astype(jnp.int32)
+    net.own = own
     clock = Clock()
 
     ff_piece, head_piece = ff // shards, width // 2 // shards
@@ -1200,16 +1283,15 @@
             before, adds = at[l - 1]["stream"], at[l - 1]["adds"]
             biases = [common["vectors"][3], common["vectors"][5]]
         gains, shifts, qkv_b, _, _, _ = common["vectors"]
-        stream, unit, inv, normed, q, kv = forward_qkv(
-            own, l, clock.tie(before), adds, biases, gains, shifts, qkv_b, tables, a.arrays, a.group, shards
+        stream, unit, inv, normed, q, kv, tail = forward_qkv(
+            own, l, clock.tie(before), adds, biases, gains, shifts, qkv_b, tables, a.arrays, a.group, shards,
+            reach,
         )
         clock.mark(q)
-        at[l].update(stream=stream, unit=unit, inv=inv, normed=normed, q=q, kv=kv)
+        at[l].update(stream=stream, unit=unit, inv=inv, normed=normed, q=q, kv=kv, tail=tail)
 
     def send_halo(l):
-        part = clock.tie(at[l]["kv"])[rows - reach :]
-        clock.mark(part)
-        at[l]["halo"] = net.next_chip(part)
+        at[l]["halo"] = net.next_chip(clock.tie(at[l]["tail"]))
 
     def forward_second(l):
         at[l]["activated"], at[l]["slope"] = forward_up(
@@ -1252,24 +1334,10 @@
         reduce("u", l, group_u, [at[l]["normed"]], at[l]["pre_grad"])
 
     def grads_qkv(l):
-        qkv_sum = at[l]["qkv_sum"].reshape(3 * shards, 1, -1)
-        nothing = jnp.zeros_like(qkv_sum)
-        qkv_sum = jnp.concatenate([pick(core, qkv_sum, nothing), pick(core, nothing, qkv_sum)], axis=1)
-
-        def line(v, width):
-            v = v.reshape(shards, -1)
-            return jnp.pad(v, ((0, 0), (0, width - v.shape[1])))
-
-        extra = jnp.concatenate(
-            [
-                line(at[l]["gain_sum"], COLS // 2),
-                line(at[l]["shift_sum"], COLS // 2),
-                line(at[l]["branch_sum"], COLS),
-                line(at[l]["up_sum"], COLS),
-                line(qkv_sum, 13 * COLS),
-            ],
-            axis=1,
-        ).reshape(shards * 16, COLS)
+        d = at[l]
+        extra = extra_rows(
+            own, d["gain_sum"], d["shift_sum"], d["branch_sum"], d["up_sum"], d["qkv_sum"], shards
+        )
         reduce("a", l, grads_a, [at[l]["normed"]], at[l]["packed_grad"], extra)
 
     def backward_first(l):
@@ -1281,15 +1349,13 @@
 
     def backward_attention(l):
         d = at[l]
-        d["dq"], d["dkv"] = attend_back(
+        d["dq"], d["dkv"], d["far"] = attend_back(
             meta, clock.tie(d["q"]), d["kv"], d["halo"], start_row, d["attended_grad"], d["attended"], d["lse"], tables
         )
         clock.mark(d["dq"])
 
     def send_halo_back(l):
-        part = clock.tie(at[l]["dkv"])[:reach]
-        clock.mark(part)
-        at[l]["halo_grad"] = net.last_chip(part)
+        at[l]["halo_grad"] = net.last_chip(clock.tie(at[l]["far"]))
 
     def backward_norm_in(l):
         d = at[l]

time: 772 us -> 740 us (0.959)
  other arithmetic: 69.9 us -> 13.7 us
  Pallas kernels: 292 us -> 328 us
  local copies, waits for them, and re-layouts: 51.1 us -> 43.2 us
    convert_element_type x34 -> x0, other arithmetic: 42 us -> none  [sum_low(): return total.astype(bf16)]
    pallas_call x35 -> x76, Pallas kernels: 292 us -> 328 us  [call(): pl.pallas_call(kernel, grid_spec=pltpu.PrefetchScalarGridSpec(num_scalar_...]
    slice x16 -> x0, local copies, waits for them, and re-layouts: 12.4 us -> none  [the longest x12 6.3 us: far(): part = source[half] if len(source) == 2 else source[0][lo:hi]]
    unnamed x268 -> x246, local copies, waits for them, and re-layouts: 34.3 us -> 39.7 us
  transfers between devices with their start and end apart: 86 -> 86, of which waited for: 28 -> 41; matrix products, arithmetic and copies ran while one was open for 11% -> 2% of each run, Pallas kernels for 36% -> 38%
where the time goes in v3:
time: 740 us; the launch traced here: 731 us
  Pallas kernels  328 us (44%)
  waiting for transfers between devices  179 us (24%)
  starting transfers between devices  153 us (21%)
  local copies, waits for them, and re-layouts  43.2 us (6%)
  other arithmetic  13.7 us (2%)
  blocking collectives  11.8 us (2%)
    pallas_call x76, Pallas kernels, call(): pl.pallas_call(kernel, grid_spec=pltpu.PrefetchScalarGridSpec(num_scalar_...  328 us
    ppermute x86, waiting for transfers between devices, send(): return lax.ppermute(value, AXES, pairs)  179 us
    ppermute x86, starting transfers between devices, send(): return lax.ppermute(value, AXES, pairs)  153 us
    unnamed x246, local copies, waits for them, and re-layouts  39.7 us
  transfers between devices with their start and end apart: 86, of which 41 were waited for; matrix products, arithmetic and copies ran while one was open for 2% of the time, Pallas kernels for 38%

profile of v3, /device:TPU:1, one launch (start us, length us, event | category | flops | bytes accessed | tf_op | source)
XLA Modules:
  0.0 730.9 jit_solution(15092731640027377831)
XLA Ops:
  12.4 11.8 %all-gather.1 = s32[8,2,4]{2,1,0:T(2,128)S(1)} all-gather(s32[1,2,4]{2,1,0:T(2,128)S(1)} %add_bitcast_fusion), channel_id=2, replica_groups=mesh['shard'=4,'rep'=8] {'rep'}, dimensions={0}, use_global_device_ids=true | all-gather | bytes 288 | tf_op jit(solution)/shard_map/all_gather | solution.py:1246
  48.2 10.1 %shard_map.233 = (f32[1024,1024]{1,0:T(8,128)}, bf16[1024,1024]{1,0:T(8,128)(2,1)}, f32[1024,128]{1,0:T(8,128)S(1)}, bf16[1024,1024]{1,0:T(8,128)(2,1)}, bf16[10...) custom-call(s32[3]{0:T(128)S(1)} %pad_add_fusion.own_ref, ...), custom_call_target="tpu_custom_call" | custom-call | flops 1 | bytes 1 | tf_op jit(solution)/shard_map/pallas_call | solution.py:42
  85.2 15.8 %shard_map.238 = (bf16[1024,2048]{1,0:T(8,128)(2,1)}, bf16[1024,2048]{1,0:T(8,128)(2,1)}) custom-call(s32[3]{0:T(128)S(1)} %pad_add_fusion.own_ref, bf16[1024,1024]{1,0:T(8,128)(2,1)} %get-tuple-element.455.x_ref.refs_0_, f32[8,2048]{1,0:T(8,128)S(1)} %get-tuple-element.278.b_ref, bf16[1024,512]{1,0:T(8,128)(2,1)S(1)} %copy-done.18, ...), custom_call_target="tpu_custom_call" | custom-call | flops 1 | bytes 1 | tf_op jit(solution)/shard_map/pallas_call | solution.py:42
  101.1 11.6 %shard_map.239 = (bf16[1024,512]{1,0:T(8,128)(2,1)S(1)}, f32[8,1024]{1,0:T(8,128)S(1)}) custom-call(s32[4]{0:T(128)S(1)} %subtract_clamp_fusion.meta_ref, bf16[1024,512]{1,0:T(8,128)(2,1)S(1)} %copy-done.37, bf16[1024,1024]{1,0:T(8,128)(2,1)S(1)} %copy-done.23, bf16[512,1024]{1,0:T(8,128)(2,1)} %collective-permute-done.11.halo_ref, s32[1024,1]{1,0:T(8,128)S(1)} %copy-done.36), custom_call_target="tpu_custom_call" | custom-call | flops 1 | bytes 1 | tf_op jit(solution)/shard_map/pallas_call | solution.py:42
  126.8 11.4 %shard_map.241.refs_1_ = bf16[1024,1024]{1,0:T(8,128)(2,1)} custom-call(s32[3]{0:T(128)S(1)} %pad_add_fusion.own_ref, bf16[1024,512]{1,0:T(8,128)(2,1)S(1)} %get-tuple-element.296.att_ref.refs_1_.o_ref, bf16[1024,2048]{1,0:T(8,128)(2,1)} %get-tuple-element.395.act_ref.refs_0_, bf16[1280,512]{1,0:T(8,128)(2,1)} %shard_map.236.rest_0_, ...), custom_call_target="tpu_custom_call" | custom-call | flops 1 | bytes 1 | tf_op jit(solution)/shard_map/pallas_call | solution.py:42
  138.3 11.0 %collective-permute-start.18 = (bf16[1024,1024]{1,0:T(8,128)(2,1)}, bf16[1024,1024]{1,0:T(8,128)(2,1)}, u32[]{:S(2)}, u32[]{:S(2)}) collective-permute-start(bf16[1024,1024]{1,0:T(8,128)(2,1)} %shard_map.241.refs_1_), channel_id=1, source_target_pairs={{0,1},{1,0},{2,3},{3,2},{4,5},{5,4},{6,7},{7,6},{8,9},{9,8},{10,11... | collective-permute-start | bytes 6291464 | tf_op jit(solution)/shard_map/ppermute | solution.py:990
  163.2 12.1 %shard_map.243 = (f32[1024,1024]{1,0:T(8,128)}, bf16[1024,1024]{1,0:T(8,128)(2,1)}, f32[1024,128]{1,0:T(8,128)S(1)}, bf16[1024,1024]{1,0:T(8,128)(2,1)}, bf16[10...) custom-call(s32[3]{0:T(128)S(1)} %pad_add_fusion.own_ref, ...), custom_call_target="tpu_custom_call" | custom-call | flops 1 | bytes 1 | tf_op jit(solution)/shard_map/pallas_call | solution.py:42
  209.7 15.8 %shard_map.246 = (bf16[1024,2048]{1,0:T(8,128)(2,1)}, bf16[1024,2048]{1,0:T(8,128)(2,1)}) custom-call(s32[3]{0:T(128)S(1)} %pad_add_fusion.own_ref, bf16[1024,1024]{1,0:T(8,128)(2,1)} %get-tuple-element.376.x_ref.refs_0_, f32[8,2048]{1,0:T(8,128)S(1)} %get-tuple-element.278.b_ref, bf16[1024,512]{1,0:T(8,128)(2,1)S(1)} %shard_map.234.rest_0_.rest_5_, ...), custom_call_target="tpu_custom_call" | custom-call | flops 1 | bytes 1 | tf_op jit(solution)/shard_map/pallas_call | solution.py:42
  225.5 11.7 %shard_map.247 = (bf16[1024,512]{1,0:T(8,128)(2,1)S(1)}, f32[8,1024]{1,0:T(8,128)S(1)}) custom-call(s32[4]{0:T(128)S(1)} %subtract_clamp_fusion.meta_ref, bf16[1024,512]{1,0:T(8,128)(2,1)S(1)} %copy-done.39, bf16[1024,1024]{1,0:T(8,128)(2,1)S(1)} %copy-done.24, bf16[512,1024]{1,0:T(8,128)(2,1)} %collective-permute-done.25.halo_ref, s32[1024,1]{1,0:T(8,128)S(1)} %copy-done.36), custom_call_target="tpu_custom_call" | custom-call | flops 1 | bytes 1 | tf_op jit(solution)/shard_map/pallas_call | solution.py:42
  243.2 11.3 %shard_map.249 = (bf16[1280,512]{1,0:T(8,128)(2,1)S(1)}, bf16[1280,512]{1,0:T(8,128)(2,1)S(1)}, bf16[1280,512]{1,0:T(8,128)(2,1)}, bf16[640,512]{1,0:T(8,128)(2,1)S(1)}, bf16[640,512]{1,0:T(8,128)(2,1)S(1)}) custom-call(s32[3]{0:T(128)S(1)} %pad_add_fusion.own_ref, bf16[1024,2048]{1,0:T(8,128)(2,1)} %get-tuple-element.339.refs_0_.act_ref, ...), custom_call_target="tpu_custom_call" | custom-call | flops 1 | bytes 1 | tf_op jit(solution)/shard_map/pallas_call | solution.py:42
  254.5 10.9 %shard_map.250 = bf16[1024,1024]{1,0:T(8,128)(2,1)} custom-call(s32[3]{0:T(128)S(1)} %pad_add_fusion.own_ref, bf16[1024,512]{1,0:T(8,128)(2,1)S(1)} %get-tuple-element.346.refs_1_.att_ref.o_ref, bf16[1024,2048]{1,0:T(8,128)(2,1)} %get-tuple-element.339.refs_0_.act_ref, bf16[1280,512]{1,0:T(8,128)(2,1)S(1)} %shard_map.244.rest_0_, ...), custom_call_target="tpu_custom_call" | custom-call | flops 1 | bytes 1 | tf_op jit(solution)/shard_map/pallas_call | solution.py:42
  270.9 12.1 %shard_map.251 = (bf16[1024,2048]{1,0:T(8,128)(2,1)}, bf16[1024,512]{1,0:T(8,128)(2,1)S(1)}, f32[1,2048]{1,0:T(1,128)S(1)}, f32[1,1024]{1,0:T(1,128)S(1)}) custom-call(s32[3]{0:T(128)S(1)} %pad_add_fusion.own_ref, bf16[1024,1024]{1,0:T(8,128)(2,1)} %pad_maximum_fusion.1.refs_2_.g_ref, bf16[1024,2048]{1,0:T(8,128)(2,1)} %get-tuple-element.329.slope_ref, ...), custom_call_target="tpu_custom_call" | custom-call | flops 1 | bytes 1 | tf_op jit(solution)/shard_map/pallas_call | solution.py:42
  284.0 17.4 %shard_map.252 = (bf16[1024,512]{1,0:T(8,128)(2,1)S(1)}, bf16[1024,1024]{1,0:T(8,128)(2,1)}, bf16[512,1024]{1,0:T(8,128)(2,1)}) custom-call(s32[4]{0:T(128)S(1)} %subtract_clamp_fusion.meta_ref, bf16[1024,512]{1,0:T(8,128)(2,1)S(1)} %copy-done.40, bf16[1024,1024]{1,0:T(8,128)(2,1)} %get-tuple-element.331.kv_ref, ...), custom_call_target="tpu_custom_call" | custom-call | flops 1 | bytes 1 | tf_op jit(solution)/shard_map/pallas_call | solution.py:42
  315.9 9.7 %shard_map.254 = (bf16[1024,512]{1,0:T(8,128)(2,1)S(1)}, bf16[1024,512]{1,0:T(8,128)(2,1)}, bf16[1024,512]{1,0:T(8,128)(2,1)}, bf16[512,512]{1,0:T(8,128)(2,1)S(1)}, bf16[512,512]{1,0:T(8,128)(2,1)S(1)}) custom-call(s32[3]{0:T(128)S(1)} %pad_add_fusion.own_ref, bf16[1024,1024]{1,0:T(8,128)(2,1)} %get-tuple-element.376.x_ref.refs_0_, ...), custom_call_target="tpu_custom_call" | custom-call | flops 1 | bytes 1 | tf_op jit(solution)/shard_map/pallas_call | solution.py:42
  330.5 16.3 %shard_map.256 = (bf16[1024,1536]{1,0:T(8,128)(2,1)}, bf16[1024,1024]{1,0:T(8,128)(2,1)}, f32[1,1536]{1,0:T(1,128)S(1)}, f32[1,1024]{1,0:T(1,128)S(1)}, f32[1,1024]{1,0:T(1,128)S(1)}) custom-call(s32[3]{0:T(128)S(1)} %pad_add_fusion.own_ref, bf16[1024,512]{1,0:T(8,128)(2,1)} %copy-done.72, bf16[1024,1024]{1,0:T(8,128)(2,1)} %get-tuple-element.371.dkv_ref, ...), custom_call_target="tpu_custom_call" | custom-call | flops 1 | bytes 1 | tf_op jit(solution)/shard_map/pallas_call | solution.py:42
  361.4 11.9 %collective-permute-done.32.refs_3_ = bf16[1024,512]{1,0:T(8,128)(2,1)S(1)} collective-permute-done((bf16[1024,512]{1,0:T(8,128)(2,1)}, bf16[1024,512]{1,0:T(8,128)(2,1)S(1)}, u32[]{:S(2)}, u32[]{:S(2)}) %collective-permute-start.32) | collective-permute-done | bytes 1048608 | tf_op jit(solution)/shard_map/ppermute | solution.py:990
  395.0 11.3 %shard_map.263 = (bf16[1280,512]{1,0:T(8,128)(2,1)S(1)}, bf16[1280,512]{1,0:T(8,128)(2,1)S(1)}, bf16[1280,512]{1,0:T(8,128)(2,1)}, bf16[640,512]{1,0:T(8,128)(2,1)S(1)}, bf16[640,512]{1,0:T(8,128)(2,1)S(1)}) custom-call(s32[3]{0:T(128)S(1)} %pad_add_fusion.own_ref, bf16[1024,2048]{1,0:T(8,128)(2,1)} %get-tuple-element.395.act_ref.refs_0_, ...), custom_call_target="tpu_custom_call" | custom-call | flops 1 | bytes 1 | tf_op jit(solution)/shard_map/pallas_call | solution.py:42
  413.0 12.3 %shard_map.265 = (bf16[1024,2048]{1,0:T(8,128)(2,1)}, bf16[1024,512]{1,0:T(8,128)(2,1)S(1)}, f32[1,2048]{1,0:T(1,128)S(1)}, f32[1,1024]{1,0:T(1,128)S(1)}) custom-call(s32[3]{0:T(128)S(1)} %pad_add_fusion.own_ref, bf16[1024,1024]{1,0:T(8,128)(2,1)} %copy-done.25, bf16[1024,2048]{1,0:T(8,128)(2,1)} %get-tuple-element.282.slope_ref, ...), custom_call_target="tpu_custom_call" | custom-call | flops 1 | bytes 1 | tf_op jit(solution)/shard_map/pallas_call | solution.py:42
  445.0 17.4 %shard_map.269 = (bf16[1024,512]{1,0:T(8,128)(2,1)S(1)}, bf16[1024,1024]{1,0:T(8,128)(2,1)}, bf16[512,1024]{1,0:T(8,128)(2,1)}) custom-call(s32[4]{0:T(128)S(1)} %subtract_clamp_fusion.meta_ref, bf16[1024,512]{1,0:T(8,128)(2,1)S(1)} %copy-done.38, bf16[1024,1024]{1,0:T(8,128)(2,1)} %get-tuple-element.284.kv_ref, ...), custom_call_target="tpu_custom_call" | custom-call | flops 1 | bytes 1 | tf_op jit(solution)/shard_map/pallas_call | solution.py:42
  510.0 14.6 %collective-permute-done.52.refs_2_ = bf16[640,512]{1,0:T(8,128)(2,1)S(1)} collective-permute-done((bf16[640,512]{1,0:T(8,128)(2,1)S(1)}, bf16[640,512]{1,0:T(8,128)(2,1)S(1)}, u32[]{:S(2)}, u32[]{:S(2)}) %collective-permute-start.52) | collective-permute-done | bytes 655392 | tf_op jit(solution)/shard_map/ppermute | solution.py:990
  531.7 16.2 %shard_map.280 = (bf16[1024,1536]{1,0:T(8,128)(2,1)}, bf16[1024,1024]{1,0:T(8,128)(2,1)}, f32[1,1536]{1,0:T(1,128)S(1)}, f32[1,1024]{1,0:T(1,128)S(1)}, f32[1,1024]{1,0:T(1,128)S(1)}) custom-call(s32[3]{0:T(128)S(1)} %pad_add_fusion.own_ref, bf16[1024,512]{1,0:T(8,128)(2,1)} %copy-done.71, bf16[1024,1024]{1,0:T(8,128)(2,1)} %get-tuple-element.440.dkv_ref, ...), custom_call_target="tpu_custom_call" | custom-call | flops 1 | bytes 1 | tf_op jit(solution)/shard_map/pallas_call | solution.py:42
  551.3 17.9 %collective-permute-start.56 = (bf16[1280,512]{1,0:T(8,128)(2,1)S(1)}, bf16[1280,512]{1,0:T(8,128)(2,1)S(1)}, u32[]{:S(2)}, u32[]{:S(2)}) collective-permute-start(bf16[1280,512]{1,0:T(8,128)(2,1)S(1)} %shard_map.277.refs_0_), channel_id=1, source_target_pairs={{0,2},{1,3},{6,4},{7,5},{8,10},{9,11},{14,12},{15,13},{16,18},{17,... | collective-permute-start | bytes 3932168 | tf_op jit(solution)/shard_map/ppermute | solution.py:990
  577.3 19.3 %collective-permute-done.56.refs_1_ = bf16[1280,512]{1,0:T(8,128)(2,1)S(1)} collective-permute-done((bf16[1280,512]{1,0:T(8,128)(2,1)S(1)}, bf16[1280,512]{1,0:T(8,128)(2,1)S(1)}, u32[]{:S(2)}, u32[]{:S(2)}) %collective-permute-start.56) | collective-permute-done | bytes 1310752 | tf_op jit(solution)/shard_map/ppermute | solution.py:990
  685.7 17.7 %collective-permute-done.82.b_ref = bf16[384,512]{1,0:T(8,128)(2,1)S(1)} collective-permute-done((bf16[384,512]{1,0:T(8,128)(2,1)S(1)}, bf16[384,512]{1,0:T(8,128)(2,1)S(1)}, u32[]{:S(2)}, u32[]{:S(2)}) %collective-permute-start.82) | collective-permute-done | bytes 393248 | tf_op jit(solution)/shard_map/ppermute | solution.py:990
  (515 shorter events, 400.4 us)
Async XLA Ops:
  10.8 33.3 %collective-permute-start = (bf16[512,1024]{1,0:T(8,128)(2,1)}, bf16[512,1024]{1,0:T(8,128)(2,1)}, u32[]{:S(2)}, u32[]{:S(2)}) collective-permute-start(bf16[512,1024]{1,0:T(8,128)(2,1)} %param.14), channel_id=1, source_target_pairs={{0,1},{1,0},{2,3},{3,2},{4,5},{5,4},{6,7},{7,6},{8,9},{9,8},{10,11... | collective-permute-start | bytes 3145736 | tf_op jit(solution)/shard_map/ppermute | solution.py:990
  75.3 37.5 %collective-permute-start.10 = (bf16[1280,512]{1,0:T(8,128)(2,1)}, bf16[1280,512]{1,0:T(8,128)(2,1)}, u32[]{:S(2)}, u32[]{:S(2)}) collective-permute-start(bf16[1280,512]{1,0:T(8,128)(2,1)} %shard_map.236.rest_0_), channel_id=1, source_target_pairs={{0,16},{1,17},{2,18},{3,19},{4,20},{5,21},{6,22},{7,23},{8,24},{9,... | collective-permute-start | bytes 3932168 | tf_op jit(solution)/shard_map/ppermute | solution.py:990
  76.4 36.4 %collective-permute-start.9 = (bf16[1280,512]{1,0:T(8,128)(2,1)}, bf16[1280,512]{1,0:T(8,128)(2,1)}, u32[]{:S(2)}, u32[]{:S(2)}) collective-permute-start(bf16[1280,512]{1,0:T(8,128)(2,1)} %shard_map.236.rest_0_), channel_id=1, source_target_pairs={{0,8},{1,9},{2,10},{3,11},{4,12},{5,13},{6,14},{7,15},{8,0},{9,1},... | collective-permute-start | bytes 3932168 | tf_op jit(solution)/shard_map/ppermute | solution.py:990
  198.3 39.0 %collective-permute-start.24 = (bf16[1280,512]{1,0:T(8,128)(2,1)S(1)}, bf16[1280,512]{1,0:T(8,128)(2,1)S(1)}, u32[]{:S(2)}, u32[]{:S(2)}) collective-permute-start(bf16[1280,512]{1,0:T(8,128)(2,1)S(1)} %shard_map.244.rest_0_), channel_id=1, source_target_pairs={{0,16},{1,17},{2,18},{3,19},{4,20},{5,21},{6,22},{7,23},{8,24},{9,... | collective-permute-start | bytes 3932168 | tf_op jit(solution)/shard_map/ppermute | solution.py:990
  199.2 38.1 %collective-permute-start.23 = (bf16[1280,512]{1,0:T(8,128)(2,1)S(1)}, bf16[1280,512]{1,0:T(8,128)(2,1)S(1)}, u32[]{:S(2)}, u32[]{:S(2)}) collective-permute-start(bf16[1280,512]{1,0:T(8,128)(2,1)S(1)} %shard_map.244.rest_0_), channel_id=1, source_target_pairs={{0,8},{1,9},{2,10},{3,11},{4,12},{5,13},{6,14},{7,15},{8,0},{9,1},... | collective-permute-start | bytes 3932168 | tf_op jit(solution)/shard_map/ppermute | solution.py:990
  203.5 36.5 %collective-permute-start.26 = (bf16[512,1024]{1,0:T(8,128)(2,1)}, bf16[512,1024]{1,0:T(8,128)(2,1)}, u32[]{:S(2)}, u32[]{:S(2)}) collective-permute-start(bf16[512,1024]{1,0:T(8,128)(2,1)} %param.17), channel_id=1, source_target_pairs={{0,1},{1,0},{2,3},{3,2},{4,5},{5,4},{6,7},{7,6},{8,9},{9,8},{10,11... | collective-permute-start | bytes 3145736 | tf_op jit(solution)/shard_map/ppermute | solution.py:990
  265.5 46.8 %collective-permute-start.31 = (bf16[1024,1024]{1,0:T(8,128)(2,1)}, bf16[1024,1024]{1,0:T(8,128)(2,1)}, u32[]{:S(2)}, u32[]{:S(2)}) collective-permute-start(bf16[1024,1024]{1,0:T(8,128)(2,1)} %shard_map.250), channel_id=1, source_target_pairs={{0,1},{1,0},{2,3},{3,2},{4,5},{5,4},{6,7},{7,6},{8,9},{9,8},{10,11... | collective-permute-start | bytes 6291464 | tf_op jit(solution)/shard_map/ppermute | solution.py:990
  269.3 38.9 %collective-permute-start.27 = (bf16[1280,512]{1,0:T(8,128)(2,1)}, bf16[1280,512]{1,0:T(8,128)(2,1)S(1)}, u32[]{:S(2)}, u32[]{:S(2)}) collective-permute-start(bf16[1280,512]{1,0:T(8,128)(2,1)} %get-tuple-element.343), channel_id=1, source_target_pairs={{0,8},{1,9},{2,10},{3,11},{4,12},{5,13},{6,14},{7,15},{8,0},{9,1},... | collective-permute-start | bytes 3932168 | tf_op jit(solution)/shard_map/ppermute | solution.py:990
  269.9 38.3 %collective-permute-start.28 = (bf16[1280,512]{1,0:T(8,128)(2,1)S(1)}, bf16[1280,512]{1,0:T(8,128)(2,1)S(1)}, u32[]{:S(2)}, u32[]{:S(2)}) collective-permute-start(bf16[1280,512]{1,0:T(8,128)(2,1)S(1)} %get-tuple-element.344), channel_id=1, source_target_pairs={{0,16},{1,17},{2,18},{3,19},{4,20},{5,21},{6,22},{7,23},{8,24},{9,... | collective-permute-start | bytes 3932168 | tf_op jit(solution)/shard_map/ppermute | solution.py:990
  346.8 30.5 %collective-permute-start.37 = (bf16[1024,1024]{1,0:T(8,128)(2,1)}, bf16[1024,1024]{1,0:T(8,128)(2,1)}, u32[]{:S(2)}, u32[]{:S(2)}) collective-permute-start(bf16[1024,1024]{1,0:T(8,128)(2,1)} %get-tuple-element.375.p0_ref), channel_id=1, source_target_pairs={{0,1},{1,0},{2,3},{3,2},{4,5},{5,4},{6,7},{7,6},{8,9},{9,8},{10,11... | collective-permute-start | bytes 6291464 | tf_op jit(solution)/shard_map/ppermute | solution.py:990
  350.7 35.0 %collective-permute-start.40 = (bf16[1280,512]{1,0:T(8,128)(2,1)S(1)}, bf16[1280,512]{1,0:T(8,128)(2,1)S(1)}, u32[]{:S(2)}, u32[]{:S(2)}) collective-permute-start(bf16[1280,512]{1,0:T(8,128)(2,1)S(1)} %shard_map.255.refs_0_), channel_id=1, source_target_pairs={{0,2},{1,3},{6,4},{7,5},{8,10},{9,11},{14,12},{15,13},{16,18},{17,... | collective-permute-start | bytes 3932168 | tf_op jit(solution)/shard_map/ppermute | solution.py:990
  386.5 39.6 %collective-permute-start.43 = (bf16[1280,512]{1,0:T(8,128)(2,1)S(1)}, bf16[1280,512]{1,0:T(8,128)(2,1)}, u32[]{:S(2)}, u32[]{:S(2)}) collective-permute-start(bf16[1280,512]{1,0:T(8,128)(2,1)S(1)} %shard_map.261.refs_0_), channel_id=1, source_target_pairs={{2,4},{3,5},{4,2},{5,3},{10,12},{11,13},{12,10},{13,11},{18,20},{1... | collective-permute-start | bytes 3932168 | tf_op jit(solution)/shard_map/ppermute | solution.py:990
  389.6 35.7 %collective-permute-start.44 = (bf16[1024,512]{1,0:T(8,128)(2,1)S(1)}, bf16[1024,512]{1,0:T(8,128)(2,1)S(1)}, u32[]{:S(2)}, u32[]{:S(2)}) collective-permute-start(bf16[1024,512]{1,0:T(8,128)(2,1)S(1)} %shard_map.262.refs_0_), channel_id=1, source_target_pairs={{0,2},{1,3},{6,4},{7,5},{8,10},{9,11},{14,12},{15,13},{16,18},{17,... | collective-permute-start | bytes 3145736 | tf_op jit(solution)/shard_map/ppermute | solution.py:990
  428.3 37.8 %collective-permute-start.47 = (bf16[1280,512]{1,0:T(8,128)(2,1)S(1)}, bf16[1280,512]{1,0:T(8,128)(2,1)}, u32[]{:S(2)}, u32[]{:S(2)}) collective-permute-start(bf16[1280,512]{1,0:T(8,128)(2,1)S(1)} %shard_map.267.a_ref), channel_id=1, source_target_pairs={{2,0},{3,1},{4,6},{5,7},{10,8},{11,9},{12,14},{13,15},{18,16},{19,... | collective-permute-start | bytes 3932168 | tf_op jit(solution)/shard_map/ppermute | solution.py:990
  431.0 31.4 %collective-permute-start.51 = (bf16[1024,512]{1,0:T(8,128)(2,1)S(1)}, bf16[1024,512]{1,0:T(8,128)(2,1)S(1)}, u32[]{:S(2)}, u32[]{:S(2)}) collective-permute-start(bf16[1024,512]{1,0:T(8,128)(2,1)S(1)} %shard_map.266.refs_0_), channel_id=1, source_target_pairs={{2,4},{3,5},{4,2},{5,3},{10,12},{11,13},{12,10},{13,11},{18,20},{1... | collective-permute-start | bytes 3145736 | tf_op jit(solution)/shard_map/ppermute | solution.py:990
  443.7 31.6 %collective-permute-start.41 = (bf16[1280,512]{1,0:T(8,128)(2,1)}, bf16[1280,512]{1,0:T(8,128)(2,1)S(1)}, u32[]{:S(2)}, u32[]{:S(2)}) collective-permute-start(bf16[1280,512]{1,0:T(8,128)(2,1)} %get-tuple-element.397), channel_id=1, source_target_pairs={{0,8},{1,9},{2,10},{3,11},{4,12},{5,13},{6,14},{7,15},{8,0},{9,1},... | collective-permute-start | bytes 3932168 | tf_op jit(solution)/shard_map/ppermute | solution.py:990
  444.0 31.3 %collective-permute-start.42 = (bf16[1280,512]{1,0:T(8,128)(2,1)}, bf16[1280,512]{1,0:T(8,128)(2,1)S(1)}, u32[]{:S(2)}, u32[]{:S(2)}) collective-permute-start(bf16[1280,512]{1,0:T(8,128)(2,1)} %copy-done.109), channel_id=1, source_target_pairs={{0,16},{1,17},{2,18},{3,19},{4,20},{5,21},{6,22},{7,23},{8,24},{9,... | collective-permute-start | bytes 3932168 | tf_op jit(solution)/shard_map/ppermute | solution.py:990
  547.9 50.5 %collective-permute-start.62 = (bf16[1024,1024]{1,0:T(8,128)(2,1)}, bf16[1024,1024]{1,0:T(8,128)(2,1)S(1)}, u32[]{:S(2)}, u32[]{:S(2)}) collective-permute-start(bf16[1024,1024]{1,0:T(8,128)(2,1)} %get-tuple-element.444.p0_ref), channel_id=1, source_target_pairs={{0,1},{1,0},{2,3},{3,2},{4,5},{5,4},{6,7},{7,6},{8,9},{9,8},{10,11... | collective-permute-start | bytes 6291464 | tf_op jit(solution)/shard_map/ppermute | solution.py:990
  551.3 45.3 %collective-permute-start.56 = (bf16[1280,512]{1,0:T(8,128)(2,1)S(1)}, bf16[1280,512]{1,0:T(8,128)(2,1)S(1)}, u32[]{:S(2)}, u32[]{:S(2)}) collective-permute-start(bf16[1280,512]{1,0:T(8,128)(2,1)S(1)} %shard_map.277.refs_0_), channel_id=1, source_target_pairs={{0,2},{1,3},{6,4},{7,5},{8,10},{9,11},{14,12},{15,13},{16,18},{17,... | collective-permute-start | bytes 3932168 | tf_op jit(solution)/shard_map/ppermute | solution.py:990
  575.7 31.4 %collective-permute-start.63 = (bf16[512,512]{1,0:T(8,128)(2,1)S(1)}, bf16[512,512]{1,0:T(8,128)(2,1)S(1)}, u32[]{:S(2)}, u32[]{:S(2)}) collective-permute-start(bf16[512,512]{1,0:T(8,128)(2,1)S(1)} %get-tuple-element.447), channel_id=1, source_target_pairs={{0,8},{1,9},{2,10},{3,11},{4,12},{5,13},{6,14},{7,15},{8,0},{9,1},... | collective-permute-start | bytes 1572872 | tf_op jit(solution)/shard_map/ppermute | solution.py:990
  576.1 31.0 %collective-permute-start.64 = (bf16[512,512]{1,0:T(8,128)(2,1)S(1)}, bf16[512,512]{1,0:T(8,128)(2,1)S(1)}, u32[]{:S(2)}, u32[]{:S(2)}) collective-permute-start(bf16[512,512]{1,0:T(8,128)(2,1)S(1)} %get-tuple-element.448), channel_id=1, source_target_pairs={{0,16},{1,17},{2,18},{3,19},{4,20},{5,21},{6,22},{7,23},{8,24},{9,... | collective-permute-start | bytes 1572872 | tf_op jit(solution)/shard_map/ppermute | solution.py:990
  638.2 34.3 %collective-permute-start.77 = (bf16[1280,512]{1,0:T(8,128)(2,1)S(1)}, bf16[1280,512]{1,0:T(8,128)(2,1)S(1)}, u32[]{:S(2)}, u32[]{:S(2)}) collective-permute-start(bf16[1280,512]{1,0:T(8,128)(2,1)S(1)} %shard_map.287.a_ref), channel_id=1, source_target_pairs={{2,0},{3,1},{4,6},{5,7},{10,8},{11,9},{12,14},{13,15},{18,16},{19,... | collective-permute-start | bytes 3932168 | tf_op jit(solution)/shard_map/ppermute | solution.py:990
  661.1 42.9 %collective-permute-start.81 = (bf16[1024,512]{1,0:T(8,128)(2,1)S(1)}, bf16[1024,512]{1,0:T(8,128)(2,1)S(1)}, u32[]{:S(2)}, u32[]{:S(2)}) collective-permute-start(bf16[1024,512]{1,0:T(8,128)(2,1)S(1)} %shard_map.292.a_ref), channel_id=1, source_target_pairs={{2,0},{3,1},{4,6},{5,7},{10,8},{11,9},{12,14},{13,15},{18,16},{19,... | collective-permute-start | bytes 3145736 | tf_op jit(solution)/shard_map/ppermute | solution.py:990
  673.2 36.9 %collective-permute-start.80 = (bf16[1280,512]{1,0:T(8,128)(2,1)S(1)}, bf16[1280,512]{1,0:T(8,128)(2,1)S(1)}, u32[]{:S(2)}, u32[]{:S(2)}) collective-permute-start(bf16[1280,512]{1,0:T(8,128)(2,1)S(1)} %shard_map.296.refs_0_), channel_id=1, source_target_pairs={{0,1},{1,0},{2,3},{3,2},{4,5},{5,4},{6,7},{7,6},{8,9},{9,8},{10,11... | collective-permute-start | bytes 3932168 | tf_op jit(solution)/shard_map/ppermute | solution.py:990
  (184 other events, 2104.3 us)

commit v4 on v3

--- a/solution.py
+++ b/solution.py
@@ -1,4 +1,5 @@
 import math
+from types import SimpleNamespace
 
 import jax
 import jax.numpy as jnp
@@ -36,6 +37,9 @@
 
 
 ANY = pl.BlockSpec(memory_space=pl.ANY)
+
+
+HINT = {"flops": 1}
 
 
 def call(kernel, scalars, inputs, outputs, grid, scratch=(), aliases={}, flops=0, bytes_=0):
@@ -51,7 +55,7 @@
         out_shape=[o for o, _ in outputs],
         input_output_aliases=aliases,
         compiler_params=pltpu.CompilerParams(vmem_limit_bytes=VMEM_BYTES),
-        cost_estimate=pl.CostEstimate(flops=1, bytes_accessed=1, transcendentals=0),
+        cost_estimate=pl.CostEstimate(flops=HINT["flops"], bytes_accessed=1, transcendentals=0),
     )(scalars, *[a for a, _ in inputs])
 
 
@@ -1168,14 +1172,15 @@
         yield "r6"
 
 
+COSTS = {"ab1": 200 * 10**8, "bb1": 400 * 10**8, "f21": 100 * 10**8, "f30": 200 * 10**8, "f31": 60 * 10**8, "wa1": 10 * 10**8}
 ORDER = (
     "g0a0", "docs", "g1a0", "g2a0", "g0u0", "f10", "g1u0", "h0", "g2u0", "g0o0", "f20", "f30", "g1o0", "g2o0",
     "g0a1", "f40", "g1a1", "g2a1", "g0u1", "f11", "g1u1", "h1", "g2u1", "g0o1", "f21", "f31", "g1o1", "wo1",
-    "f41", "g2o1", "r0o1", "bb1", "ab1", "p1", "r1o1", "out", "wu1", "r0u1", "r2o1", "bn1", "wa1", "r1u1",
-    "nb1", "r0a1", "r3o1", "r2u1", "wo0", "r1a1", "bb0", "r3u1", "r4o1", "r2a1", "r0o0", "ab0", "r4u1", "r3a1",
-    "r5o1", "r1o0", "r6o1", "p0", "wu0", "r5u1", "r2o0", "r6u1", "r0u0", "r4a1", "bn0", "r1u0", "r3o0", "nb0",
-    "r2u0", "wa0", "r0a0", "r4o0", "r3u0", "r1a0", "r5a1", "r2a0", "r4u0", "r3a0a", "r3a0b", "r4a0a", "r5o0", "r6a1",
-    "r4a0b", "r5a0a", "r5u0", "r6o0", "r5a0b", "r6u0", "r6a0",
+    "f41", "g2o1", "r0o1", "bb1", "ab1", "p1", "r1o1", "out", "wu1", "r0u1", "r2o1", "q1", "bn1", "wa1",
+    "r1u1", "nb1", "r0a1", "r3o1", "r2u1", "wo0", "r1a1", "bb0", "r2a1", "r3u1", "r4o1", "r0o0", "ab0", "r4u1",
+    "p0", "r3a1", "r5o1", "r1o0", "wu0", "r5u1", "r2o0", "q0", "bn0", "r0u0", "r1u0", "r6o1", "r2u0", "wa0",
+    "r0a0", "r3o0", "r4a1", "nb0", "r4o0", "r3u0", "r1a0", "r5a1", "r2a0", "r4u0", "r3a0a", "r3a0b", "r4a0a", "r5o0",
+    "r6u1", "r6a1", "r4a0b", "r5a0a", "r5u0", "r6o0", "r5a0b", "r6u0", "r6a0",
 )
 
 
@@ -1267,60 +1272,61 @@
     stream0 = pair_rows(tokens)
     branch_top = pair_rows(cotangent)
     top = layers - 1
-    at = [dict() for _ in range(layers)]
+    at = [SimpleNamespace() for _ in range(layers)]
     sums = {}
-    common = {}
+    common = SimpleNamespace(smalls={}, made={})
 
     def forward_first(l):
         a = gathers[3 * l]
         if l == 0:
-            common["vectors"] = whole_vectors(
+            common.vectors = whole_vectors(
                 own, a.arrays, group_a0, 3 * piece, {n: v.shape for n, v in small.items()}, shards,
                 {"gain": 0, "shift": 0, "qkv": 3, "out": 0, "up": 1, "down": 0},
             )
             before, adds, biases = stream0, [], []
         else:
-            before, adds = at[l - 1]["stream"], at[l - 1]["adds"]
-            biases = [common["vectors"][3], common["vectors"][5]]
-        gains, shifts, qkv_b, _, _, _ = common["vectors"]
+            before, adds = at[l - 1].stream, at[l - 1].adds
+            biases = [common.vectors[3], common.vectors[5]]
+        gains, shifts, qkv_b, _, _, _ = common.vectors
         stream, unit, inv, normed, q, kv, tail = forward_qkv(
             own, l, clock.tie(before), adds, biases, gains, shifts, qkv_b, tables, a.arrays, a.group, shards,
             reach,
         )
         clock.mark(q)
-        at[l].update(stream=stream, unit=unit, inv=inv, normed=normed, q=q, kv=kv, tail=tail)
+        s = at[l]
+        s.stream, s.unit, s.inv, s.normed, s.q, s.kv, s.tail = stream, unit, inv, normed, q, kv, tail
 
     def send_halo(l):
-        at[l]["halo"] = net.next_chip(clock.tie(at[l]["tail"]))
+        at[l].halo = net.next_chip(clock.tie(at[l].tail))
 
     def forward_second(l):
-        at[l]["activated"], at[l]["slope"] = forward_up(
-            own, l, clock.tie(at[l]["normed"]), common["vectors"][4], gathers[3 * l + 1].arrays, group_u, shards
+        at[l].activated, at[l].slope = forward_up(
+            own, l, clock.tie(at[l].normed), common.vectors[4], gathers[3 * l + 1].arrays, group_u, shards
         )
-        clock.mark(at[l]["slope"])
+        clock.mark(at[l].slope)
 
     def forward_third(l):
-        at[l]["attended"], at[l]["lse"] = attend(
-            meta, clock.tie(at[l]["q"]), at[l]["kv"], at[l]["halo"], start_column
+        at[l].attended, at[l].lse = attend(
+            meta, clock.tie(at[l].q), at[l].kv, at[l].halo, start_column
         )
-        clock.mark(at[l]["lse"])
+        clock.mark(at[l].lse)
 
     def forward_fourth(l):
         partial = forward_out(
-            own, clock.tie(at[l]["attended"]), at[l]["activated"], gathers[3 * l + 2].arrays, group_o, shards
+            own, clock.tie(at[l].attended), at[l].activated, gathers[3 * l + 2].arrays, group_o, shards
         )
         clock.mark(partial)
-        at[l]["adds"] = [partial, net.other_core(partial)]
+        at[l].adds = [partial, net.other_core(partial)]
 
     def branch_of(l):
-        return branch_top if l == top else at[l + 1]["branch"]
+        return branch_top if l == top else at[l + 1].branch
 
     def output():
-        adds = at[top]["adds"]
-        value = own_rows(clock.tie(at[top]["stream"])) + own_rows(adds[0]).astype(f32) + own_rows(adds[1]).astype(f32)
-        out_b, down_b = common["vectors"][3], common["vectors"][5]
-        common["output"] = (value + out_b[top : top + 1] + down_b[top : top + 1]).astype(bf16)
-        clock.mark(common["output"])
+        adds = at[top].adds
+        value = own_rows(clock.tie(at[top].stream)) + own_rows(adds[0]).astype(f32) + own_rows(adds[1]).astype(f32)
+        out_b, down_b = common.vectors[3], common.vectors[5]
+        common.output = (value + out_b[top : top + 1] + down_b[top : top + 1]).astype(bf16)
+        clock.mark(common.output)
 
     def reduce(name, l, group, lefts, rights, extra=None):
         got = weight_grads(own, [clock.tie(lefts[0])] + lefts[1:], rights, extra, group, shards)
@@ -1328,52 +1334,57 @@
         sums[name, l] = Reduce(net, clock, group, got, name == "a" and l == 0)
 
     def grads_out(l):
-        reduce("o", l, group_o, [at[l]["activated"], at[l]["attended"]], branch_of(l))
+        reduce("o", l, group_o, [at[l].activated, at[l].attended], branch_of(l))
 
     def grads_up(l):
-        reduce("u", l, group_u, [at[l]["normed"]], at[l]["pre_grad"])
+        reduce("u", l, group_u, [at[l].normed], at[l].pre_grad)
 
     def grads_qkv(l):
         d = at[l]
         extra = extra_rows(
-            own, d["gain_sum"], d["shift_sum"], d["branch_sum"], d["up_sum"], d["qkv_sum"], shards
+            own, d.gain_sum, d.shift_sum, d.branch_sum, d.up_sum, d.qkv_sum, shards
         )
-        reduce("a", l, grads_a, [at[l]["normed"]], at[l]["packed_grad"], extra)
+        reduce("a", l, grads_a, [at[l].normed], at[l].packed_grad, extra)
 
     def backward_first(l):
         pre_grad, attended_grad, up_sum, branch_sum = backward_branch(
-            own, clock.tie(branch_of(l)), at[l]["slope"], gathers[3 * l + 2].arrays, group_o, shards
+            own, clock.tie(branch_of(l)), at[l].slope, gathers[3 * l + 2].arrays, group_o, shards
         )
         clock.mark(attended_grad)
-        at[l].update(pre_grad=pre_grad, attended_grad=attended_grad, up_sum=up_sum, branch_sum=branch_sum)
+        s = at[l]
+        s.pre_grad, s.attended_grad, s.up_sum, s.branch_sum = pre_grad, attended_grad, up_sum, branch_sum
 
     def backward_attention(l):
         d = at[l]
-        d["dq"], d["dkv"], d["far"] = attend_back(
-            meta, clock.tie(d["q"]), d["kv"], d["halo"], start_row, d["attended_grad"], d["attended"], d["lse"], tables
+        d.dq, d.dkv, d.far = attend_back(
+            meta, clock.tie(d.q), d.kv, d.halo, start_row, d.attended_grad, d.attended, d.lse, tables
         )
-        clock.mark(d["dq"])
+        clock.mark(d.dq)
 
     def send_halo_back(l):
-        at[l]["halo_grad"] = net.last_chip(clock.tie(at[l]["far"]))
+        at[l].halo_grad = net.last_chip(clock.tie(at[l].far))
+
+    def halo_back_came(l):
+        at[l].halo_grad = clock.tie(at[l].halo_grad)
+        clock.mark(at[l].halo_grad)
 
     def backward_norm_in(l):
         d = at[l]
         a = gathers[3 * l]
-        d["packed_grad"], part, d["qkv_sum"], d["gain_sum"], d["shift_sum"] = backward_normed(
-            own, clock.tie(d["dq"]), d["dkv"], d["halo_grad"], d["pre_grad"], d["unit"], tables,
+        d.packed_grad, part, d.qkv_sum, d.gain_sum, d.shift_sum = backward_normed(
+            own, clock.tie(d.dq), d.dkv, d.halo_grad, d.pre_grad, d.unit, tables,
             a.arrays, gathers[3 * l + 1].arrays, a.group, group_u, shards,
         )
         clock.mark(part)
-        d["parts"] = [part, net.other_core(part)]
+        d.parts = [part, net.other_core(part)]
 
     def backward_norm(l):
         d = at[l]
-        grad = branch_top if l == top else at[l + 1]["grad"]
-        d["grad"], d["branch"] = norm_backward(
-            own, l, clock.tie(grad), d["parts"], d["unit"], d["inv"], common["vectors"][0]
+        grad = branch_top if l == top else at[l + 1].grad
+        d.grad, d.branch = norm_backward(
+            own, l, clock.tie(grad), d.parts, d.unit, d.inv, common.vectors[0]
         )
-        clock.mark(d["branch"])
+        clock.mark(d.branch)
 
     def finish(name, l):
         chains = [c for _, c in sorted(sums[name, l].chains.items())]
@@ -1381,22 +1392,23 @@
             c.step("r6")
         mine, theirs = [c.mine for c in chains], [c.theirs for c in chains]
         if name == "o":
-            got = unpack_rows(own, mine, theirs, common.get(name), l, layers, (ff_piece, head_piece), width)
+            got = unpack_rows(own, mine, theirs, common.made.get(name), l, layers, (ff_piece, head_piece), width)
         else:
             kinds, w = (3, head_piece) if name == "a" else (1, ff_piece)
-            got = unpack_columns(own, mine, theirs, common.get(name), l, layers, piece, kinds, w, shards)
-        common[name] = got
+            got = unpack_columns(own, mine, theirs, common.made.get(name), l, layers, piece, kinds, w, shards)
+        common.made[name] = got
         clock.mark(got)
         if name == "a":
-            common["small", l] = mine[-1][-16:], theirs[-1][-16:]
+            common.smalls[l] = mine[-1][-16:], theirs[-1][-16:]
 
     kernels = {
         "f1": forward_first, "f2": forward_second, "f3": forward_third, "f4": forward_fourth, "h": send_halo,
         "wo": grads_out, "wu": grads_up, "wa": grads_qkv, "bb": backward_first, "ab": backward_attention,
-        "p": send_halo_back, "bn": backward_norm_in, "nb": backward_norm,
+        "p": send_halo_back, "q": halo_back_came, "bn": backward_norm_in, "nb": backward_norm,
     }
     others = {"docs": lambda: clock.mark(docs), "out": output}
     for token in ORDER:
+        HINT["flops"] = COSTS.get(token, 1)
         if token in others:
             others[token]()
         elif token[:-1] in kernels:
@@ -1416,10 +1428,10 @@
                 sums[name, l].step(stage)
             else:
                 sums[name, l].chains[token[4:]].step(stage)
-    block_output, input_grad = common["output"], own_rows(at[0]["branch"])
-    (down_g, out_g), up_g, qkv_g = common["o"], common["u"], common["a"]
+    block_output, input_grad = common.output, own_rows(at[0].branch)
+    (down_g, out_g), up_g, qkv_g = (common.made[n] for n in "oua")
     mine, theirs = (
-        jnp.stack([common["small", l][i] for l in range(layers)]).astype(f32) for i in range(2)
+        jnp.stack([common.smalls[l][i] for l in range(layers)]).astype(f32) for i in range(2)
     )
     low, high = pick(core, mine, theirs), pick(core, theirs, mine)
     both = low + high

time: 740 us -> 686 us (0.927)
  waiting for transfers between devices: 179 us -> 113 us
  starting transfers between devices: 153 us -> 163 us
    ppermute x86, waiting for transfers between devices: 179 us -> 113 us  [send(): return lax.ppermute(value, AXES, pairs)]
    ppermute x86, starting transfers between devices: 153 us -> 163 us  [send(): return lax.ppermute(value, AXES, pairs)]
    unnamed x246 -> x234, local copies, waits for them, and re-layouts: 39.7 us -> 41.4 us
  transfers between devices with their start and end apart: 86 -> 86, of which waited for: 41 -> 28; matrix products, arithmetic and copies ran while one was open for 2% -> 2% of each run, Pallas kernels for 38% -> 45%
where the time goes in v4:
time: 686 us; the launch traced here: 679 us
  Pallas kernels  330 us (48%)
  starting transfers between devices  163 us (24%)
  waiting for transfers between devices  113 us (16%)
  local copies, waits for them, and re-layouts  44.9 us (7%)
  other arithmetic  13.5 us (2%)
  blocking collectives  11.8 us (2%)
    pallas_call x76, Pallas kernels, call(): pl.pallas_call(kernel, grid_spec=pltpu.PrefetchScalarGridSpec(num_scalar_...  330 us
    ppermute x86, starting transfers between devices, send(): return lax.ppermute(value, AXES, pairs)  163 us
    ppermute x86, waiting for transfers between devices, send(): return lax.ppermute(value, AXES, pairs)  113 us
    unnamed x234, local copies, waits for them, and re-layouts  41.4 us
  transfers between devices with their start and end apart: 86, of which 28 were waited for; matrix products, arithmetic and copies ran while one was open for 2% of the time, Pallas kernels for 45%

profile of v4, /device:TPU:1, one launch (start us, length us, event | category | flops | bytes accessed | tf_op | source)
XLA Modules:
  0.0 679.2 jit_solution(873650947055046064)
XLA Ops:
  12.4 11.8 %all-gather.1 = s32[8,2,4]{2,1,0:T(2,128)S(1)} all-gather(s32[1,2,4]{2,1,0:T(2,128)S(1)} %add_bitcast_fusion), channel_id=2, replica_groups=mesh['shard'=4,'rep'=8] {'rep'}, dimensions={0}, use_global_device_ids=true | all-gather | bytes 288 | tf_op jit(solution)/shard_map/all_gather | solution.py:1251
  48.2 10.1 %shard_map.233 = (f32[1024,1024]{1,0:T(8,128)}, bf16[1024,1024]{1,0:T(8,128)(2,1)}, f32[1024,128]{1,0:T(8,128)S(1)}, bf16[1024,1024]{1,0:T(8,128)(2,1)}, bf16[10...) custom-call(s32[3]{0:T(128)S(1)} %pad_add_fusion.own_ref, ...), custom_call_target="tpu_custom_call" | custom-call | flops 1 | bytes 1 | tf_op jit(solution)/shard_map/pallas_call | solution.py:46
  80.8 17.1 %shard_map.238 = (bf16[1024,2048]{1,0:T(8,128)(2,1)}, bf16[1024,2048]{1,0:T(8,128)(2,1)}) custom-call(s32[3]{0:T(128)S(1)} %pad_add_fusion.own_ref, bf16[1024,1024]{1,0:T(8,128)(2,1)} %get-tuple-element.453.x_ref.refs_0_, f32[8,2048]{1,0:T(8,128)S(1)} %get-tuple-element.280.b_ref, bf16[1024,512]{1,0:T(8,128)(2,1)S(1)} %copy-done.20, ...), custom_call_target="tpu_custom_call" | custom-call | flops 1 | bytes 1 | tf_op jit(solution)/shard_map/pallas_call | solution.py:46
  99.0 10.3 %shard_map.239 = (bf16[1024,512]{1,0:T(8,128)(2,1)S(1)}, f32[8,1024]{1,0:T(8,128)S(1)}) custom-call(s32[4]{0:T(128)S(1)} %subtract_clamp_fusion.meta_ref, bf16[1024,512]{1,0:T(8,128)(2,1)S(1)} %copy-done.61, bf16[1024,1024]{1,0:T(8,128)(2,1)S(1)} %copy-done.51, bf16[512,1024]{1,0:T(8,128)(2,1)} %collective-permute-done.11.halo_ref, s32[1024,1]{1,0:T(8,128)S(1)} %copy-done.86), custom_call_target="tpu_custom_call" | custom-call | flops 20000000000 | bytes 1 | tf_op jit(solution)/shard_map/pallas_call | solution.py:46
  123.5 11.4 %shard_map.241.refs_1_ = bf16[1024,1024]{1,0:T(8,128)(2,1)} custom-call(s32[3]{0:T(128)S(1)} %pad_add_fusion.own_ref, bf16[1024,512]{1,0:T(8,128)(2,1)S(1)} %get-tuple-element.298.att_ref.refs_1_.o_ref, bf16[1024,2048]{1,0:T(8,128)(2,1)} %get-tuple-element.400.act_ref.refs_0_, bf16[1280,512]{1,0:T(8,128)(2,1)S(1)} %copy-done.10, ...), custom_call_target="tpu_custom_call" | custom-call | flops 1 | bytes 1 | tf_op jit(solution)/shard_map/pallas_call | solution.py:46
  135.0 14.9 %collective-permute-start.18 = (bf16[1024,1024]{1,0:T(8,128)(2,1)}, bf16[1024,1024]{1,0:T(8,128)(2,1)}, u32[]{:S(2)}, u32[]{:S(2)}) collective-permute-start(bf16[1024,1024]{1,0:T(8,128)(2,1)} %shard_map.241.refs_1_), channel_id=1, source_target_pairs={{0,1},{1,0},{2,3},{3,2},{4,5},{5,4},{6,7},{7,6},{8,9},{9,8},{10,11... | collective-permute-start | bytes 6291464 | tf_op jit(solution)/shard_map/ppermute | solution.py:994
  162.5 12.2 %shard_map.243 = (f32[1024,1024]{1,0:T(8,128)}, bf16[1024,1024]{1,0:T(8,128)(2,1)}, f32[1024,128]{1,0:T(8,128)S(1)}, bf16[1024,1024]{1,0:T(8,128)(2,1)}, bf16[10...) custom-call(s32[3]{0:T(128)S(1)} %pad_add_fusion.own_ref, ...), custom_call_target="tpu_custom_call" | custom-call | flops 1 | bytes 1 | tf_op jit(solution)/shard_map/pallas_call | solution.py:46
  199.0 15.8 %shard_map.246 = (bf16[1024,2048]{1,0:T(8,128)(2,1)}, bf16[1024,2048]{1,0:T(8,128)(2,1)}) custom-call(s32[3]{0:T(128)S(1)} %pad_add_fusion.own_ref, bf16[1024,1024]{1,0:T(8,128)(2,1)} %get-tuple-element.379.x_ref.refs_0_, f32[8,2048]{1,0:T(8,128)S(1)} %get-tuple-element.280.b_ref, bf16[1024,512]{1,0:T(8,128)(2,1)S(1)} %shard_map.234.rest_0_.rest_5_, ...), custom_call_target="tpu_custom_call" | custom-call | flops 10000000000 | bytes 1 | tf_op jit(solution)/shard_map/pallas_call | solution.py:46
  216.1 10.4 %shard_map.247 = (bf16[1024,512]{1,0:T(8,128)(2,1)S(1)}, f32[8,1024]{1,0:T(8,128)S(1)}) custom-call(s32[4]{0:T(128)S(1)} %subtract_clamp_fusion.meta_ref, bf16[1024,512]{1,0:T(8,128)(2,1)S(1)} %copy-done.107, bf16[1024,1024]{1,0:T(8,128)(2,1)S(1)} %copy-done.106, bf16[512,1024]{1,0:T(8,128)(2,1)} %collective-permute-done.25.halo_ref, s32[1024,1]{1,0:T(8,128)S(1)} %copy-done.87), custom_call_target="tpu_custom_call" | custom-call | flops 6000000000 | bytes 1 | tf_op jit(solution)/shard_map/pallas_call | solution.py:46
  233.8 11.4 %shard_map.249 = (bf16[1280,512]{1,0:T(8,128)(2,1)S(1)}, bf16[1280,512]{1,0:T(8,128)(2,1)S(1)}, bf16[1280,512]{1,0:T(8,128)(2,1)}, bf16[640,512]{1,0:T(8,128)(2,1)S(1)}, bf16[640,512]{1,0:T(8,128)(2,1)S(1)}) custom-call(s32[3]{0:T(128)S(1)} %pad_add_fusion.own_ref, bf16[1024,2048]{1,0:T(8,128)(2,1)} %get-tuple-element.341.refs_0_.act_ref, ...), custom_call_target="tpu_custom_call" | custom-call | flops 1 | bytes 1 | tf_op jit(solution)/shard_map/pallas_call | solution.py:46
  247.0 10.9 %shard_map.250 = bf16[1024,1024]{1,0:T(8,128)(2,1)} custom-call(s32[3]{0:T(128)S(1)} %pad_add_fusion.own_ref, bf16[1024,512]{1,0:T(8,128)(2,1)S(1)} %get-tuple-element.348.refs_1_.att_ref.o_ref, bf16[1024,2048]{1,0:T(8,128)(2,1)} %get-tuple-element.341.refs_0_.act_ref, bf16[1280,512]{1,0:T(8,128)(2,1)S(1)} %shard_map.244.rest_0_, ...), custom_call_target="tpu_custom_call" | custom-call | flops 1 | bytes 1 | tf_op jit(solution)/shard_map/pallas_call | solution.py:46
  262.8 12.1 %shard_map.251 = (bf16[1024,2048]{1,0:T(8,128)(2,1)}, bf16[1024,512]{1,0:T(8,128)(2,1)S(1)}, f32[1,2048]{1,0:T(1,128)S(1)}, f32[1,1024]{1,0:T(1,128)S(1)}) custom-call(s32[3]{0:T(128)S(1)} %pad_add_fusion.own_ref, bf16[1024,1024]{1,0:T(8,128)(2,1)} %pad_maximum_fusion.1.refs_2_.g_ref, bf16[1024,2048]{1,0:T(8,128)(2,1)} %get-tuple-element.331.slope_ref, ...), custom_call_target="tpu_custom_call" | custom-call | flops 40000000000 | bytes 1 | tf_op jit(solution)/shard_map/pallas_call | solution.py:46
  276.0 16.8 %shard_map.252 = (bf16[1024,512]{1,0:T(8,128)(2,1)S(1)}, bf16[1024,1024]{1,0:T(8,128)(2,1)}, bf16[512,1024]{1,0:T(8,128)(2,1)}) custom-call(s32[4]{0:T(128)S(1)} %subtract_clamp_fusion.meta_ref, bf16[1024,512]{1,0:T(8,128)(2,1)S(1)} %copy-done.108, bf16[1024,1024]{1,0:T(8,128)(2,1)} %get-tuple-element.333.kv_ref, ...), custom_call_target="tpu_custom_call" | custom-call | flops 20000000000 | bytes 1 | tf_op jit(solution)/shard_map/pallas_call | solution.py:46
  313.6 9.8 %shard_map.254 = (bf16[1024,512]{1,0:T(8,128)(2,1)S(1)}, bf16[1024,512]{1,0:T(8,128)(2,1)}, bf16[1024,512]{1,0:T(8,128)(2,1)}, bf16[512,512]{1,0:T(8,128)(2,1)S(1)}, bf16[512,512]{1,0:T(8,128)(2,1)S(1)}) custom-call(s32[3]{0:T(128)S(1)} %pad_add_fusion.own_ref, bf16[1024,1024]{1,0:T(8,128)(2,1)} %get-tuple-element.379.x_ref.refs_0_, ...), custom_call_target="tpu_custom_call" | custom-call | flops 1 | bytes 1 | tf_op jit(solution)/shard_map/pallas_call | solution.py:46
  327.9 16.3 %shard_map.256 = (bf16[1024,1536]{1,0:T(8,128)(2,1)}, bf16[1024,1024]{1,0:T(8,128)(2,1)}, f32[1,1536]{1,0:T(1,128)S(1)}, f32[1,1024]{1,0:T(1,128)S(1)}, f32[1,1024]{1,0:T(1,128)S(1)}) custom-call(s32[3]{0:T(128)S(1)} %pad_add_fusion.own_ref, bf16[1024,512]{1,0:T(8,128)(2,1)} %copy-done.64, bf16[1024,1024]{1,0:T(8,128)(2,1)} %get-tuple-element.376.dkv_ref, ...), custom_call_target="tpu_custom_call" | custom-call | flops 1 | bytes 1 | tf_op jit(solution)/shard_map/pallas_call | solution.py:46
  360.2 10.2 %collective-permute-done.32.refs_3_ = bf16[1024,512]{1,0:T(8,128)(2,1)S(1)} collective-permute-done((bf16[1024,512]{1,0:T(8,128)(2,1)}, bf16[1024,512]{1,0:T(8,128)(2,1)S(1)}, u32[]{:S(2)}, u32[]{:S(2)}) %collective-permute-start.32) | collective-permute-done | bytes 1048608 | tf_op jit(solution)/shard_map/ppermute | solution.py:994
  391.1 11.7 %shard_map.263 = (bf16[1280,512]{1,0:T(8,128)(2,1)S(1)}, bf16[1280,512]{1,0:T(8,128)(2,1)}, bf16[1280,512]{1,0:T(8,128)(2,1)}, bf16[640,512]{1,0:T(8,128)(2,1)S(1)}, bf16[640,512]{1,0:T(8,128)(2,1)S(1)}) custom-call(s32[3]{0:T(128)S(1)} %pad_add_fusion.own_ref, bf16[1024,2048]{1,0:T(8,128)(2,1)} %get-tuple-element.400.act_ref.refs_0_, ...), custom_call_target="tpu_custom_call" | custom-call | flops 1 | bytes 1 | tf_op jit(solution)/shard_map/pallas_call | solution.py:46
  409.6 12.1 %shard_map.265 = (bf16[1024,2048]{1,0:T(8,128)(2,1)}, bf16[1024,512]{1,0:T(8,128)(2,1)S(1)}, f32[1,2048]{1,0:T(1,128)S(1)}, f32[1,1024]{1,0:T(1,128)S(1)}) custom-call(s32[3]{0:T(128)S(1)} %pad_add_fusion.own_ref, bf16[1024,1024]{1,0:T(8,128)(2,1)} %copy-done.24, bf16[1024,2048]{1,0:T(8,128)(2,1)} %get-tuple-element.284.slope_ref, ...), custom_call_target="tpu_custom_call" | custom-call | flops 1 | bytes 1 | tf_op jit(solution)/shard_map/pallas_call | solution.py:46
  435.5 16.7 %shard_map.269 = (bf16[1024,512]{1,0:T(8,128)(2,1)S(1)}, bf16[1024,1024]{1,0:T(8,128)(2,1)}, bf16[512,1024]{1,0:T(8,128)(2,1)}) custom-call(s32[4]{0:T(128)S(1)} %subtract_clamp_fusion.meta_ref, bf16[1024,512]{1,0:T(8,128)(2,1)S(1)} %copy-done.62, bf16[1024,1024]{1,0:T(8,128)(2,1)} %get-tuple-element.286.kv_ref, ...), custom_call_target="tpu_custom_call" | custom-call | flops 1 | bytes 1 | tf_op jit(solution)/shard_map/pallas_call | solution.py:46
  469.0 9.6 %shard_map.274 = (bf16[1024,512]{1,0:T(8,128)(2,1)S(1)}, bf16[1024,512]{1,0:T(8,128)(2,1)}, bf16[1024,512]{1,0:T(8,128)(2,1)}, bf16[512,512]{1,0:T(8,128)(2,1)S(1)}, bf16[512,512]{1,0:T(8,128)(2,1)S(1)}) custom-call(s32[3]{0:T(128)S(1)} %pad_add_fusion.own_ref, bf16[1024,1024]{1,0:T(8,128)(2,1)} %get-tuple-element.453.x_ref.refs_0_, ...), custom_call_target="tpu_custom_call" | custom-call | flops 1 | bytes 1 | tf_op jit(solution)/shard_map/pallas_call | solution.py:46
  502.4 16.5 %shard_map.277 = (bf16[1024,1536]{1,0:T(8,128)(2,1)}, bf16[1024,1024]{1,0:T(8,128)(2,1)}, f32[1,1536]{1,0:T(1,128)S(1)}, f32[1,1024]{1,0:T(1,128)S(1)}, f32[1,1024]{1,0:T(1,128)S(1)}) custom-call(s32[3]{0:T(128)S(1)} %pad_add_fusion.own_ref, bf16[1024,512]{1,0:T(8,128)(2,1)} %copy-done.63, bf16[1024,1024]{1,0:T(8,128)(2,1)} %get-tuple-element.439.dkv_ref, ...), custom_call_target="tpu_custom_call" | custom-call | flops 1 | bytes 1 | tf_op jit(solution)/shard_map/pallas_call | solution.py:46
  550.2 11.9 %collective-permute-start.66 = (bf16[1024,512]{1,0:T(8,128)(2,1)S(1)}, bf16[1024,512]{1,0:T(8,128)(2,1)S(1)}, u32[]{:S(2)}, u32[]{:S(2)}) collective-permute-start(bf16[1024,512]{1,0:T(8,128)(2,1)S(1)} %shard_map.280.refs_0_), channel_id=1, source_target_pairs={{0,2},{1,3},{6,4},{7,5},{8,10},{9,11},{14,12},{15,13},{16,18},{17,... | collective-permute-start | bytes 3145736 | tf_op jit(solution)/shard_map/ppermute | solution.py:994
  595.8 10.2 %collective-permute-start.72 = (bf16[384,512]{1,0:T(8,128)(2,1)S(1)}, bf16[384,512]{1,0:T(8,128)(2,1)S(1)}, u32[]{:S(2)}, u32[]{:S(2)}) collective-permute-start(bf16[384,512]{1,0:T(8,128)(2,1)S(1)} %get-tuple-element.480.refs_0_), channel_id=1, source_target_pairs={{0,2},{1,3},{6,4},{7,5},{8,10},{9,11},{14,12},{15,13},{16,18},{17,... | collective-permute-start | bytes 1179656 | tf_op jit(solution)/shard_map/ppermute | solution.py:994
  635.2 14.9 %collective-permute-done.82.b_ref = bf16[384,512]{1,0:T(8,128)(2,1)S(1)} collective-permute-done((bf16[384,512]{1,0:T(8,128)(2,1)S(1)}, bf16[384,512]{1,0:T(8,128)(2,1)S(1)}, u32[]{:S(2)}, u32[]{:S(2)}) %collective-permute-start.82) | collective-permute-done | bytes 393248 | tf_op jit(solution)/shard_map/ppermute | solution.py:994
  (503 shorter events, 370.9 us)
Async XLA Ops:
  10.8 33.3 %collective-permute-start = (bf16[512,1024]{1,0:T(8,128)(2,1)}, bf16[512,1024]{1,0:T(8,128)(2,1)}, u32[]{:S(2)}, u32[]{:S(2)}) collective-permute-start(bf16[512,1024]{1,0:T(8,128)(2,1)} %param.14), channel_id=1, source_target_pairs={{0,1},{1,0},{2,3},{3,2},{4,5},{5,4},{6,7},{7,6},{8,9},{9,8},{10,11... | collective-permute-start | bytes 3145736 | tf_op jit(solution)/shard_map/ppermute | solution.py:994
  64.2 33.7 %collective-permute-start.11 = (bf16[512,1024]{1,0:T(8,128)(2,1)}, bf16[512,1024]{1,0:T(8,128)(2,1)}, u32[]{:S(2)}, u32[]{:S(2)}) collective-permute-start(bf16[512,1024]{1,0:T(8,128)(2,1)} %get-tuple-element.288), channel_id=1, source_target_pairs={{0,2},{1,3},{2,4},{3,5},{4,6},{5,7},{6,0},{7,1},{8,10},{9,11},{10,... | collective-permute-start | bytes 3145736 | tf_op jit(solution)/shard_map/ppermute | solution.py:994
  75.1 34.9 %collective-permute-start.10 = (bf16[1280,512]{1,0:T(8,128)(2,1)}, bf16[1280,512]{1,0:T(8,128)(2,1)S(1)}, u32[]{:S(2)}, u32[]{:S(2)}) collective-permute-start(bf16[1280,512]{1,0:T(8,128)(2,1)} %copy-done.9), channel_id=1, source_target_pairs={{0,16},{1,17},{2,18},{3,19},{4,20},{5,21},{6,22},{7,23},{8,24},{9,... | collective-permute-start | bytes 3932168 | tf_op jit(solution)/shard_map/ppermute | solution.py:994
  76.0 34.0 %collective-permute-start.9 = (bf16[1280,512]{1,0:T(8,128)(2,1)}, bf16[1280,512]{1,0:T(8,128)(2,1)S(1)}, u32[]{:S(2)}, u32[]{:S(2)}) collective-permute-start(bf16[1280,512]{1,0:T(8,128)(2,1)} %copy-done.9), channel_id=1, source_target_pairs={{0,8},{1,9},{2,10},{3,11},{4,12},{5,13},{6,14},{7,15},{8,0},{9,1},... | collective-permute-start | bytes 3932168 | tf_op jit(solution)/shard_map/ppermute | solution.py:994
  190.9 39.7 %collective-permute-start.26 = (bf16[512,1024]{1,0:T(8,128)(2,1)}, bf16[512,1024]{1,0:T(8,128)(2,1)}, u32[]{:S(2)}, u32[]{:S(2)}) collective-permute-start(bf16[512,1024]{1,0:T(8,128)(2,1)} %param.17), channel_id=1, source_target_pairs={{0,1},{1,0},{2,3},{3,2},{4,5},{5,4},{6,7},{7,6},{8,9},{9,8},{10,11... | collective-permute-start | bytes 3145736 | tf_op jit(solution)/shard_map/ppermute | solution.py:994
  246.3 56.0 %collective-permute-start.27 = (bf16[1280,512]{1,0:T(8,128)(2,1)}, bf16[1280,512]{1,0:T(8,128)(2,1)S(1)}, u32[]{:S(2)}, u32[]{:S(2)}) collective-permute-start(bf16[1280,512]{1,0:T(8,128)(2,1)} %get-tuple-element.345), channel_id=1, source_target_pairs={{0,8},{1,9},{2,10},{3,11},{4,12},{5,13},{6,14},{7,15},{8,0},{9,1},... | collective-permute-start | bytes 3932168 | tf_op jit(solution)/shard_map/ppermute | solution.py:994
  246.7 55.5 %collective-permute-start.28 = (bf16[1280,512]{1,0:T(8,128)(2,1)S(1)}, bf16[1280,512]{1,0:T(8,128)(2,1)S(1)}, u32[]{:S(2)}, u32[]{:S(2)}) collective-permute-start(bf16[1280,512]{1,0:T(8,128)(2,1)S(1)} %get-tuple-element.346), channel_id=1, source_target_pairs={{0,16},{1,17},{2,18},{3,19},{4,20},{5,21},{6,22},{7,23},{8,24},{9,... | collective-permute-start | bytes 3932168 | tf_op jit(solution)/shard_map/ppermute | solution.py:994
  257.9 51.9 %collective-permute-start.31 = (bf16[1024,1024]{1,0:T(8,128)(2,1)}, bf16[1024,1024]{1,0:T(8,128)(2,1)}, u32[]{:S(2)}, u32[]{:S(2)}) collective-permute-start(bf16[1024,1024]{1,0:T(8,128)(2,1)} %shard_map.250), channel_id=1, source_target_pairs={{0,1},{1,0},{2,3},{3,2},{4,5},{5,4},{6,7},{7,6},{8,9},{9,8},{10,11... | collective-permute-start | bytes 6291464 | tf_op jit(solution)/shard_map/ppermute | solution.py:994
  293.7 34.1 %collective-permute-start.34 = (bf16[512,1024]{1,0:T(8,128)(2,1)}, bf16[512,1024]{1,0:T(8,128)(2,1)}, u32[]{:S(2)}, u32[]{:S(2)}) collective-permute-start(bf16[512,1024]{1,0:T(8,128)(2,1)} %get-tuple-element.370), channel_id=1, source_target_pairs={{0,6},{1,7},{2,0},{3,1},{4,2},{5,3},{6,4},{7,5},{8,14},{9,15},{10,... | collective-permute-start | bytes 3145736 | tf_op jit(solution)/shard_map/ppermute | solution.py:994
  347.1 36.6 %collective-permute-start.42 = (bf16[1280,512]{1,0:T(8,128)(2,1)S(1)}, bf16[1280,512]{1,0:T(8,128)(2,1)S(1)}, u32[]{:S(2)}, u32[]{:S(2)}) collective-permute-start(bf16[1280,512]{1,0:T(8,128)(2,1)S(1)} %shard_map.255.refs_0_), channel_id=1, source_target_pairs={{0,2},{1,3},{6,4},{7,5},{8,10},{9,11},{14,12},{15,13},{16,18},{17,... | collective-permute-start | bytes 3932168 | tf_op jit(solution)/shard_map/ppermute | solution.py:994
  386.3 38.4 %collective-permute-start.46 = (bf16[1024,512]{1,0:T(8,128)(2,1)S(1)}, bf16[1024,512]{1,0:T(8,128)(2,1)S(1)}, u32[]{:S(2)}, u32[]{:S(2)}) collective-permute-start(bf16[1024,512]{1,0:T(8,128)(2,1)S(1)} %shard_map.262.refs_0_), channel_id=1, source_target_pairs={{0,2},{1,3},{6,4},{7,5},{8,10},{9,11},{14,12},{15,13},{16,18},{17,... | collective-permute-start | bytes 3145736 | tf_op jit(solution)/shard_map/ppermute | solution.py:994
  389.9 36.5 %collective-permute-start.48 = (bf16[1280,512]{1,0:T(8,128)(2,1)S(1)}, bf16[1280,512]{1,0:T(8,128)(2,1)S(1)}, u32[]{:S(2)}, u32[]{:S(2)}) collective-permute-start(bf16[1280,512]{1,0:T(8,128)(2,1)S(1)} %shard_map.261.refs_0_), channel_id=1, source_target_pairs={{2,4},{3,5},{4,2},{5,3},{10,12},{11,13},{12,10},{13,11},{18,20},{1... | collective-permute-start | bytes 3932168 | tf_op jit(solution)/shard_map/ppermute | solution.py:994
  427.2 31.0 %collective-permute-start.52 = (bf16[1280,512]{1,0:T(8,128)(2,1)S(1)}, bf16[1280,512]{1,0:T(8,128)(2,1)S(1)}, u32[]{:S(2)}, u32[]{:S(2)}) collective-permute-start(bf16[1280,512]{1,0:T(8,128)(2,1)S(1)} %shard_map.268.a_ref), channel_id=1, source_target_pairs={{2,0},{3,1},{4,6},{5,7},{10,8},{11,9},{12,14},{13,15},{18,16},{19,... | collective-permute-start | bytes 3932168 | tf_op jit(solution)/shard_map/ppermute | solution.py:994
  463.0 39.4 %collective-permute-start.59 = (bf16[512,1024]{1,0:T(8,128)(2,1)}, bf16[512,1024]{1,0:T(8,128)(2,1)}, u32[]{:S(2)}, u32[]{:S(2)}) collective-permute-start(bf16[512,1024]{1,0:T(8,128)(2,1)} %get-tuple-element.436), channel_id=1, source_target_pairs={{0,6},{1,7},{2,0},{3,1},{4,2},{5,3},{6,4},{7,5},{8,14},{9,15},{10,... | collective-permute-start | bytes 3145736 | tf_op jit(solution)/shard_map/ppermute | solution.py:994
  481.1 42.1 %collective-permute-start.57 = (bf16[1024,512]{1,0:T(8,128)(2,1)}, bf16[1024,512]{1,0:T(8,128)(2,1)S(1)}, u32[]{:S(2)}, u32[]{:S(2)}) collective-permute-start(bf16[1024,512]{1,0:T(8,128)(2,1)} %get-tuple-element.433), channel_id=1, source_target_pairs={{0,8},{1,9},{2,10},{3,11},{4,12},{5,13},{6,14},{7,15},{8,0},{9,1},... | collective-permute-start | bytes 3145736 | tf_op jit(solution)/shard_map/ppermute | solution.py:994
  481.1 42.1 %collective-permute-start.58 = (bf16[1024,512]{1,0:T(8,128)(2,1)}, bf16[1024,512]{1,0:T(8,128)(2,1)S(1)}, u32[]{:S(2)}, u32[]{:S(2)}) collective-permute-start(bf16[1024,512]{1,0:T(8,128)(2,1)} %get-tuple-element.434), channel_id=1, source_target_pairs={{0,16},{1,17},{2,18},{3,19},{4,20},{5,21},{6,22},{7,23},{8,24},{9,... | collective-permute-start | bytes 3145736 | tf_op jit(solution)/shard_map/ppermute | solution.py:994
  481.2 44.3 %collective-permute-start.62 = (bf16[1280,512]{1,0:T(8,128)(2,1)S(1)}, bf16[1280,512]{1,0:T(8,128)(2,1)S(1)}, u32[]{:S(2)}, u32[]{:S(2)}) collective-permute-start(bf16[1280,512]{1,0:T(8,128)(2,1)S(1)} %shard_map.272.refs_0_), channel_id=1, source_target_pairs={{0,1},{1,0},{2,3},{3,2},{4,5},{5,4},{6,7},{7,6},{8,9},{9,8},{10,11... | collective-permute-start | bytes 3932168 | tf_op jit(solution)/shard_map/ppermute | solution.py:994
  494.0 54.5 %collective-permute-start.56 = (bf16[1280,512]{1,0:T(8,128)(2,1)S(1)}, bf16[1280,512]{1,0:T(8,128)(2,1)S(1)}, u32[]{:S(2)}, u32[]{:S(2)}) collective-permute-start(bf16[1280,512]{1,0:T(8,128)(2,1)S(1)} %shard_map.276.refs_0_), channel_id=1, source_target_pairs={{0,2},{1,3},{6,4},{7,5},{8,10},{9,11},{14,12},{15,13},{16,18},{17,... | collective-permute-start | bytes 3932168 | tf_op jit(solution)/shard_map/ppermute | solution.py:994
  519.0 45.6 %collective-permute-start.63 = (bf16[1024,1024]{1,0:T(8,128)(2,1)}, bf16[1024,1024]{1,0:T(8,128)(2,1)}, u32[]{:S(2)}, u32[]{:S(2)}) collective-permute-start(bf16[1024,1024]{1,0:T(8,128)(2,1)} %get-tuple-element.441.p0_ref), channel_id=1, source_target_pairs={{0,1},{1,0},{2,3},{3,2},{4,5},{5,4},{6,7},{7,6},{8,9},{9,8},{10,11... | collective-permute-start | bytes 6291464 | tf_op jit(solution)/shard_map/ppermute | solution.py:994
  525.5 37.1 %collective-permute-start.49 = (bf16[784,512]{1,0:T(8,128)(2,1)S(1)}, bf16[784,512]{1,0:T(8,128)(2,1)}, u32[]{:S(2)}, u32[]{:S(2)}) collective-permute-start(bf16[784,512]{1,0:T(8,128)(2,1)S(1)} %copy-done.46), channel_id=1, source_target_pairs={{2,4},{3,5},{4,2},{5,3},{10,12},{11,13},{12,10},{13,11},{18,20},{1... | collective-permute-start | bytes 2408456 | tf_op jit(solution)/shard_map/ppermute | solution.py:994
  550.2 32.6 %collective-permute-start.66 = (bf16[1024,512]{1,0:T(8,128)(2,1)S(1)}, bf16[1024,512]{1,0:T(8,128)(2,1)S(1)}, u32[]{:S(2)}, u32[]{:S(2)}) collective-permute-start(bf16[1024,512]{1,0:T(8,128)(2,1)S(1)} %shard_map.280.refs_0_), channel_id=1, source_target_pairs={{0,2},{1,3},{6,4},{7,5},{8,10},{9,11},{14,12},{15,13},{16,18},{17,... | collective-permute-start | bytes 3145736 | tf_op jit(solution)/shard_map/ppermute | solution.py:994
  584.4 37.5 %collective-permute-start.77 = (bf16[1280,512]{1,0:T(8,128)(2,1)S(1)}, bf16[1280,512]{1,0:T(8,128)(2,1)S(1)}, u32[]{:S(2)}, u32[]{:S(2)}) collective-permute-start(bf16[1280,512]{1,0:T(8,128)(2,1)S(1)} %shard_map.286.a_ref), channel_id=1, source_target_pairs={{2,0},{3,1},{4,6},{5,7},{10,8},{11,9},{12,14},{13,15},{18,16},{19,... | collective-permute-start | bytes 3932168 | tf_op jit(solution)/shard_map/ppermute | solution.py:994
  613.4 37.2 %collective-permute-start.81 = (bf16[1024,512]{1,0:T(8,128)(2,1)S(1)}, bf16[1024,512]{1,0:T(8,128)(2,1)S(1)}, u32[]{:S(2)}, u32[]{:S(2)}) collective-permute-start(bf16[1024,512]{1,0:T(8,128)(2,1)S(1)} %shard_map.291.a_ref), channel_id=1, source_target_pairs={{2,0},{3,1},{4,6},{5,7},{10,8},{11,9},{12,14},{13,15},{18,16},{19,... | collective-permute-start | bytes 3145736 | tf_op jit(solution)/shard_map/ppermute | solution.py:994
  622.5 35.8 %collective-permute-start.80 = (bf16[1280,512]{1,0:T(8,128)(2,1)S(1)}, bf16[1280,512]{1,0:T(8,128)(2,1)S(1)}, u32[]{:S(2)}, u32[]{:S(2)}) collective-permute-start(bf16[1280,512]{1,0:T(8,128)(2,1)S(1)} %shard_map.295.refs_0_), channel_id=1, source_target_pairs={{0,1},{1,0},{2,3},{3,2},{4,5},{5,4},{6,7},{7,6},{8,9},{9,8},{10,11... | collective-permute-start | bytes 3932168 | tf_op jit(solution)/shard_map/ppermute | solution.py:994
  (178 other events, 2118.5 us)
